TPU v7x, 32 devices: a whole 2x2x4 slice. The times are simulated.
32 devices in a mesh: rep: 4 (over x, core), grp: 8 (over z, y).
Axes of the slice: x: 2, y: 2, z: 4, core: 2. Of those that a mesh axis runs over, the one named last changes fastest.
Arguments:
- tokens: bfloat16 [2, 4, 8, 128, 2048], P(None, None, 'grp', 'rep'), may hold values from -6 to 6
- cotangent: bfloat16 [2, 4, 1024, 2048], P(None, 'rep', 'grp'), may hold values from -6 to 6
- seq_lengths: int32 [2, 4], replicated, may hold values from 256 to 1024, as said below
- bin_order: int32 [2, 4], replicated, may hold values from 0 to 3, each once within a row
- norm_gain: bfloat16 [2048], P('grp'), may hold values from 0.5 to 1.5
- w_query: bfloat16 [2048, 2048], P('grp'), may hold values from -0.125 to 0.125
- w_key: bfloat16 [2048, 2048], P('grp'), may hold values from -0.125 to 0.125
- w_value: bfloat16 [2048, 3456], P('grp'), may hold values from -0.125 to 0.125
- w_gate: bfloat16 [2048, 3456], P('grp'), may hold values from -0.125 to 0.125
- w_out: bfloat16 [3456, 2048], P('grp'), may hold values from -0.109375 to 0.109375
- mlp_gain: bfloat16 [2048], P('grp'), may hold values from 0.5 to 1.5
- w_proj: bfloat16 [2048, 3456], P('grp'), may hold values from -0.125 to 0.125
- w_up: bfloat16 [2048, 3456], P('grp'), may hold values from -0.125 to 0.125
- w_down: bfloat16 [3456, 2048], P('grp'), may hold values from -0.109375 to 0.109375
Outputs:
- bin_out: bfloat16 [2, 4, 1024, 2048], P(None, 'rep', 'grp')
- token_grad: bfloat16 [2, 4, 8, 128, 2048], P(None, None, 'grp', 'rep')
- norm_gain_grad: float32 [2048], P('grp')
- query_grad: float32 [2048, 2048], P('grp')
- key_grad: float32 [2048, 2048], P('grp')
- value_grad: float32 [2048, 3456], P('grp')
- gate_grad: float32 [2048, 3456], P('grp')
- out_grad: float32 [3456, 2048], P('grp')
- mlp_gain_grad: float32 [2048], P('grp')
- proj_grad: float32 [2048, 3456], P('grp')
- up_grad: float32 [2048, 3456], P('grp')
- down_grad: float32 [3456, 2048], P('grp')
Inputs may be any that keep to these rules, and one draw needn't show every extreme that they name: `seq_lengths`: in every micro-batch some sequence has exactly 1024 live tokens. `bin_order`: each row is a permutation of the 4 bins.
All inputs are finite; a program needn't handle non-finite values.
Results may differ from a plain program's by a relative error of at most 0.019.
Values may be sent and summed in bfloat16 or wider, within the bound.
No kernel may reach another device: no remote copies, remote signals or barrier semaphores. Data moves between devices by JAX's collectives and lax.ppermute only.
A program may use at most 640 MiB of HBM per device.

v0:
```python
import math

import jax
import jax.numpy as jnp
from jax import lax
from jax.sharding import PartitionSpec as P

HEADS = 8
KEY_DIM = 256
VAL_DIM = 432


EPS = 1e-06
GROUP_EPS = 1.0


def entering(part, axis, combine, identity):
    place = lax.axis_index(axis)
    gathered = jax.tree.map(lambda a: lax.all_gather(a, axis), part)
    state = jax.tree.map(lambda a, e: jnp.zeros_like(a) + jnp.asarray(e, a.dtype), part, identity)

    def one(turn, state):
        return combine(
            state, jax.tree.map(lambda a: lax.dynamic_index_in_dim(a, turn, 0, False), gathered)
        )

    return lax.fori_loop(0, place, one, state)


def entering_2(value, axis, join, neutral):
    count = lax.axis_size(axis)
    place = lax.axis_index(axis)
    ahead = count - 1 - place
    gathered = jax.tree.map(
        lambda a, kind: lax.all_gather(a.astype(kind), axis), value, (jnp.bfloat16, jnp.bfloat16)
    )
    state = jax.tree.map(lambda a, e: jnp.zeros_like(a) + jnp.asarray(e, a.dtype), value, neutral)

    def one(turn, state):
        source = count - 1 - turn
        return join(
            state,
            jax.tree.map(
                lambda a, own: lax.dynamic_index_in_dim(a, source, 0, False).astype(own.dtype),
                gathered,
                value,
            ),
        )

    return lax.fori_loop(0, ahead, one, state)


def norm_rows(values, gain_vec):
    return values * lax.rsqrt(jnp.mean(values * values, axis=-1, keepdims=True) + EPS) * gain_vec


def rotate(values, cosine, sine):
    half_size = values.shape[-1] // 2
    front_half = values[..., :half_size]
    back_half = values[..., half_size:]
    return jnp.concatenate(
        [front_half * cosine - back_half * sine, back_half * cosine + front_half * sine], axis=-1
    )


def rotary_tables(positions, key_size):
    frequency = jnp.exp(
        -jnp.arange(key_size // 2, dtype=jnp.float32) * (2.0 / key_size) * math.log(10000.0)
    )
    angles = positions[:, None] * frequency[None, :]
    return (jnp.cos(angles), jnp.sin(angles))


def decay_tables(head_count, row_count):
    head_ids = jnp.arange(head_count, dtype=jnp.float32)
    log_gamma = jnp.log(1.0 - jnp.exp2(-5.0 - head_ids))
    positions = jnp.arange(row_count, dtype=jnp.float32)
    lag_steps = positions[:, None] - positions[None, :]
    inner_decay = jnp.where(
        lag_steps[None] >= 0,
        jnp.exp(jnp.maximum(lag_steps, 0.0)[None] * log_gamma[:, None, None]),
        0.0,
    )
    query_decay = jnp.exp((positions[:, None] + 1.0) * log_gamma[None, :])
    key_decay = jnp.exp((row_count - 1.0 - positions[:, None]) * log_gamma[None, :])
    block_decay = jnp.exp(row_count * log_gamma)
    return (inner_decay, query_decay, key_decay, block_decay)


def mix_tail(retained, gate_pre):
    normed = retained * lax.rsqrt(jnp.mean(retained * retained, axis=-1, keepdims=True) + GROUP_EPS)
    return jax.nn.silu(gate_pre) * normed.reshape(gate_pre.shape)


def glu_act(proj_pre, up_pre):
    return jax.nn.gelu(proj_pre, approximate=True) * up_pre


def chain_step(earlier, later):
    return (earlier[0] * later[1][:, None, None] + later[0], earlier[1] * later[1])


def times_transposed(left, right):
    return lax.dot_general(
        left, right, (((1,), (1,)), ((), ())), preferred_element_type=jnp.float32
    )


def gain_owners(full_grad):
    return lax.psum_scatter(full_grad, "grp", scatter_dimension=0, tiled=True)


def weight_owners(inputs_b, outputs_b, shard_rows, member):
    first_row = member * shard_rows
    inputs_piece = lax.all_gather(inputs_b, "grp", axis=0, tiled=True)
    outputs_piece = lax.all_gather(outputs_b, "grp", axis=0, tiled=True)
    columns = lax.dynamic_slice_in_dim(inputs_piece, first_row, shard_rows, 1)
    return lax.dot_general(
        columns, outputs_piece, (((0,), (0,)), ((), ())), preferred_element_type=jnp.float32
    )


def body(
    tokens,
    cotangent,
    seq_lengths,
    bin_order,
    norm_gain,
    w_query,
    w_key,
    w_value,
    w_gate,
    w_out,
    mlp_gain,
    w_proj,
    w_up,
    w_down,
):
    micro = tokens.shape[0]
    seq_count = tokens.shape[1]
    replica = lax.axis_index("rep")
    member = lax.axis_index("grp")
    selector = (
        bin_order[:, None, :] == jnp.arange(seq_count, dtype=jnp.int32)[None, :, None]
    ).astype(jnp.bfloat16)
    ordered = jnp.einsum(
        "mks,msgrd->mkgrd", selector, tokens, preferred_element_type=jnp.float32
    ).astype(jnp.bfloat16)
    arrived = lax.all_to_all(ordered, "rep", split_axis=1, concat_axis=3, tiled=True)
    row_count = arrived.shape[3]
    width = arrived.shape[4]
    total_rows = micro * row_count
    input_f32 = arrived.reshape(total_rows, width).astype(jnp.float32)
    live_len = jnp.sum(jnp.where(bin_order == replica, seq_lengths, 0), axis=1)
    positions = member * row_count + jnp.arange(row_count, dtype=jnp.int32)
    live = (positions[None, :] < live_len[:, None]).astype(jnp.float32).reshape(total_rows, 1)
    query_full, key_full, value_full, gate_full, out_full, gain_one = (
        lax.all_gather(w_query, "grp", axis=0, tiled=True),
        lax.all_gather(w_key, "grp", axis=0, tiled=True),
        lax.all_gather(w_value, "grp", axis=0, tiled=True),
        lax.all_gather(w_gate, "grp", axis=0, tiled=True),
        lax.all_gather(w_out, "grp", axis=0, tiled=True),
        lax.all_gather(norm_gain, "grp", axis=0, tiled=True),
    )
    normed_in, norm_pullback = jax.vjp(norm_rows, input_f32, gain_one.astype(jnp.float32))
    activations = normed_in.astype(jnp.bfloat16)
    query_pre = jnp.dot(activations, query_full, preferred_element_type=jnp.float32)
    key_pre = jnp.dot(activations, key_full, preferred_element_type=jnp.float32)
    value_b = jnp.dot(activations, value_full, preferred_element_type=jnp.float32).astype(
        jnp.bfloat16
    )
    gate_pre = jnp.dot(activations, gate_full, preferred_element_type=jnp.float32)
    cosine, sine = rotary_tables(positions.astype(jnp.float32), KEY_DIM)
    cosine_rows = cosine[None, :, None, :]
    sine_rows = sine[None, :, None, :]

    def turn(values):
        return rotate(values, cosine_rows, sine_rows)

    key_shape = (micro, row_count, HEADS, KEY_DIM)
    query_rot, query_pullback = jax.vjp(turn, query_pre.reshape(key_shape))
    key_rot, key_pullback = jax.vjp(turn, key_pre.reshape(key_shape))
    query_b = query_rot.astype(jnp.bfloat16)
    key_b = key_rot.astype(jnp.bfloat16)
    value_heads = value_b.reshape(micro, row_count, HEADS, VAL_DIM)
    inner_decay, query_decay, key_decay, block_decay = decay_tables(HEADS, row_count)
    scores = jnp.einsum("mihd,mjhd->mhij", query_b, key_b, preferred_element_type=jnp.float32)
    weights_b = (scores * inner_decay[None]).astype(jnp.bfloat16)
    intra = jnp.einsum(
        "mhij,mjhe->mihe", weights_b, value_heads, preferred_element_type=jnp.float32
    )
    key_dec = (key_b.astype(jnp.float32) * key_decay[None, :, :, None]).astype(jnp.bfloat16)
    query_dec = (query_b.astype(jnp.float32) * query_decay[None, :, :, None]).astype(jnp.bfloat16)
    local_state = jnp.einsum(
        "mjhd,mjhe->mhde", key_dec, value_heads, preferred_element_type=jnp.float32
    )
    incoming = entering(
        (local_state, block_decay),
        "grp",
        chain_step,
        (jnp.zeros_like(local_state), jnp.ones_like(block_decay)),
    )[0]
    state_b = incoming.astype(jnp.bfloat16)
    retained = intra + jnp.einsum(
        "mihd,mhde->mihe", query_dec, state_b, preferred_element_type=jnp.float32
    )
    mixed, tail_pullback = jax.vjp(mix_tail, retained, gate_pre)
    mixed_b = mixed.astype(jnp.bfloat16)
    hidden = input_f32 + jnp.dot(mixed_b, out_full, preferred_element_type=jnp.float32)
    proj_full, up_full, down_full, gain_two = (
        lax.all_gather(w_proj, "grp", axis=0, tiled=True),
        lax.all_gather(w_up, "grp", axis=0, tiled=True),
        lax.all_gather(w_down, "grp", axis=0, tiled=True),
        lax.all_gather(mlp_gain, "grp", axis=0, tiled=True),
    )
    normed_mid, mid_pullback = jax.vjp(norm_rows, hidden, gain_two.astype(jnp.float32))
    middle_b = normed_mid.astype(jnp.bfloat16)
    proj_pre = jnp.dot(middle_b, proj_full, preferred_element_type=jnp.float32)
    up_pre = jnp.dot(middle_b, up_full, preferred_element_type=jnp.float32)
    glu_rows, glu_pullback = jax.vjp(glu_act, proj_pre, up_pre)
    glu_b = glu_rows.astype(jnp.bfloat16)
    out_rows = hidden + jnp.dot(glu_b, down_full, preferred_element_type=jnp.float32)
    bin_out = out_rows.astype(jnp.bfloat16).reshape(micro, 1, row_count, width)
    out_grad_rows = cotangent.reshape(total_rows, width).astype(jnp.float32) * live
    out_grad_b = out_grad_rows.astype(jnp.bfloat16)
    glu_grad = times_transposed(out_grad_b, down_full)
    proj_grad_rows, up_grad_rows = glu_pullback(glu_grad)
    proj_grad_b = proj_grad_rows.astype(jnp.bfloat16)
    up_grad_b = up_grad_rows.astype(jnp.bfloat16)
    middle_grad = times_transposed(proj_grad_b, proj_full) + times_transposed(up_grad_b, up_full)
    hidden_from_norm, gain_two_grad = mid_pullback(middle_grad)
    hidden_grad = out_grad_rows + hidden_from_norm
    branch_grad_b = hidden_grad.astype(jnp.bfloat16)
    mixed_grad = times_transposed(branch_grad_b, out_full)
    retained_grad, gate_grad_rows = tail_pullback(mixed_grad)
    gate_grad_b = gate_grad_rows.astype(jnp.bfloat16)
    retained_grad_b = retained_grad.astype(jnp.bfloat16)
    into_state = jnp.einsum(
        "mihd,mihe->mhde", query_dec, retained_grad_b, preferred_element_type=jnp.float32
    )
    outgoing = entering_2(
        (into_state, block_decay),
        "grp",
        chain_step,
        (jnp.zeros_like(into_state), jnp.ones_like(block_decay)),
    )[0]
    out_state_b = outgoing.astype(jnp.bfloat16)
    weight_grad = jnp.einsum(
        "mihe,mjhe->mhij", retained_grad_b, value_heads, preferred_element_type=jnp.float32
    )
    score_grad_b = (weight_grad * inner_decay[None]).astype(jnp.bfloat16)
    value_grad_rows = jnp.einsum(
        "mhij,mihe->mjhe", weights_b, retained_grad_b, preferred_element_type=jnp.float32
    )
    value_grad_rows = value_grad_rows + jnp.einsum(
        "mjhd,mhde->mjhe", key_dec, out_state_b, preferred_element_type=jnp.float32
    )
    query_grad_rot = jnp.einsum(
        "mhij,mjhd->mihd", score_grad_b, key_b, preferred_element_type=jnp.float32
    )
    query_grad_rot = (
        query_grad_rot
        + jnp.einsum(
            "mihe,mhde->mihd", retained_grad_b, state_b, preferred_element_type=jnp.float32
        )
        * query_decay[None, :, :, None]
    )
    key_grad_rot = jnp.einsum(
        "mhij,mihd->mjhd", score_grad_b, query_b, preferred_element_type=jnp.float32
    )
    key_grad_rot = (
        key_grad_rot
        + jnp.einsum(
            "mjhe,mhde->mjhd", value_heads, out_state_b, preferred_element_type=jnp.float32
        )
        * key_decay[None, :, :, None]
    )
    query_grad_b = query_pullback(query_grad_rot)[0].reshape(total_rows, -1).astype(jnp.bfloat16)
    key_grad_b = key_pullback(key_grad_rot)[0].reshape(total_rows, -1).astype(jnp.bfloat16)
    value_grad_b = value_grad_rows.reshape(total_rows, -1).astype(jnp.bfloat16)
    act_grad = times_transposed(query_grad_b, query_full) + times_transposed(key_grad_b, key_full)
    act_grad = (
        act_grad
        + times_transposed(value_grad_b, value_full)
        + times_transposed(gate_grad_b, gate_full)
    )
    input_from_norm, gain_one_grad = norm_pullback(act_grad)
    input_grad = hidden_grad + input_from_norm
    leaving = input_grad.astype(jnp.bfloat16).reshape(micro, 1, 1, row_count, width)
    returned = lax.all_to_all(leaving, "rep", split_axis=3, concat_axis=1, tiled=True)
    token_grad = jnp.einsum(
        "mks,mkgrd->msgrd", selector, returned, preferred_element_type=jnp.float32
    ).astype(jnp.bfloat16)
    gain_one_owned = gain_owners(gain_one_grad)
    query_owned = weight_owners(activations, query_grad_b, w_query.shape[0], member)
    key_owned = weight_owners(activations, key_grad_b, w_key.shape[0], member)
    value_owned = weight_owners(activations, value_grad_b, w_value.shape[0], member)
    gate_owned = weight_owners(activations, gate_grad_b, w_gate.shape[0], member)
    out_owned = weight_owners(mixed_b, branch_grad_b, w_out.shape[0], member)
    gain_two_owned = gain_owners(gain_two_grad)
    proj_owned = weight_owners(middle_b, proj_grad_b, w_proj.shape[0], member)
    up_owned = weight_owners(middle_b, up_grad_b, w_up.shape[0], member)
    down_owned = weight_owners(glu_b, out_grad_b, w_down.shape[0], member)
    (
        gain_one_owned,
        query_owned,
        key_owned,
        value_owned,
        gate_owned,
        out_owned,
        gain_two_owned,
        proj_owned,
        up_owned,
        down_owned,
    ) = (
        lax.psum(gain_one_owned.astype(jnp.bfloat16), "rep").astype(jnp.float32),
        lax.psum(query_owned.astype(jnp.bfloat16), "rep").astype(jnp.float32),
        lax.psum(key_owned.astype(jnp.bfloat16), "rep").astype(jnp.float32),
        lax.psum(value_owned.astype(jnp.bfloat16), "rep").astype(jnp.float32),
        lax.psum(gate_owned.astype(jnp.bfloat16), "rep").astype(jnp.float32),
        lax.psum(out_owned.astype(jnp.bfloat16), "rep").astype(jnp.float32),
        lax.psum(gain_two_owned.astype(jnp.bfloat16), "rep").astype(jnp.float32),
        lax.psum(proj_owned.astype(jnp.bfloat16), "rep").astype(jnp.float32),
        lax.psum(up_owned.astype(jnp.bfloat16), "rep").astype(jnp.float32),
        lax.psum(down_owned.astype(jnp.bfloat16), "rep").astype(jnp.float32),
    )
    return (
        bin_out,
        token_grad,
        gain_one_owned,
        query_owned,
        key_owned,
        value_owned,
        gate_owned,
        out_owned,
        gain_two_owned,
        proj_owned,
        up_owned,
        down_owned,
    )


def solution(mesh):
    return jax.shard_map(
        body,
        mesh=mesh,
        in_specs=(
            P(None, None, "grp", "rep", None),
            P(None, "rep", "grp", None),
            P(),
            P(),
            P("grp"),
            P("grp", None),
            P("grp", None),
            P("grp", None),
            P("grp", None),
            P("grp", None),
            P("grp"),
            P("grp", None),
            P("grp", None),
            P("grp", None),
        ),
        out_specs=(
            P(None, "rep", "grp", None),
            P(None, None, "grp", "rep", None),
            P("grp"),
            P("grp", None),
            P("grp", None),
            P("grp", None),
            P("grp", None),
            P("grp", None),
            P("grp"),
            P("grp", None),
            P("grp", None),
            P("grp", None),
        ),
        check_vma=False,
    )
```

profile of v0, /device:TPU:0, one launch (start us, length us, event | category | flops | bytes accessed | tf_op | source)
XLA Modules:
  0.0 5353.7 jit_solution(10712748251646824416)
XLA Ops:
  40.2 97.7 %all-gather.33.cloned.1.call-done = bf16[2048,2048]{1,0:T(8,128)(2,1)} async-done(((bf16[256,2048]{1,0:T(8,128)(2,1)}), bf16[2048,2048]{1,0:T(8,128)(2,1)}) %all-gather.33.cloned.1.call-update) | async-done | bytes 8388624 | tf_op jit(solution)/shard_map/all_gather | solution.py:158
  150.5 112.7 %all-gather.35.cloned.1.call-done = bf16[2048,2048]{1,0:T(8,128)(2,1)} async-done(((bf16[256,2048]{1,0:T(8,128)(2,1)}), bf16[2048,2048]{1,0:T(8,128)(2,1)}) %all-gather.35.cloned.1.call-update) | async-done | bytes 8388624 | tf_op jit(solution)/shard_map/all_gather | solution.py:159
  285.4 173.7 %all-gather.31.cloned.1.call-done = bf16[2048,3456]{1,0:T(8,128)(2,1)} async-done(((bf16[256,3456]{1,0:T(8,128)(2,1)}), bf16[2048,3456]{1,0:T(8,128)(2,1)}) %all-gather.31.cloned.1.call-update) | async-done | bytes 14155792 | tf_op jit(solution)/shard_map/all_gather | solution.py:160
  488.9 89.6 %all-gather.4 = bf16[8,1,256]{2,1,0:T(2,128)(2,1)S(1)} all-gather(bf16[1,1,256]{2,1,0:T(2,128)(2,1)S(1)} %reshape.449), channel_id=1, replica_groups=mesh['rep'=4,'grp'=8] {'grp'}, dimensions={0}, use_global_device_ids=true | all-gather | bytes 4608 | tf_op jit(solution)/shard_map/all_gather | solution.py:214
  606.9 947.4 %all-gather.69.cloned.1.call-done = f32[16,8,256,432]{2,3,1,0:T(8,128)} async-done(((f32[2,8,256,432]{2,3,1,0:T(8,128)}), f32[16,8,256,432]{2,3,1,0:T(8,128)}) %all-gather.69.cloned.1.call-update) | async-done | bytes 56623120 | tf_op jit(solution)/shard_map/all_gather | solution.py:19
  1580.8 171.1 %all-gather.29.cloned.1.call-done = bf16[2048,3456]{1,0:T(8,128)(2,1)} async-done(((bf16[256,3456]{1,0:T(8,128)(2,1)}), bf16[2048,3456]{1,0:T(8,128)(2,1)}) %all-gather.29.cloned.1.call-update) | async-done | bytes 14155792 | tf_op jit(solution)/shard_map/all_gather | solution.py:161
  1764.0 183.9 %all-gather.37.cloned.1.call-done = bf16[3456,2048]{1,0:T(8,128)(2,1)} async-done(((bf16[432,2048]{1,0:T(8,128)(2,1)}), bf16[3456,2048]{1,0:T(8,128)(2,1)}) %all-gather.37.cloned.1.call-update) | async-done | bytes 14155792 | tf_op jit(solution)/shard_map/all_gather | solution.py:162
  1959.6 184.3 %all-gather.39.cloned.1.call-done = bf16[2048,3456]{1,0:T(8,128)(2,1)} async-done(((bf16[256,3456]{1,0:T(8,128)(2,1)}), bf16[2048,3456]{1,0:T(8,128)(2,1)}) %all-gather.39.cloned.1.call-update) | async-done | bytes 14155792 | tf_op jit(solution)/shard_map/all_gather | solution.py:211
  2152.9 187.0 %all-gather.41.cloned.1.call-done = bf16[2048,3456]{1,0:T(8,128)(2,1)} async-done(((bf16[256,3456]{1,0:T(8,128)(2,1)}), bf16[2048,3456]{1,0:T(8,128)(2,1)}) %all-gather.41.cloned.1.call-update) | async-done | bytes 14155792 | tf_op jit(solution)/shard_map/all_gather | solution.py:212
  2348.9 187.0 %all-gather.43.cloned.1.call-done = bf16[3456,2048]{1,0:T(8,128)(2,1)} async-done(((bf16[432,2048]{1,0:T(8,128)(2,1)}), bf16[3456,2048]{1,0:T(8,128)(2,1)}) %all-gather.43.cloned.1.call-update) | async-done | bytes 14155792 | tf_op jit(solution)/shard_map/all_gather | solution.py:213
  2680.6 471.5 %all-gather.71.cloned.1.call-done = bf16[16,8,256,432]{2,3,1,0:T(8,128)(2,1)} async-done(((bf16[2,8,256,432]{2,3,1,0:T(8,128)(2,1)}), bf16[16,8,256,432]{2,3,1,0:T(8,128)(2,1)}) %all-gather.71.cloned.1.call-update) | async-done | bytes 28311568 | tf_op jit(solution)/shard_map/all_gather | solution.py:35
  3156.5 138.3 %while.27 = (s32[]{:T(128)}, f32[2,8,256,432]{3,2,1,0:T(8,128)}, s32[]{:T(128)}, bf16[8,8]{1,0:T(8,128)(2,1)S(1)}, bf16[8,2,8,256,432]{3,4,2,1,0:T(8,128)(2,1)},...) while((s32[]{:T(128)}, f32[2,8,256,432]{3,2,1,0:T(8,128)}, s32[]{:T(128)}, bf16[8,8]{1,0:T(8,128)(2,1)S(1)}, ...), condition=%wide.region_9.10_spmd, body=%wide.region_8.9_spmd.sunk | while | flops 5308430 | bytes 31850724 | solution.py:50
  3316.0 159.7 %all-gather.55.cloned.1.call-done = bf16[2048,3456]{1,0:T(8,128)(2,1)} async-done(((bf16[256,3456]{1,0:T(8,128)(2,1)}), bf16[2048,3456]{1,0:T(8,128)(2,1)}) %all-gather.55.cloned.1.call-update) | async-done | bytes 14155792 | tf_op jit(solution)/shard_map/all_gather | solution.py:115
  3485.2 116.3 %all-gather.67.cloned.1.call-done = bf16[2048,2048]{1,0:T(8,128)(2,1)} async-done(((bf16[256,2048]{1,0:T(8,128)(2,1)}), bf16[2048,2048]{1,0:T(8,128)(2,1)}) %all-gather.67.cloned.1.call-update) | async-done | bytes 8388624 | tf_op jit(solution)/shard_map/all_gather | solution.py:116
  3601.5 195.9 %all-gather.65.cloned.1.call-done = bf16[2048,3456]{1,0:T(8,128)(2,1)} async-done(((bf16[256,3456]{1,0:T(8,128)(2,1)}), bf16[2048,3456]{1,0:T(8,128)(2,1)}) %all-gather.65.cloned.1.call-update) | async-done | bytes 14155792 | tf_op jit(solution)/shard_map/all_gather | solution.py:115
  3806.9 115.6 %all-gather.59.cloned.1.call-done = bf16[2048,2048]{1,0:T(8,128)(2,1)} async-done(((bf16[256,2048]{1,0:T(8,128)(2,1)}), bf16[2048,2048]{1,0:T(8,128)(2,1)}) %all-gather.59.cloned.1.call-update) | async-done | bytes 8388624 | tf_op jit(solution)/shard_map/all_gather | solution.py:115
  3922.5 195.9 %all-gather.63.cloned.1.call-done = bf16[2048,3456]{1,0:T(8,128)(2,1)} async-done(((bf16[256,3456]{1,0:T(8,128)(2,1)}), bf16[2048,3456]{1,0:T(8,128)(2,1)}) %all-gather.63.cloned.1.call-update) | async-done | bytes 14155792 | tf_op jit(solution)/shard_map/all_gather | solution.py:116
  4129.0 185.3 %all-gather.61.cloned.1.call-done = bf16[2048,3456]{1,0:T(8,128)(2,1)} async-done(((bf16[256,3456]{1,0:T(8,128)(2,1)}), bf16[2048,3456]{1,0:T(8,128)(2,1)}) %all-gather.61.cloned.1.call-update) | async-done | bytes 14155792 | tf_op jit(solution)/shard_map/all_gather | solution.py:116
  4325.3 114.7 %all-gather.45.cloned.1.call-done = bf16[2048,2048]{1,0:T(8,128)(2,1)} async-done(((bf16[256,2048]{1,0:T(8,128)(2,1)}), bf16[2048,2048]{1,0:T(8,128)(2,1)}) %all-gather.45.cloned.1.call-update) | async-done | bytes 8388624 | tf_op jit(solution)/shard_map/all_gather | solution.py:115
  4440.0 196.6 %all-gather.53.cloned.1.call-done = bf16[2048,3456]{1,0:T(8,128)(2,1)} async-done(((bf16[256,3456]{1,0:T(8,128)(2,1)}), bf16[2048,3456]{1,0:T(8,128)(2,1)}) %all-gather.53.cloned.1.call-update) | async-done | bytes 14155792 | tf_op jit(solution)/shard_map/all_gather | solution.py:116
  4647.2 114.5 %all-gather.49.cloned.1.call-done = bf16[2048,2048]{1,0:T(8,128)(2,1)} async-done(((bf16[256,2048]{1,0:T(8,128)(2,1)}), bf16[2048,2048]{1,0:T(8,128)(2,1)}) %all-gather.49.cloned.1.call-update) | async-done | bytes 8388624 | tf_op jit(solution)/shard_map/all_gather | solution.py:116
  4768.8 118.2 %all-gather.47.cloned.1.call-done = bf16[2048,2048]{1,0:T(8,128)(2,1)} async-done(((bf16[256,2048]{1,0:T(8,128)(2,1)}), bf16[2048,2048]{1,0:T(8,128)(2,1)}) %all-gather.47.cloned.1.call-update) | async-done | bytes 8388624 | tf_op jit(solution)/shard_map/all_gather | solution.py:116
  4894.1 189.5 %all-gather.51.cloned.1.call-done = bf16[2048,3456]{0,1:T(8,128)(2,1)} async-done(((bf16[256,3456]{0,1:T(8,128)(2,1)}), bf16[2048,3456]{0,1:T(8,128)(2,1)}) %all-gather.51.cloned.1.call-update) | async-done | bytes 14155792 | tf_op jit(solution)/shard_map/all_gather | solution.py:116
  5191.9 137.4 %all-reduce.11.cloned.1.call-done = (bf16[256,2048]{1,0:T(8,128)(2,1)}, bf16[256,2048]{1,0:T(8,128)(2,1)}, bf16[256,3456]{1,0:T(8,128)(2,1)}, bf16[256,3456]{1,0...) async-done(((bf16[256,2048]{1,0:T(8,128)(2,1)}, bf16[256,2048]{1,0:T(8,128)(2,1)}, ...) | async-done | bytes 12714000 | tf_op jit(solution)/shard_map/psum | solution.py:317
  (317 shorter events, 692.1 us)
Async XLA Ops:
  7.2 130.7 %all-gather.33.cloned.1.call-start = ((), (), s32[]{:S(2)}) async-start(), calls=%async_computation.4 | async-start | bytes 9437184 | tf_op jit(solution)/shard_map/all_gather | solution.py:158
  7.9 255.2 %all-gather.35.cloned.1.call-start = ((), (), s32[]{:S(2)}) async-start(), calls=%async_computation.5 | async-start | bytes 9437184 | tf_op jit(solution)/shard_map/all_gather | solution.py:159
  8.7 450.5 %all-gather.31.cloned.1.call-start = ((), (), s32[]{:S(2)}) async-start(), calls=%async_computation.3 | async-start | bytes 15925248 | tf_op jit(solution)/shard_map/all_gather | solution.py:160
  16.5 1537.7 %all-gather.69.cloned.1.call-start = ((), (), s32[]{:S(2)}) async-start(), calls=%async_computation.22 | async-start | bytes 63700992 | tf_op jit(solution)/shard_map/all_gather | solution.py:19
  485.4 1266.5 %all-gather.29.cloned.1.call-start = ((), (), s32[]{:S(2)}) async-start(), calls=%async_computation.2 | async-start | bytes 15925248 | tf_op jit(solution)/shard_map/all_gather | solution.py:161
  486.0 1461.8 %all-gather.37.cloned.1.call-start = ((), (), s32[]{:S(2)}) async-start(), calls=%async_computation.6 | async-start | bytes 15925248 | tf_op jit(solution)/shard_map/all_gather | solution.py:162
  486.6 1657.3 %all-gather.39.cloned.1.call-start = ((), (), s32[]{:S(2)}) async-start(), calls=%async_computation.7 | async-start | bytes 15925248 | tf_op jit(solution)/shard_map/all_gather | solution.py:211
  487.4 1852.6 %all-gather.41.cloned.1.call-start = ((), (), s32[]{:S(2)}) async-start(), calls=%async_computation.8 | async-start | bytes 15925248 | tf_op jit(solution)/shard_map/all_gather | solution.py:212
  488.1 2047.8 %all-gather.43.cloned.1.call-start = ((), (), s32[]{:S(2)}) async-start(), calls=%async_computation.9 | async-start | bytes 15925248 | tf_op jit(solution)/shard_map/all_gather | solution.py:213
  488.8 2663.3 %all-gather.71.cloned.1.call-start = ((), (), s32[]{:S(2)}) async-start(), calls=%async_computation.23 | async-start | bytes 31850496 | tf_op jit(solution)/shard_map/all_gather | solution.py:35
  2614.3 701.7 %all-gather.57.cloned.1.call-start = ((), (), s32[]{:S(2)}) async-start(), calls=%async_computation.16 | async-start | bytes 9437184 | tf_op jit(solution)/shard_map/all_gather | solution.py:116
  2615.0 860.6 %all-gather.55.cloned.1.call-start = ((), (), s32[]{:S(2)}) async-start(), calls=%async_computation.15 | async-start | bytes 15925248 | tf_op jit(solution)/shard_map/all_gather | solution.py:115
  2615.6 985.9 %all-gather.67.cloned.1.call-start = ((), (), s32[]{:S(2)}) async-start(), calls=%async_computation.21 | async-start | bytes 9437184 | tf_op jit(solution)/shard_map/all_gather | solution.py:116
  2616.3 1181.0 %all-gather.65.cloned.1.call-start = ((), (), s32[]{:S(2)}) async-start(), calls=%async_computation.20 | async-start | bytes 15925248 | tf_op jit(solution)/shard_map/all_gather | solution.py:115
  2616.9 1305.6 %all-gather.59.cloned.1.call-start = ((), (), s32[]{:S(2)}) async-start(), calls=%async_computation.17 | async-start | bytes 9437184 | tf_op jit(solution)/shard_map/all_gather | solution.py:115
  2617.5 1500.8 %all-gather.63.cloned.1.call-start = ((), (), s32[]{:S(2)}) async-start(), calls=%async_computation.19 | async-start | bytes 15925248 | tf_op jit(solution)/shard_map/all_gather | solution.py:116
  2618.1 1696.1 %all-gather.61.cloned.1.call-start = ((), (), s32[]{:S(2)}) async-start(), calls=%async_computation.18 | async-start | bytes 15925248 | tf_op jit(solution)/shard_map/all_gather | solution.py:116
  2618.7 1821.3 %all-gather.45.cloned.1.call-start = ((), (), s32[]{:S(2)}) async-start(), calls=%async_computation.10 | async-start | bytes 9437184 | tf_op jit(solution)/shard_map/all_gather | solution.py:115
  2619.3 2017.3 %all-gather.53.cloned.1.call-start = ((), (), s32[]{:S(2)}) async-start(), calls=%async_computation.14 | async-start | bytes 15925248 | tf_op jit(solution)/shard_map/all_gather | solution.py:116
  2620.0 2141.7 %all-gather.49.cloned.1.call-start = ((), (), s32[]{:S(2)}) async-start(), calls=%async_computation.12 | async-start | bytes 9437184 | tf_op jit(solution)/shard_map/all_gather | solution.py:116
  3304.1 1582.9 %all-gather.47.cloned.1.call-start = ((), (), s32[]{:S(2)}) async-start(), calls=%async_computation.11 | async-start | bytes 9437184 | tf_op jit(solution)/shard_map/all_gather | solution.py:116
  3306.2 1777.3 %all-gather.51.cloned.1.call-start = ((), (), s32[]{:S(2)}) async-start(), calls=%async_computation.13 | async-start | bytes 15925248 | tf_op jit(solution)/shard_map/all_gather | solution.py:116
  3315.7 2013.7 %all-reduce.11.cloned.1.call-start = ((), (), s32[]{:S(2)}) async-start(), calls=%async_computation.24 | async-start | bytes 25427968 | tf_op jit(solution)/shard_map/psum | solution.py:317
  5132.2 56.7 %all-to-all-start.1 = ((bf16[2,1,1,128,2048]{4,0,2,1,3:T(2,128)(2,1)}), bf16[2,1,1,128,2048]{4,0,2,1,3:T(2,128)(2,1)S(1)}, u32[]{:S(2)}, u32[]{:S(2)}) async-start(bf16[2,1,1,128,2048]{4,0,2,1,3:T(2,128)(2,1)} %copy.161), calls=%async_computation.1 | async-start | bytes 2097152 | tf_op jit(solution)/shard_map/all_to_all | solution.py:290
  (61 other events, 4416.0 us)
Sparse Core Ops, SparseCore 0:
  10.2 127.6 all-gather.32
  140.0 123.1 all-gather.34
  265.3 193.7 all-gather.30
  485.5 1068.6 all-gather.68
  1556.3 195.5 all-gather.28
  1753.9 193.8 all-gather.36
  1950.0 193.7 all-gather.38
  2146.1 193.7 all-gather.40
  2342.1 193.7 all-gather.42
  2614.4 537.6 all-gather.70
  3154.3 124.8 all-gather.56
  3281.8 193.7 all-gather.54
  3478.3 123.1 all-gather.66
  3603.6 193.7 all-gather.64
  3799.4 123.1 all-gather.58
  3924.6 193.7 all-gather.62
  4120.4 193.7 all-gather.60
  4316.8 123.1 all-gather.44
  4442.7 193.7 all-gather.52
  4638.5 123.1 all-gather.48
  4763.8 123.1 all-gather.46
  4889.6 193.9 all-gather.50
  5094.5 234.8 all-reduce.10
where the time goes:
time: 5360 us; the launch traced here: 5350 us
  waiting for transfers between devices  4570 us (85%)
  matrix products  275 us (5%)
  blocking collectives  222 us (4%)
  local copies, waits for them, and re-layouts  160 us (3%)
  other arithmetic  105 us (2%)
    all_gather x8, waiting for transfers between devices, weight_owners(): outputs_piece = lax.all_gather(outputs_b, 'grp', axis=0, tiled=True)  1120 us
    all_gather x1, waiting for transfers between devices, entering(): gathered = jax.tree.map(lambda a: lax.all_gather(a, axis), part)  947 us
    all_gather x4, waiting for transfers between devices, weight_owners(): inputs_piece = lax.all_gather(inputs_b, 'grp', axis=0, tiled=True)  586 us
    all_gather x1, waiting for transfers between devices, entering_2(): lax.all_gather(a.astype(kind), axis)  472 us
    all_gather x1, waiting for transfers between devices, body(): lax.all_gather(w_down, 'grp', axis=0, tiled=True)  187 us
    all_gather x1, waiting for transfers between devices, body(): lax.all_gather(w_up, 'grp', axis=0, tiled=True)  187 us
    all_gather x1, waiting for transfers between devices, body(): lax.all_gather(w_proj, 'grp', axis=0, tiled=True)  184 us
    all_gather x1, waiting for transfers between devices, body(): lax.all_gather(w_out, 'grp', axis=0, tiled=True)  184 us
  transfers between devices with their start and end apart: 25, of which 22 were waited for; matrix products, arithmetic and copies ran while one was open for 8% of the time, Pallas kernels for 0%

commit v1 on v0

v1 whole, which is shorter than its diff:
```python
import math

import jax
import jax.numpy as jnp
from jax import lax
from jax.sharding import PartitionSpec as P

HEADS = 8
KEY_DIM = 256
VAL_DIM = 432

EPS = 1e-06
GROUP_EPS = 1.0

f32 = jnp.float32
bf16 = jnp.bfloat16


def norm_rows(values, gain_vec):
    return values * lax.rsqrt(jnp.mean(values * values, axis=-1, keepdims=True) + EPS) * gain_vec


def dot(left, right):
    return jnp.dot(left, right, preferred_element_type=f32)


def dot_t(left, right):
    return lax.dot_general(left, right, (((1,), (1,)), ((), ())), preferred_element_type=f32)


def t_dot(left, right):
    return lax.dot_general(left, right, (((0,), (0,)), ((), ())), preferred_element_type=f32)


def swap(value, bit):
    count = lax.axis_size("rep")
    return lax.ppermute(value, "rep", [(i, i ^ bit) for i in range(count)])


def bits_high():
    count = lax.axis_size("rep")
    return [1 << b for b in reversed(range(count.bit_length() - 1))]


def pieces_of_replicas(value):
    pieces = {0: value}
    for bit in bits_high():
        for place in list(pieces):
            pieces[place | bit] = swap(pieces[place], bit)
    return [pieces[place] for place in range(len(pieces))]


def rows_of_replicas(value):
    return jnp.concatenate(pieces_of_replicas(value), axis=0)


def sum_to_replicas(partial):
    count = lax.axis_size("rep")
    rows = partial.shape[0] // count
    held = {o: partial[o * rows : (o + 1) * rows] for o in range(count)}
    for bit in reversed(bits_high()):
        places = [o for o in held if not o & bit]
        sent = jnp.concatenate([held[o | bit] for o in places], axis=0).astype(bf16)
        came = swap(sent, bit)
        held = {
            o: held[o].astype(f32) + came[i * rows : (i + 1) * rows].astype(f32)
            for i, o in enumerate(places)
        }
    return held[0]


def columns_of_replicas(value):
    count = lax.axis_size("rep")
    rank = lax.axis_index("rep")
    stacked = jnp.stack(pieces_of_replicas(value))
    return jnp.concatenate(
        [lax.dynamic_index_in_dim(stacked, rank ^ o, 0, False) for o in range(count)], axis=1
    )


def own_columns(weight):
    count = lax.axis_size("rep")
    width = weight.shape[1] // count
    return lax.dynamic_slice_in_dim(weight, lax.axis_index("rep") * width, width, 1)


def gather_members(part):
    return lax.all_gather(part, "grp", axis=0, tiled=True)


def scatter_members(full):
    return lax.psum_scatter(full, "grp", scatter_dimension=0, tiled=True)


def slab_route():
    reps, members = lax.axis_size("rep"), lax.axis_size("grp")
    per = members // reps
    return [
        (s * members + m, (m // per) * members + reps * (m % per) + s)
        for s in range(reps)
        for m in range(members)
    ]


def gather_slab(weight):
    reps, members = lax.axis_size("rep"), lax.axis_size("grp")
    per = members // reps
    piece = lax.ppermute(own_columns(weight), ("rep", "grp"), slab_route())
    rows, width = piece.shape
    full = gather_members(piece).reshape(per, reps, rows, width)
    return full.transpose(0, 2, 1, 3).reshape(per * rows, reps * width)


def scatter_slab(grad):
    reps, members = lax.axis_size("rep"), lax.axis_size("grp")
    per = members // reps
    rows, width = grad.shape[0] // per, grad.shape[1] // reps
    parts = grad.reshape(per, rows, reps, width).transpose(0, 2, 1, 3)
    owned = scatter_members(parts.reshape(members * rows, width))
    piece = lax.ppermute(owned, ("rep", "grp"), [(b, a) for a, b in slab_route()])
    return columns_of_replicas(piece).astype(f32)


def body(
    tokens,
    cotangent,
    seq_lengths,
    bin_order,
    norm_gain,
    w_query,
    w_key,
    w_value,
    w_gate,
    w_out,
    mlp_gain,
    w_proj,
    w_up,
    w_down,
):
    reps, members = lax.axis_size("rep"), lax.axis_size("grp")
    rank, member = lax.axis_index("rep"), lax.axis_index("grp")
    micro, seqs, _, strip, width = tokens.shape
    own_rows = members * strip
    block = reps * strip
    heads = HEADS // reps
    qk_cols = heads * KEY_DIM
    val_cols = heads * VAL_DIM

    x_b = lax.all_to_all(
        tokens.reshape(members, strip, width), "grp", split_axis=0, concat_axis=0, tiled=True
    ).reshape(own_rows, width)
    x = x_b.astype(f32)

    gains = lax.all_gather(jnp.stack([norm_gain, mlp_gain]), "grp", axis=1, tiled=True).astype(f32)
    gain_one, gain_two = gains[0], gains[1]

    weight_qk = gather_members(jnp.concatenate([own_columns(w_query), own_columns(w_key)], axis=1))
    weight_vg = gather_members(jnp.concatenate([own_columns(w_value), own_columns(w_gate)], axis=1))
    weight_out = gather_slab(w_out)
    weight_pu = gather_members(jnp.concatenate([own_columns(w_proj), own_columns(w_up)], axis=1))
    weight_down = gather_slab(w_down)
    hid_cols = weight_down.shape[0]

    selector = (
        bin_order[:, :, None] == jnp.arange(seqs, dtype=jnp.int32)[None, None, :]
    ).astype(bf16)
    cot_bins = lax.all_to_all(
        cotangent.reshape(micro, reps, strip, width), "rep", split_axis=1, concat_axis=1, tiled=True
    )
    cot_seqs = jnp.einsum("msk,mkrd->msrd", selector, cot_bins, preferred_element_type=f32)
    cot_own = lax.all_to_all(
        cot_seqs.astype(bf16).reshape(members, strip, width),
        "grp",
        split_axis=0,
        concat_axis=0,
        tiled=True,
    ).reshape(own_rows, width)

    strip_pos = (
        jnp.arange(members, dtype=jnp.int32)[:, None] * block
        + jnp.arange(strip, dtype=jnp.int32)[None, :]
    ).reshape(own_rows)
    positions = jnp.concatenate([strip_pos + strip * (rank ^ o) for o in range(reps)])
    live_len = lax.dynamic_index_in_dim(seq_lengths.reshape(-1), member, 0, False)
    live = (positions[:own_rows] < live_len).astype(f32)[:, None]
    out_grad = cot_own.astype(f32) * live
    out_grad_full = rows_of_replicas(out_grad.astype(bf16))

    normed, norm_pullback = jax.vjp(norm_rows, x, gain_one)
    acts = rows_of_replicas(normed.astype(bf16))
    qk_pre = dot(acts, weight_qk)
    vg_pre = dot(acts, weight_vg)
    value = vg_pre[:, :val_cols].astype(bf16)
    gate_pre = vg_pre[:, val_cols:]

    frequency = jnp.exp(
        -jnp.arange(KEY_DIM // 2, dtype=f32) * (2.0 / KEY_DIM) * math.log(10000.0)
    )
    angles = positions.astype(f32)[:, None] * frequency[None, :]
    cosine, sine = jnp.cos(angles), jnp.sin(angles)

    def turn(pre, sign):
        half = KEY_DIM // 2
        front, back = pre[:, :half], pre[:, half:]
        return jnp.concatenate(
            [front * cosine - sign * back * sine, back * cosine + sign * front * sine], axis=1
        )

    lag = (positions[:, None] - positions[None, :]).astype(f32)

    def decay(h):
        head = (rank * heads + h).astype(f32)
        log_gamma = jnp.log(1.0 - jnp.exp2(-5.0 - head))
        return jnp.where(lag >= 0, jnp.exp(jnp.maximum(lag, 0.0) * log_gamma), 0.0)

    def mix_tail(retained, gate):
        normed = retained * lax.rsqrt(
            jnp.mean(retained * retained, axis=-1, keepdims=True) + GROUP_EPS
        )
        return jax.nn.silu(gate) * normed

    query, key, values, weights, mixed, tails = [], [], [], [], [], []
    for h in range(heads):
        query.append(turn(qk_pre[:, h * KEY_DIM : (h + 1) * KEY_DIM], 1.0).astype(bf16))
        key.append(
            turn(qk_pre[:, qk_cols + h * KEY_DIM : qk_cols + (h + 1) * KEY_DIM], 1.0).astype(bf16)
        )
        values.append(value[:, h * VAL_DIM : (h + 1) * VAL_DIM])
        weights.append((dot_t(query[h], key[h]) * decay(h)).astype(bf16))
        retained = dot(weights[h], values[h])
        mix, pull = jax.vjp(mix_tail, retained, gate_pre[:, h * VAL_DIM : (h + 1) * VAL_DIM])
        mixed.append(mix.astype(bf16))
        tails.append(pull)
    mixed_b = jnp.concatenate(mixed, axis=1)

    hidden = x + sum_to_replicas(dot(mixed_b, weight_out))
    normed_mid, mid_pullback = jax.vjp(norm_rows, hidden, gain_two)
    middle = rows_of_replicas(normed_mid.astype(bf16))
    pu_pre = dot(middle, weight_pu)

    def glu_act(proj_pre, up_pre):
        return jax.nn.gelu(proj_pre, approximate=True) * up_pre

    glu_rows, glu_pullback = jax.vjp(glu_act, pu_pre[:, :hid_cols], pu_pre[:, hid_cols:])
    glu_b = glu_rows.astype(bf16)
    out_rows = hidden + sum_to_replicas(dot(glu_b, weight_down))

    out_seqs = lax.all_to_all(
        out_rows.astype(bf16).reshape(members, strip, width),
        "grp",
        split_axis=0,
        concat_axis=0,
        tiled=True,
    ).reshape(micro, seqs, strip, width)
    out_bins = jnp.einsum("msk,msrd->mkrd", selector, out_seqs, preferred_element_type=f32)
    bin_out = lax.all_to_all(
        out_bins.astype(bf16), "rep", split_axis=1, concat_axis=1, tiled=True
    ).reshape(micro, 1, block, width)

    glu_grad = dot_t(out_grad_full, weight_down)
    proj_grad, up_grad = glu_pullback(glu_grad)
    pu_grad = jnp.concatenate([proj_grad, up_grad], axis=1).astype(bf16)
    down_owned = scatter_slab(t_dot(glu_b, out_grad_full).astype(bf16))
    pu_owned = scatter_members(t_dot(middle, pu_grad).astype(bf16))
    middle_grad = sum_to_replicas(dot_t(pu_grad, weight_pu))
    hidden_grad = out_grad + mid_pullback(middle_grad)[0]
    branch = rows_of_replicas(hidden_grad.astype(bf16))
    out_owned = scatter_slab(t_dot(mixed_b, branch).astype(bf16))
    mixed_grad = dot_t(branch, weight_out)

    query_grads, key_grads, value_grads, gate_grads = [], [], [], []
    for h in range(heads):
        retained_grad, gate_grad = tails[h](mixed_grad[:, h * VAL_DIM : (h + 1) * VAL_DIM])
        retained_b = retained_grad.astype(bf16)
        gate_grads.append(gate_grad.astype(bf16))
        score_b = (dot_t(retained_b, values[h]) * decay(h)).astype(bf16)
        value_grads.append(t_dot(weights[h], retained_b).astype(bf16))
        query_grads.append(turn(dot(score_b, key[h]), -1.0).astype(bf16))
        key_grads.append(turn(t_dot(score_b, query[h]), -1.0).astype(bf16))
    vg_grad = jnp.concatenate(value_grads + gate_grads, axis=1)
    qk_grad = jnp.concatenate(query_grads + key_grads, axis=1)
    vg_owned = scatter_members(t_dot(acts, vg_grad).astype(bf16))
    qk_owned = scatter_members(t_dot(acts, qk_grad).astype(bf16))
    act_grad = sum_to_replicas(dot_t(qk_grad, weight_qk) + dot_t(vg_grad, weight_vg))
    input_grad = hidden_grad + norm_pullback(act_grad)[0]
    token_grad = lax.all_to_all(
        input_grad.astype(bf16).reshape(members, strip, width),
        "grp",
        split_axis=0,
        concat_axis=0,
        tiled=True,
    ).reshape(tokens.shape)

    def finish(owned, split):
        return (
            columns_of_replicas(owned[:, :split]).astype(f32),
            columns_of_replicas(owned[:, split:]).astype(f32),
        )

    proj_owned, up_owned = finish(pu_owned, hid_cols)
    value_owned, gate_owned = finish(vg_owned, val_cols)
    query_owned, key_owned = finish(qk_owned, qk_cols)

    def gain_grad(gain, pairs):
        total = sum(jnp.sum(w.astype(f32) * g, axis=1) for w, g in pairs)
        return total / gain.astype(f32)

    gain_one_owned = gain_grad(
        norm_gain,
        (
            (w_query, query_owned),
            (w_key, key_owned),
            (w_value, value_owned),
            (w_gate, gate_owned),
        ),
    )
    gain_two_owned = gain_grad(mlp_gain, ((w_proj, proj_owned), (w_up, up_owned)))
    return (
        bin_out,
        token_grad,
        gain_one_owned,
        query_owned,
        key_owned,
        value_owned,
        gate_owned,
        out_owned,
        gain_two_owned,
        proj_owned,
        up_owned,
        down_owned,
    )


def solution(mesh):
    return jax.shard_map(
        body,
        mesh=mesh,
        in_specs=(
            P(None, None, "grp", "rep", None),
            P(None, "rep", "grp", None),
            P(),
            P(),
            P("grp"),
            P("grp", None),
            P("grp", None),
            P("grp", None),
            P("grp", None),
            P("grp", None),
            P("grp"),
            P("grp", None),
            P("grp", None),
            P("grp", None),
        ),
        out_specs=(
            P(None, "rep", "grp", None),
            P(None, None, "grp", "rep", None),
            P("grp"),
            P("grp", None),
            P("grp", None),
            P("grp", None),
            P("grp", None),
            P("grp", None),
            P("grp"),
            P("grp", None),
            P("grp", None),
            P("grp", None),
        ),
        check_vma=False,
    )
```

time: 5360 us -> 1250 us (0.23)
  waiting for transfers between devices: 4570 us -> 620 us
  blocking collectives: 222 us -> 42.6 us
  starting transfers between devices: 8.76 us -> 185 us
  matrix products: 275 us -> 179 us
    all_gather x22 -> x5, waiting for transfers between devices: 4420 us -> 205 us  [gather_members(): return lax.all_gather(part, 'grp', axis=0, tiled=True)]
    reduce_scatter x0 -> x5, waiting for transfers between devices: none -> 206 us  [scatter_members(): return lax.psum_scatter(full, 'grp', scatter_dimension=0, tiled=True)]
    ppermute x0 -> x48, waiting for transfers between devices: none -> 152 us  [the longest x44 152 us: swap(): return lax.ppermute(value, 'rep', [(i, i ^ bit) for i in range(count)])]
    all_gather x4 -> x1, blocking collectives: 181 us -> 42.6 us  [body(): lax.all_gather(jnp.stack([norm_gain, mlp_gain]), 'grp', axis=1, tiled=True)]
    psum x1 -> x0, waiting for transfers between devices: 137 us -> none  [body(): lax.psum(query_owned.astype(jnp.bfloat16), 'rep').astype(jnp.float32)]
    ppermute x0 -> x48, starting transfers between devices: none -> 104 us  [the longest x44 96.2 us: swap(): return lax.ppermute(value, 'rep', [(i, i ^ bit) for i in range(count)])]
    dot_general x38 -> x29, matrix products: 275 us -> 179 us  [the longest x9 67 us: dot_t(): lax.dot_general(left, right, (((1,), (1,)), ((), ())), preferred_element_...]
    all_to_all x2 -> x6, starting transfers between devices: 7.72 us -> 80.4 us  [the longest x1 56.8 us: body(): lax.all_to_all(tokens.reshape(members, strip, width), 'grp', split_axis=0...]
  transfers between devices with their start and end apart: 25 -> 64, of which waited for: 22 -> 24; matrix products, arithmetic and copies ran while one was open for 8% -> 26% of each run, Pallas kernels for 0% -> 0%
where the time goes in v1:
time: 1250 us
  waiting for transfers between devices  620 us (50%)
  starting transfers between devices  185 us (15%)
  matrix products  179 us (14%)
  local copies, waits for them, and re-layouts  107 us (9%)
  other arithmetic  95.1 us (8%)
  blocking collectives  42.6 us (3%)
  between operations  16.4 us (1%)
    reduce_scatter x5, waiting for transfers between devices, scatter_members(): return lax.psum_scatter(full, 'grp', scatter_dimension=0, tiled=True)  206 us
    all_gather x5, waiting for transfers between devices, gather_members(): return lax.all_gather(part, 'grp', axis=0, tiled=True)  205 us
    ppermute x44, waiting for transfers between devices, swap(): return lax.ppermute(value, 'rep', [(i, i ^ bit) for i in range(count)])  152 us
    ppermute x44, starting transfers between devices, swap(): return lax.ppermute(value, 'rep', [(i, i ^ bit) for i in range(count)])  96.2 us
    dot_general x9, matrix products, dot_t(): lax.dot_general(left, right, (((1,), (1,)), ((), ())), preferred_element_...  67 us
    dot_general x9, matrix products, dot(): return jnp.dot(left, right, preferred_element_type=f32)  58.5 us
    all_to_all x1, starting transfers between devices, body(): lax.all_to_all(tokens.reshape(members, strip, width), 'grp', split_axis=0...  56.8 us
    unnamed x224, local copies, waits for them, and re-layouts  51.5 us
  transfers between devices with their start and end apart: 64, of which 24 were waited for; matrix products, arithmetic and copies ran while one was open for 26% of the time, Pallas kernels for 0%

profile of v1, /device:TPU:0, one launch (start us, length us, event | category | flops | bytes accessed | tf_op | source)
XLA Modules:
  0.0 1245.7 jit_solution(17834495869704101999)
XLA Ops:
  17.9 56.8 %all-to-all-start = ((bf16[8,32,2048]{2,1,0:T(8,128)(2,1)}), bf16[8,32,2048]{2,1,0:T(8,128)(2,1)S(1)}, u32[]{:S(2)}, u32[]{:S(2)}) async-start(bf16[8,32,2048]{2,1,0:T(8,128)(2,1)} %bitcast.1), calls=%async_computation | async-start | bytes 2097152 | tf_op jit(solution)/shard_map/all_to_all | solution.py:149
  74.8 42.6 %all_gather.18 = bf16[2,2048]{1,0:T(2,128)(2,1)S(1)} all-gather(bf16[2,256]{1,0:T(2,128)(2,1)S(1)} %pad_maximum_fusion.46), channel_id=1, replica_groups=mesh['rep'=4,'grp'=8] {'grp'}, dimensions={1}, use_global_device_ids=true | all-gather | bytes 9216 | tf_op jit(solution)/shard_map/all_gather | solution.py:154
  118.1 37.4 %collective-permute-start.1 = (bf16[256,2048]{1,0:T(8,128)(2,1)S(1)}, bf16[256,2048]{1,0:T(8,128)(2,1)}, u32[]{:S(2)}, u32[]{:S(2)}) collective-permute-start(bf16[256,2048]{1,0:T(8,128)(2,1)S(1)} %fusion.27), channel_id=1, source_target_pairs={{0,16},{8,24},{16,0},{24,8},{1,17},{9,25},{17,1},{25,9},{2,18},{10... | collective-permute-start | bytes 3145736 | tf_op jit(solution)/shard_map/ppermute | solution.py:37
  178.1 54.0 %all-gather.8.cloned.1.call-done = bf16[2048,1024]{1,0:T(8,128)(2,1)} async-done(((bf16[256,1024]{1,0:T(8,128)(2,1)}), bf16[2048,1024]{1,0:T(8,128)(2,1)}) %all-gather.8.cloned.1.call-update) | async-done | bytes 4194320 | tf_op jit(solution)/shard_map/all_gather | solution.py:88
  248.9 96.3 %all-gather.6.cloned.1.call-done = bf16[2048,1728]{1,0:T(8,128)(2,1)} async-done(((bf16[256,1728]{1,0:T(8,128)(2,1)}), bf16[2048,1728]{1,0:T(8,128)(2,1)}) %all-gather.6.cloned.1.call-update) | async-done | bytes 7077904 | tf_op jit(solution)/shard_map/all_gather | solution.py:88
  345.2 14.7 %fusion.165 = (bf16[1024,1728]{0,1:T(8,128)(2,1)}, f32[1024,1728]{0,1:T(8,128)}) fusion(bf16[2048,1728]{1,0:T(8,128)(2,1)} %all-gather.6.cloned.1.call-done, bf16[256,2048]{1,0:T(8,128)(2,1)} %collective-permute-done.2, bf16[256,2048]{1,0:T(8,128)(2,1)} %collective-permute-done.1, bf16[256,2048]{1,0:T(8,128)(2,1)} %collective-permute-done, ...), kind=kOutput, calls=%fused_computation.324 | convolution fusion | flops 7266304000 | bytes 21889024 | tf_op jit(solution)/shard_map/dot_general | solution.py:24
  405.4 13.9 %collective-permute-done.5 = bf16[256,2048]{1,0:T(8,128)(2,1)} collective-permute-done((bf16[256,2048]{1,0:T(8,128)(2,1)S(1)}, bf16[256,2048]{1,0:T(8,128)(2,1)}, u32[]{:S(2)}, u32[]{:S(2)}) %collective-permute-start.5) | collective-permute-done | bytes 1048608 | tf_op jit(solution)/shard_map/ppermute | solution.py:37
  424.2 13.5 %all-to-all-done.4 = bf16[8,32,2048]{2,1,0:T(8,128)(2,1)} async-done(((bf16[8,32,2048]{2,1,0:T(8,128)(2,1)}), bf16[8,32,2048]{2,1,0:T(8,128)(2,1)}, u32[]{:S(2)}, u32[]{:S(2)}) %all-to-all-start.4) | async-done | bytes 1048608 | tf_op jit(solution)/shard_map/all_to_all | solution.py:171
  449.2 20.6 %collective-permute-done.13 = bf16[256,2048]{1,0:T(8,128)(2,1)} collective-permute-done((bf16[256,2048]{1,0:T(8,128)(2,1)}, bf16[256,2048]{1,0:T(8,128)(2,1)}, u32[]{:S(2)}, u32[]{:S(2)}) %collective-permute-start.13) | collective-permute-done | bytes 1048608 | tf_op jit(solution)/shard_map/ppermute | solution.py:37
  477.5 54.6 %all-gather.12.cloned.1.call-done = bf16[2048,1728]{1,0:T(8,128)(2,1)} async-done(((bf16[256,1728]{1,0:T(8,128)(2,1)}), bf16[2048,1728]{1,0:T(8,128)(2,1)}) %all-gather.12.cloned.1.call-update) | async-done | bytes 7077904 | tf_op jit(solution)/shard_map/all_gather | solution.py:88
  532.1 14.5 %fusion.80 = f32[1024,1728]{0,1:T(8,128)} fusion(bf16[2048,1728]{1,0:T(8,128)(2,1)} %all-gather.12.cloned.1.call-done, bf16[256,2048]{1,0:T(8,128)(2,1)} %collective-permute-done.8, bf16[256,2048]{1,0:T(8,128)(2,1)} %collective-permute-done.7, bf16[256,2048]{1,0:T(8,128)(2,1)} %collective-permute-done.6, bf16[256,2048]{1,0:T(8,128)(2,1)S(1)} %multiply_convert_fusion.6), kind=kOutput, calls=%fused_computation.172 | convolution fusion | flops 7264534528 | bytes 18350080 | tf_op jit(solution)/shard_map/dot_general | solution.py:24
  546.6 11.1 fusion.6
  557.6 11.7 fusion.167
  607.6 21.7 %collective-permute-done.16 = bf16[256,2048]{1,0:T(8,128)(2,1)S(1)} collective-permute-done((bf16[256,2048]{1,0:T(8,128)(2,1)S(1)}, bf16[256,2048]{1,0:T(8,128)(2,1)S(1)}, u32[]{:S(2)}, u32[]{:S(2)}) %collective-permute-start.16) | collective-permute-done | bytes 1048608 | tf_op jit(solution)/shard_map/ppermute | solution.py:37
  631.9 19.0 %collective-permute-done.11 = bf16[256,2048]{1,0:T(8,128)(2,1)S(1)} collective-permute-done((bf16[256,2048]{1,0:T(8,128)(2,1)S(1)}, bf16[256,2048]{1,0:T(8,128)(2,1)S(1)}, u32[]{:S(2)}, u32[]{:S(2)}) %collective-permute-start.11) | collective-permute-done | bytes 1048608 | tf_op jit(solution)/shard_map/ppermute | solution.py:37
  657.5 22.8 %collective-permute-done.18 = bf16[256,2048]{1,0:T(8,128)(2,1)S(1)} collective-permute-done((bf16[256,2048]{1,0:T(8,128)(2,1)S(1)}, bf16[256,2048]{1,0:T(8,128)(2,1)S(1)}, u32[]{:S(2)}, u32[]{:S(2)}) %collective-permute-start.18) | collective-permute-done | bytes 1048608 | tf_op jit(solution)/shard_map/ppermute | solution.py:37
  752.2 12.1 convolution_convert_fusion
  770.3 11.4 convolution_convert_fusion.1
  792.6 15.8 %fusion.169 = (bf16[1024,2048]{1,0:T(8,128)(2,1)}, f32[1024,2048]{1,0:T(8,128)}) fusion(f32[1024,2048]{1,0:T(8,128)} %fusion.170, bf16[2048,1728]{1,0:T(8,128)(2,1)} %all-gather.6.cloned.1.call-done, bf16[1024,432]{0,1:T(8,128)(2,1)S(1)} %copy-done.56, bf16[1024,432]{0,1:T(8,128)(2,1)S(1)} %copy-done.55, bf16[1024,432]{0,1:T(8,128)(2,1)S(1)} %copy-done.101, ...), kind=kOutput, calls=%fused_computation.328 | convolution fusion | flops 7266107392 | bytes 31588352 | tf_op jit(solution)/shard_map/dot_general | solution.py:28
  821.9 24.0 %all-to-all-done.1 = bf16[8,32,2048]{2,1,0:T(8,128)(2,1)S(1)} async-done(((bf16[8,32,2048]{2,1,0:T(8,128)(2,1)}), bf16[8,32,2048]{2,1,0:T(8,128)(2,1)S(1)}, u32[]{:S(2)}, u32[]{:S(2)}) %all-to-all-start.1) | async-done | bytes 1048608 | tf_op jit(solution)/shard_map/all_to_all | solution.py:248
  882.5 17.0 %collective-permute-start.45 = (bf16[432,512]{1,0:T(8,128)(2,1)}, bf16[432,512]{1,0:T(8,128)(2,1)}, u32[]{:S(2)}, u32[]{:S(2)}) collective-permute-start(bf16[432,512]{1,0:T(8,128)(2,1)} %collective-permute-done.44), channel_id=1, source_target_pairs={{0,8},{8,0},{16,24},{24,16},{1,9},{9,1},{17,25},{25,17},{2,10},{10... | collective-permute-start | bytes 1327112 | tf_op jit(solution)/shard_map/ppermute | solution.py:37
  899.6 18.8 %collective-permute-start.36 = (bf16[432,512]{1,0:T(8,128)(2,1)S(1)}, bf16[432,512]{1,0:T(8,128)(2,1)}, u32[]{:S(2)}, u32[]{:S(2)}) collective-permute-start(bf16[432,512]{1,0:T(8,128)(2,1)S(1)} %collective-permute-done.34), channel_id=1, source_target_pairs={{0,16},{8,24},{16,0},{24,8},{1,17},{9,25},{17,1},{25,9},{2,18},{10... | collective-permute-start | bytes 1327112 | tf_op jit(solution)/shard_map/ppermute | solution.py:37
  958.6 99.7 %reduce-scatter.12.cloned.1.call-done = bf16[256,1728]{0,1:T(8,128)(2,1)} async-done(((bf16[2048,1728]{0,1:T(8,128)(2,1)}), bf16[256,1728]{0,1:T(8,128)(2,1)}) %reduce-scatter.12.cloned.1.call-update) | async-done | bytes 884752 | tf_op jit(solution)/shard_map/reduce_scatter | solution.py:92
  1084.1 106.1 %reduce-scatter.8.cloned.1.call-done = bf16[256,1728]{0,1:T(8,128)(2,1)} async-done(((bf16[2048,1728]{0,1:T(8,128)(2,1)}), bf16[256,1728]{0,1:T(8,128)(2,1)}) %reduce-scatter.8.cloned.1.call-update) | async-done | bytes 884752 | tf_op jit(solution)/shard_map/reduce_scatter | solution.py:92
  (480 shorter events, 419.1 us)
Async XLA Ops:
  7.2 163.2 %all-gather.10.cloned.1.call-start = ((), (), s32[]{:S(2)}) async-start(), calls=%async_computation.13 | async-start | bytes 3981312 | tf_op jit(solution)/shard_map/all_gather | solution.py:88
  10.2 221.9 %all-gather.8.cloned.1.call-start = ((), (), s32[]{:S(2)}) async-start(), calls=%async_computation.12 | async-start | bytes 4718592 | tf_op jit(solution)/shard_map/all_gather | solution.py:88
  12.2 332.9 %all-gather.6.cloned.1.call-start = ((), (), s32[]{:S(2)}) async-start(), calls=%async_computation.11 | async-start | bytes 8257536 | tf_op jit(solution)/shard_map/all_gather | solution.py:88
  15.3 454.5 %all-gather.14.cloned.1.call-start = ((), (), s32[]{:S(2)}) async-start(), calls=%async_computation.15 | async-start | bytes 3981312 | tf_op jit(solution)/shard_map/all_gather | solution.py:88
  17.9 99.5 %all-to-all-start = ((bf16[8,32,2048]{2,1,0:T(8,128)(2,1)}), bf16[8,32,2048]{2,1,0:T(8,128)(2,1)S(1)}, u32[]{:S(2)}, u32[]{:S(2)}) async-start(bf16[8,32,2048]{2,1,0:T(8,128)(2,1)} %bitcast.1), calls=%async_computation | async-start | bytes 2097152 | tf_op jit(solution)/shard_map/all_to_all | solution.py:149
  74.7 457.4 %all-gather.12.cloned.1.call-start = ((), (), s32[]{:S(2)}) async-start(), calls=%async_computation.14 | async-start | bytes 8257536 | tf_op jit(solution)/shard_map/all_gather | solution.py:88
  118.1 50.3 %collective-permute-start.1 = (bf16[256,2048]{1,0:T(8,128)(2,1)S(1)}, bf16[256,2048]{1,0:T(8,128)(2,1)}, u32[]{:S(2)}, u32[]{:S(2)}) collective-permute-start(bf16[256,2048]{1,0:T(8,128)(2,1)S(1)} %fusion.27), channel_id=1, source_target_pairs={{0,16},{8,24},{16,0},{24,8},{1,17},{9,25},{17,1},{25,9},{2,18},{10... | collective-permute-start | bytes 3145736 | tf_op jit(solution)/shard_map/ppermute | solution.py:37
  405.3 447.9 %reduce-scatter.14.cloned.1.call-start = ((), (), s32[]{:S(2)}) async-start(), calls=%async_computation.20 | async-start | bytes 3981312 | tf_op jit(solution)/shard_map/reduce_scatter | solution.py:92
  441.5 90.5 %collective-permute-start.6 = (bf16[256,2048]{1,0:T(8,128)(2,1)S(1)}, bf16[256,2048]{1,0:T(8,128)(2,1)}, u32[]{:S(2)}, u32[]{:S(2)}) collective-permute-start(bf16[256,2048]{1,0:T(8,128)(2,1)S(1)} %multiply_convert_fusion.6), channel_id=1, source_target_pairs={{0,8},{8,0},{16,24},{24,16},{1,9},{9,1},{17,25},{25,17},{2,10},{10... | collective-permute-start | bytes 3145736 | tf_op jit(solution)/shard_map/ppermute | solution.py:37
  448.7 83.4 %collective-permute-start.8 = (bf16[256,2048]{1,0:T(8,128)(2,1)}, bf16[256,2048]{1,0:T(8,128)(2,1)}, u32[]{:S(2)}, u32[]{:S(2)}) collective-permute-start(bf16[256,2048]{1,0:T(8,128)(2,1)} %collective-permute-done.7), channel_id=1, source_target_pairs={{0,8},{8,0},{16,24},{24,16},{1,9},{9,1},{17,25},{25,17},{2,10},{10... | collective-permute-start | bytes 3145736 | tf_op jit(solution)/shard_map/ppermute | solution.py:37
  448.7 97.9 %collective-permute-start.12 = (bf16[256,2048]{1,0:T(8,128)(2,1)}, bf16[256,2048]{1,0:T(8,128)(2,1)}, u32[]{:S(2)}, u32[]{:S(2)}) collective-permute-start(bf16[256,2048]{1,0:T(8,128)(2,1)} %fusion.24), channel_id=1, source_target_pairs={{0,8},{8,0},{16,24},{24,16},{1,9},{9,1},{17,25},{25,17},{2,10},{10... | collective-permute-start | bytes 3145736 | tf_op jit(solution)/shard_map/ppermute | solution.py:37
  469.8 76.8 %collective-permute-start.14 = (bf16[256,2048]{1,0:T(8,128)(2,1)}, bf16[256,2048]{1,0:T(8,128)(2,1)}, u32[]{:S(2)}, u32[]{:S(2)}) collective-permute-start(bf16[256,2048]{1,0:T(8,128)(2,1)} %collective-permute-done.13), channel_id=1, source_target_pairs={{0,8},{8,0},{16,24},{24,16},{1,9},{9,1},{17,25},{25,17},{2,10},{10... | collective-permute-start | bytes 3145736 | tf_op jit(solution)/shard_map/ppermute | solution.py:37
  601.1 279.8 %reduce-scatter.10.cloned.1.call-start = ((), (), s32[]{:S(2)}) async-start(), calls=%async_computation.18 | async-start | bytes 3981312 | tf_op jit(solution)/shard_map/reduce_scatter | solution.py:92
  607.1 43.8 %collective-permute-start.11 = (bf16[256,2048]{1,0:T(8,128)(2,1)S(1)}, bf16[256,2048]{1,0:T(8,128)(2,1)S(1)}, u32[]{:S(2)}, u32[]{:S(2)}) collective-permute-start(bf16[256,2048]{1,0:T(8,128)(2,1)S(1)} %fusion.17), channel_id=1, source_target_pairs={{0,16},{8,24},{16,0},{24,8},{1,17},{9,25},{17,1},{25,9},{2,18},{10... | collective-permute-start | bytes 3145736 | tf_op jit(solution)/shard_map/ppermute | solution.py:37
  699.0 244.4 %reduce-scatter.6.cloned.1.call-start = ((), (), s32[]{:S(2)}) async-start(), calls=%async_computation.16 | async-start | bytes 4718592 | tf_op jit(solution)/shard_map/reduce_scatter | solution.py:92
  751.0 307.3 %reduce-scatter.12.cloned.1.call-start = ((), (), s32[]{:S(2)}) async-start(), calls=%async_computation.19 | async-start | bytes 7962624 | tf_op jit(solution)/shard_map/reduce_scatter | solution.py:92
  764.3 426.0 %reduce-scatter.8.cloned.1.call-start = ((), (), s32[]{:S(2)}) async-start(), calls=%async_computation.17 | async-start | bytes 7962624 | tf_op jit(solution)/shard_map/reduce_scatter | solution.py:92
  873.8 69.7 %all-to-all-start.5 = ((bf16[8,32,2048]{2,1,0:T(8,128)(2,1)}), bf16[8,32,2048]{2,1,0:T(8,128)(2,1)S(1)}, u32[]{:S(2)}, u32[]{:S(2)}) async-start(bf16[8,32,2048]{2,1,0:T(8,128)(2,1)} %bitcast.192), calls=%async_computation.5 | async-start | bytes 2097152 | tf_op jit(solution)/shard_map/all_to_all | solution.py:286
  882.5 50.6 %collective-permute-start.45 = (bf16[432,512]{1,0:T(8,128)(2,1)}, bf16[432,512]{1,0:T(8,128)(2,1)}, u32[]{:S(2)}, u32[]{:S(2)}) collective-permute-start(bf16[432,512]{1,0:T(8,128)(2,1)} %collective-permute-done.44), channel_id=1, source_target_pairs={{0,8},{8,0},{16,24},{24,16},{1,9},{9,1},{17,25},{25,17},{2,10},{10... | collective-permute-start | bytes 1327112 | tf_op jit(solution)/shard_map/ppermute | solution.py:37
  899.6 40.7 %collective-permute-start.36 = (bf16[432,512]{1,0:T(8,128)(2,1)S(1)}, bf16[432,512]{1,0:T(8,128)(2,1)}, u32[]{:S(2)}, u32[]{:S(2)}) collective-permute-start(bf16[432,512]{1,0:T(8,128)(2,1)S(1)} %collective-permute-done.34), channel_id=1, source_target_pairs={{0,16},{8,24},{16,0},{24,8},{1,17},{9,25},{17,1},{25,9},{2,18},{10... | collective-permute-start | bytes 1327112 | tf_op jit(solution)/shard_map/ppermute | solution.py:37
  945.0 116.1 %collective-permute-start.22 = (bf16[256,512]{1,0:T(8,128)(2,1)S(1)}, bf16[256,512]{1,0:T(8,128)(2,1)}, u32[]{:S(2)}, u32[]{:S(2)}) collective-permute-start(bf16[256,512]{1,0:T(8,128)(2,1)S(1)} %get-tuple-element.117), channel_id=1, source_target_pairs={{0,8},{8,0},{16,24},{24,16},{1,9},{9,1},{17,25},{25,17},{2,10},{10... | collective-permute-start | bytes 786440 | tf_op jit(solution)/shard_map/ppermute | solution.py:37
  947.0 115.9 %collective-permute-start.25 = (bf16[256,512]{1,0:T(8,128)(2,1)S(1)}, bf16[256,512]{1,0:T(8,128)(2,1)}, u32[]{:S(2)}, u32[]{:S(2)}) collective-permute-start(bf16[256,512]{1,0:T(8,128)(2,1)S(1)} %get-tuple-element.116), channel_id=1, source_target_pairs={{0,8},{8,0},{16,24},{24,16},{1,9},{9,1},{17,25},{25,17},{2,10},{10... | collective-permute-start | bytes 786440 | tf_op jit(solution)/shard_map/ppermute | solution.py:37
  954.3 106.8 %collective-permute-start.24 = (bf16[256,512]{1,0:T(8,128)(2,1)}, bf16[256,512]{1,0:T(8,128)(2,1)S(1)}, u32[]{:S(2)}, u32[]{:S(2)}) collective-permute-start(bf16[256,512]{1,0:T(8,128)(2,1)} %collective-permute-done.23), channel_id=1, source_target_pairs={{0,8},{8,0},{16,24},{24,16},{1,9},{9,1},{17,25},{25,17},{2,10},{10... | collective-permute-start | bytes 786440 | tf_op jit(solution)/shard_map/ppermute | solution.py:37
  958.5 104.6 %collective-permute-start.27 = (bf16[256,512]{1,0:T(8,128)(2,1)}, bf16[256,512]{1,0:T(8,128)(2,1)S(1)}, u32[]{:S(2)}, u32[]{:S(2)}) collective-permute-start(bf16[256,512]{1,0:T(8,128)(2,1)} %collective-permute-done.26), channel_id=1, source_target_pairs={{0,8},{8,0},{16,24},{24,16},{1,9},{9,1},{17,25},{25,17},{2,10},{10... | collective-permute-start | bytes 786440 | tf_op jit(solution)/shard_map/ppermute | solution.py:37
  (145 other events, 2564.4 us)
Sparse Core Ops, SparseCore 0:
  10.8 131.5 all-gather.9
  145.1 86.9 all-gather.7
  234.9 110.2 all-gather.5
  347.8 65.1 all-gather.13
  415.6 116.4 all-gather.11
  601.2 77.2 reduce-scatter.13
  699.1 77.2 reduce-scatter.9
  780.0 126.9 reduce-scatter.5
  911.1 147.0 reduce-scatter.11
  1061.8 128.4 reduce-scatter.7

commit v2 on v1

v2 whole, which is shorter than its diff:
```python
import functools
import math

import jax
import jax.numpy as jnp
from jax import lax
from jax.experimental import pallas as pl
from jax.experimental.pallas import tpu as pltpu
from jax.sharding import PartitionSpec as P

HEADS = 8
KEY_DIM = 256
VAL_DIM = 432

EPS = 1e-06
GROUP_EPS = 1.0

f32 = jnp.float32
bf16 = jnp.bfloat16


def norm_rows(values, gain_vec):
    return values * lax.rsqrt(jnp.mean(values * values, axis=-1, keepdims=True) + EPS) * gain_vec


def dot(left, right):
    return jnp.dot(left, right, preferred_element_type=f32)


def dot_t(left, right):
    return lax.dot_general(left, right, (((1,), (1,)), ((), ())), preferred_element_type=f32)


def t_dot(left, right):
    return lax.dot_general(left, right, (((0,), (0,)), ((), ())), preferred_element_type=f32)


def swap(value, bit):
    count = lax.axis_size("rep")
    return lax.ppermute(value, "rep", [(i, i ^ bit) for i in range(count)])


def bits_high():
    count = lax.axis_size("rep")
    return [1 << b for b in reversed(range(count.bit_length() - 1))]


latest = {}


def fence(*states, rings=()):
    leaves, tree = jax.tree.flatten(states)
    marks = [mark for ring in rings for mark in ring.marks()]
    fenced = lax.optimization_barrier((leaves, marks))[0]
    latest["mark"] = min(fenced, key=lambda leaf: leaf.size)
    for state, new in zip(states, jax.tree.unflatten(tree, fenced)):
        state.update(new)


def pieces_far(value):
    pieces = {0: value}
    for bit in bits_high()[:-1]:
        for place in list(pieces):
            pieces[place | bit] = swap(pieces[place], bit)
    return pieces


def pieces_near(pieces):
    pieces = dict(pieces)
    for place in list(pieces):
        pieces[place | 1] = swap(pieces[place], 1)
    return [pieces[place] for place in range(len(pieces))]


def pieces_of_replicas(value):
    return pieces_near(pieces_far(value))


def rows_near(pieces):
    return jnp.concatenate(pieces_near(pieces), axis=0)


def sum_send(held, bit):
    places = [o for o in held if not o & bit]
    sent = jnp.concatenate([held[o | bit].astype(bf16) for o in places], axis=0)
    return swap(sent, bit)


def sum_take(held, came, bit):
    places = [o for o in held if not o & bit]
    rows = came.shape[0] // len(places)
    return {
        o: held[o].astype(f32) + came[i * rows : (i + 1) * rows].astype(f32)
        for i, o in enumerate(places)
    }


def by_place(partial):
    count = lax.axis_size("rep")
    rows = partial.shape[0] // count
    return {o: partial[o * rows : (o + 1) * rows] for o in range(count)}


def sum_far(held):
    for bit in reversed(bits_high()[:-1]):
        held = sum_take(held, sum_send(held, bit), bit)
    return held[0]


def own_columns(weight):
    count = lax.axis_size("rep")
    width = weight.shape[1] // count
    return lax.dynamic_slice_in_dim(weight, lax.axis_index("rep") * width, width, 1)


def ring_members():
    count = lax.axis_size("grp")
    return list(range(0, count, 2)) + list(range(count - 1, 0, -2))


def ring_place():
    count, member = lax.axis_size("grp"), lax.axis_index("grp")
    return jnp.where(member % 2 == 0, member // 2, count - (member + 1) // 2)


def ring_step(value, ahead):
    ring = ring_members()
    count = len(ring)
    return lax.ppermute(
        value, "grp", [(ring[i], ring[(i + ahead) % count]) for i in range(count)]
    )


def ring_member(ahead):
    count = lax.axis_size("grp")
    place = (ring_place() + ahead) % count
    return jnp.where(place < count // 2, 2 * place, 2 * (count - place) - 1)


def gather_members(part):
    return lax.all_gather(part, "grp", axis=0, tiled=True)


def scatter_members(full):
    return lax.psum_scatter(full, "grp", scatter_dimension=0, tiled=True)


class Ring:
    def __init__(self, wide):
        half = lax.axis_size("grp") // 2
        self.left = [half if way == wide else half - 1 for way in (0, 1)]
        self.came = [[], []]

    def rest(self):
        while max(self.left) > 0:
            self.tick(free=True)

    def marks(self):
        return [came[-2] for came in self.came if len(came) > 1]

    def tick(self, free=False):
        for way, ahead in enumerate((1, -1)):
            if self.left[way] > 0:
                value = self.next(way, ahead)
                if not free:
                    value = lax.optimization_barrier((value, latest["mark"]))[0]
                self.came[way].append(ring_step(value, ahead))
                self.left[way] -= 1


class Gather(Ring):
    def __init__(self, part, wide):
        super().__init__(wide)
        self.part = part

    def next(self, way, ahead):
        return self.came[way][-1] if self.came[way] else self.part

    def pieces(self):
        self.rest()
        count = lax.axis_size("grp")
        pieces = {0: self.part}
        for way, ahead in enumerate((1, -1)):
            for i, came in enumerate(self.came[way]):
                pieces[-ahead * (i + 1) % count] = came
        return [pieces[i] for i in range(count)]


class Scatter(Ring):
    def __init__(self, rows, grad, wide):
        super().__init__(wide)
        self.full = t_dot(rows, grad).astype(bf16)

    def term(self, i):
        size = self.full.shape[0] // lax.axis_size("grp")
        return lax.dynamic_slice_in_dim(self.full, ring_member(i) * size, size, 0)

    def next(self, way, ahead):
        term = self.term((ahead * self.left[way]) % lax.axis_size("grp"))
        if self.came[way]:
            term = term.astype(f32) + self.came[way][-1].astype(f32)
        return term.astype(bf16)

    def whole(self):
        self.rest()
        total = self.term(0).astype(f32)
        for came in self.came:
            total = total + came[-1].astype(f32)
        return total.astype(bf16)


def assemble_kernel(spots, order_ref, *refs):
    count = len(spots)
    pieces, full_ref, held, in_sems, out_sems = (
        refs[:count],
        refs[count],
        refs[count + 1 : 2 * count + 1],
        refs[2 * count + 1],
        refs[2 * count + 2],
    )
    comes, goes = [], []
    for i, (place, member_rows, row, column) in enumerate(spots):
        rows, columns = pieces[i].shape
        start = pl.multiple_of(order_ref[place] * member_rows + row, rows)
        spot = full_ref.at[pl.ds(start, rows), pl.ds(column, columns)]
        comes.append(pltpu.make_async_copy(pieces[i], held[i], in_sems.at[i]))
        goes.append(pltpu.make_async_copy(held[i], spot, out_sems.at[i]))
    for come in comes:
        come.start()
    for come, go in zip(comes, goes):
        come.wait()
        go.start()
    for go in goes:
        go.wait()


def assembled(streams, member_rows, columns):
    members = lax.axis_size("grp")
    order = jnp.stack([ring_member(i) for i in range(members)]).astype(jnp.int32)
    pieces, spots = [], []
    for gather, row, column in streams:
        for i, piece in enumerate(gather.pieces()):
            pieces.append(piece)
            spots.append((i, member_rows, row, column))
    dtype = pieces[0].dtype
    size = members * member_rows * columns * dtype.itemsize
    return pl.pallas_call(
        functools.partial(assemble_kernel, spots),
        out_shape=jax.ShapeDtypeStruct((members * member_rows, columns), dtype),
        in_specs=[pl.BlockSpec(memory_space=pltpu.SMEM)]
        + [pl.BlockSpec(memory_space=pl.ANY)] * len(pieces),
        out_specs=pl.BlockSpec(memory_space=pl.ANY),
        scratch_shapes=[pltpu.VMEM(piece.shape, dtype) for piece in pieces]
        + [pltpu.SemaphoreType.DMA((len(pieces),))] * 2,
        compiler_params=pltpu.CompilerParams(vmem_limit_bytes=size + (2 << 20)),
        cost_estimate=pl.CostEstimate(flops=0, bytes_accessed=2 * size, transcendentals=0),
    )(order, *pieces)


def finish_kernel(reps, spots, summed, rank_ref, *refs):
    count = len(spots)
    pieces, refs = refs[:reps], refs[reps:]
    if summed:
        gain_ref, refs = refs[0], refs[1:]
        weights, refs = refs[:count], refs[count:]
    outs, refs = refs[:count], refs[count:]

    def lay(rank):
        for out_ref, (column, width) in zip(outs, spots):
            for r in range(reps):
                piece = pieces[rank ^ r][:, column : column + width].astype(f32)
                out_ref[:, r * width : (r + 1) * width] = piece

    for rank in range(reps):
        pl.when(rank_ref[0] == rank)(functools.partial(lay, rank))
    if summed:
        total = 0.0
        for out_ref, weight in zip(outs, weights):
            grad = out_ref[...]
            total += jnp.sum(weight[...].astype(f32) * grad, axis=1, keepdims=True)
        refs[0][...] = total / gain_ref[...].astype(f32)


def finished(pieces, spots, gain=None, weights=()):
    reps = len(pieces)
    rows, columns = pieces[0].shape
    step = rows
    for candidate in (64, 48, 72, 32):
        if rows % candidate == 0:
            step = candidate
            break
    rank = lax.axis_index("rep").astype(jnp.int32).reshape(1)

    def blocked(width):
        return pl.BlockSpec((step, width), lambda i: (i, 0))

    operands = [rank, *pieces]
    in_specs = [pl.BlockSpec(memory_space=pltpu.SMEM)] + [blocked(columns)] * reps
    shapes = [jax.ShapeDtypeStruct((rows, reps * width), f32) for _, width in spots]
    out_specs = [blocked(reps * width) for _, width in spots]
    if gain is not None:
        operands += [gain[:, None], *weights]
        in_specs += [blocked(1)] + [blocked(weight.shape[1]) for weight in weights]
        shapes.append(jax.ShapeDtypeStruct((rows, 1), f32))
        out_specs.append(blocked(1))
    size = sum(reps * width for _, width in spots) * rows
    return pl.pallas_call(
        functools.partial(finish_kernel, reps, spots, gain is not None),
        grid=(rows // step,),
        in_specs=in_specs,
        out_specs=out_specs,
        out_shape=shapes,
        compiler_params=pltpu.CompilerParams(vmem_limit_bytes=40 << 20),
        cost_estimate=pl.CostEstimate(flops=4 * size, bytes_accessed=8 * size, transcendentals=0),
    )(*operands)


def slab_routes():
    reps, members = lax.axis_size("rep"), lax.axis_size("grp")
    per = members // reps
    return [
        [
            (s * members + m, (m // per) * members + per * s + (m % per + turn) % per)
            for s in range(reps)
            for m in range(members)
        ]
        for turn in range(per)
    ]


def selected(choices, which):
    result = choices[0]
    for s in range(1, len(choices)):
        result = jnp.where(which == s, choices[s], result)
    return result


def slab_parts(weight):
    reps, members = lax.axis_size("rep"), lax.axis_size("grp")
    rank, member = lax.axis_index("rep"), lax.axis_index("grp")
    per = members // reps
    size = weight.shape[1] // members
    blocks = [per * rank + (member % per + turn) % per for turn in range(per)]
    return [lax.dynamic_slice_in_dim(weight, block * size, size, 1).T for block in blocks]


def slab_piece(parts):
    reps, members = lax.axis_size("rep"), lax.axis_size("grp")
    member = lax.axis_index("grp")
    per = members // reps
    came = [
        lax.ppermute(sent, ("rep", "grp"), route) for sent, route in zip(parts, slab_routes())
    ]
    return jnp.concatenate(
        [selected([came[(e - a) % per] for e in range(per)], member % per) for a in range(per)],
        axis=1,
    )


def slab_rows(owned):
    reps, members = lax.axis_size("rep"), lax.axis_size("grp")
    member = lax.axis_index("grp")
    per = members // reps
    rows = owned.shape[1] // per
    came = []
    for turn, route in enumerate(slab_routes()):
        owner = (member % per - turn + per) % per
        sent = lax.dynamic_slice_in_dim(owned, owner * rows, rows, 1)
        came.append(lax.ppermute(sent, ("rep", "grp"), [(b, a) for a, b in route]))
    mine = jnp.concatenate(
        [
            selected([came[(k - e) % per] for e in range(per)], member % per).T
            for k in range(per)
        ],
        axis=1,
    )
    return mine


def padded(value):
    gap = -value.shape[1] % 128
    return jnp.pad(value, ((0, 0), (0, gap))) if gap else value


def body(
    tokens,
    cotangent,
    seq_lengths,
    bin_order,
    norm_gain,
    w_query,
    w_key,
    w_value,
    w_gate,
    w_out,
    mlp_gain,
    w_proj,
    w_up,
    w_down,
):
    reps, members = lax.axis_size("rep"), lax.axis_size("grp")
    rank, member = lax.axis_index("rep"), lax.axis_index("grp")
    micro, seqs, _, strip, width = tokens.shape
    own_rows = members * strip
    block = reps * strip
    heads = HEADS // reps
    qk_cols = heads * KEY_DIM
    val_cols = heads * VAL_DIM
    hid_cols = w_proj.shape[1] // reps
    member_rows = width // members

    strip_pos = (
        jnp.arange(members, dtype=jnp.int32)[:, None] * block
        + jnp.arange(strip, dtype=jnp.int32)[None, :]
    ).reshape(own_rows)
    positions = jnp.concatenate([strip_pos + strip * (rank ^ o) for o in range(reps)])
    live_len = lax.dynamic_index_in_dim(seq_lengths.reshape(-1), member, 0, False)
    live = (positions[:own_rows] < live_len).astype(f32)[:, None]
    selector = (
        bin_order[:, :, None] == jnp.arange(seqs, dtype=jnp.int32)[None, None, :]
    ).astype(bf16)

    qkvg_own = jnp.concatenate(
        [padded(own_columns(weight)) for weight in (w_query, w_key, w_value, w_gate)],
        axis=1,
    )
    qkvg_cols = qkvg_own.shape[1]
    cut = qkvg_cols // 2
    qkvg = [Gather(qkvg_own[:, :cut], 0), Gather(qkvg_own[:, cut:], 1)]

    def tick(rings, free=False):
        for ring in rings:
            ring.tick(free)

    def mix_tail(retained, gate):
        normed = retained * lax.rsqrt(
            jnp.mean(retained * retained, axis=-1, keepdims=True) + GROUP_EPS
        )
        return jax.nn.silu(gate) * normed

    frequency = jnp.exp(
        -jnp.arange(KEY_DIM // 2, dtype=f32) * (2.0 / KEY_DIM) * math.log(10000.0)
    )
    angles = positions.astype(f32)[:, None] * frequency[None, :]
    log_gamma = jnp.log(1.0 - jnp.exp2(-5.0 - (rank * heads + jnp.arange(heads)).astype(f32)))
    spans = positions.astype(f32)[None, :] * log_gamma[:, None]
    t = {
        "cos": jnp.cos(angles),
        "sin": jnp.sin(angles),
        "grow": jnp.exp(spans),
        "shrink": jnp.exp(-spans),
    }

    for _ in range(members // 2):
        tick(qkvg, free=True)
    e = {
        "rows": lax.all_to_all(
            tokens.reshape(members, strip, width), "grp", split_axis=0, concat_axis=0, tiled=True
        ),
        "out": slab_parts(w_out),
        "down": slab_parts(w_down),
        "pu": [padded(own_columns(w_proj)), padded(own_columns(w_up))],
        "gains": lax.all_to_all(
            jnp.broadcast_to(jnp.stack([norm_gain, mlp_gain]), (members, 2, member_rows)),
            "grp",
            split_axis=0,
            concat_axis=0,
            tiled=True,
        ),
    }
    fence(e, t)
    cosine, sine = t["cos"], t["sin"]
    lag = positions[:, None] >= positions[None, :]

    def turn(pre, sign):
        half = KEY_DIM // 2
        front, back = pre[:, :half], pre[:, half:]
        return jnp.concatenate(
            [front * cosine - sign * back * sine, back * cosine + sign * front * sine], axis=1
        )

    def decayed(scores, h):
        decay = t["grow"][h][:, None] * t["shrink"][h][None, :]
        return (scores * jnp.where(lag, decay, 0.0)).astype(bf16)

    x = e["rows"].reshape(own_rows, width).astype(f32)
    gains = e.pop("gains").transpose(1, 0, 2).reshape(2, width).astype(f32)
    gain_one, gain_two = gains[0], gains[1]
    normed, norm_pullback = jax.vjp(norm_rows, x, gain_one)
    e["acts"] = normed.astype(bf16)
    e["out"] = slab_piece(e["out"])
    e["cot"] = lax.all_to_all(
        cotangent.reshape(micro, reps, strip, width), "rep", split_axis=1, concat_axis=1, tiled=True
    )
    del e["rows"]
    fence(e)
    e["acts"] = pieces_far(e["acts"])
    fence(e)
    out = Gather(padded(e.pop("out")), 0)
    tick([out])
    e["acts"] = rows_near(e["acts"])
    e["down"] = slab_piece(e["down"])
    fence(e)

    acts = e["acts"]
    weight_qkvg = assembled([(qkvg[0], 0, 0), (qkvg[1], 0, cut)], member_rows, qkvg_cols)
    tick([out])
    pre = dot(acts, weight_qkvg)
    gate_at = 2 * qk_cols + val_cols + -val_cols % 128
    value = pre[:, 2 * qk_cols : 2 * qk_cols + val_cols].astype(bf16)
    gate_pre = pre[:, gate_at : gate_at + val_cols]
    query, key = [], []
    for h in range(heads):
        query.append(turn(pre[:, h * KEY_DIM : (h + 1) * KEY_DIM], 1.0).astype(bf16))
        key.append(
            turn(pre[:, qk_cols + h * KEY_DIM : qk_cols + (h + 1) * KEY_DIM], 1.0).astype(bf16)
        )
    e = {"query": query, "cot": e["cot"], "down": e["down"], "pu": e["pu"]}
    fence(e, rings=[out])
    query = e["query"]
    tick([out])

    values, weights, mixed, tails = [], [], [], []
    for h in range(heads):
        values.append(value[:, h * VAL_DIM : (h + 1) * VAL_DIM])
        weights.append(decayed(dot_t(query[h], key[h]), h))
        retained = dot(weights[h], values[h])
        mix, pull = jax.vjp(mix_tail, retained, gate_pre[:, h * VAL_DIM : (h + 1) * VAL_DIM])
        mixed.append(mix.astype(bf16))
        tails.append(pull)
    mixed_b = padded(jnp.concatenate(mixed, axis=1))
    tick([out], free=True)
    e = {"mixed": mixed_b, "cot": e["cot"], "down": e["down"], "pu": e["pu"]}
    fence(e, rings=[out])
    pu = [Gather(e["pu"][0], 0), Gather(e["pu"][1], 1)]
    down = Gather(padded(e["down"]), 0)
    ff = pu + [down]
    tick(ff)
    mixed_b = e["mixed"]
    cot_seqs = jnp.einsum("msk,mkrd->msrd", selector, e["cot"], preferred_element_type=f32)
    cot_seqs = cot_seqs.astype(bf16).reshape(members, strip, width)
    weight_out = assembled([(out, 0, 0)], member_rows, out.part.shape[1])

    held = by_place(dot_t(mixed_b, weight_out))
    e = {"came": sum_send(held, 1), "cot": cot_seqs}
    fence(e, rings=ff)
    held = sum_take(held, e["came"], 1)
    tick(ff)
    e = {
        "sum": sum_far(held),
        "cot": lax.all_to_all(e["cot"], "grp", split_axis=0, concat_axis=0, tiled=True),
    }
    fence(e, rings=ff)

    hidden = x + e["sum"]
    out_grad = e["cot"].reshape(own_rows, width).astype(f32) * live
    normed_mid, mid_pullback = jax.vjp(norm_rows, hidden, gain_two)
    tick(ff)
    e = {"mid": pieces_far(normed_mid.astype(bf16)), "cot": out_grad.astype(bf16)}
    fence(e, rings=ff)
    tick(ff)
    e = {"mid": rows_near(e["mid"]), "cot": pieces_far(e["cot"])}
    fence(e, rings=ff)

    middle = e["mid"]
    hid = pu[0].part.shape[1]
    weight_pu = assembled([(pu[0], 0, 0), (pu[1], 0, hid)], member_rows, 2 * hid)
    pu_pre = dot(middle, weight_pu)
    proj_pre, up_pre = pu_pre[:, :hid], pu_pre[:, hid:]
    out_grad_full = rows_near(e["cot"])

    def glu_act(proj_pre, up_pre):
        return jax.nn.gelu(proj_pre, approximate=True) * up_pre

    glu_rows, glu_pullback = jax.vjp(glu_act, proj_pre, up_pre)
    glu_b = glu_rows.astype(bf16)
    ring_down = [Scatter(out_grad_full, glu_b, 0)]
    e = {"cot": out_grad_full, "glu": glu_b}
    fence(e, rings=ring_down)
    weight_down = assembled([(down, 0, 0)], member_rows, down.part.shape[1])
    tick(ring_down)
    proj_grad, up_grad = glu_pullback(dot(e["cot"], weight_down))
    pu_grad = jnp.concatenate([proj_grad, up_grad], axis=1).astype(bf16)
    held = by_place(dot_t(pu_grad, weight_pu))
    glu_b = e["glu"]
    e = {"came": sum_send(held, 1), "pu": pu_grad}
    fence(e)
    ring_ff = [Scatter(middle, e["pu"][:, :hid], 0), Scatter(middle, e["pu"][:, hid:], 1)]
    held = sum_take(held, e["came"], 1)
    tick(ring_ff)
    ring_ff = ring_ff + ring_down
    e = {"sum": sum_far(held), "glu": glu_b}
    fence(e)
    glu_b = e["glu"]

    hidden_grad = out_grad + mid_pullback(e["sum"])[0]
    tick(ring_ff)
    e = {"branch": pieces_far(hidden_grad.astype(bf16)), "glu": glu_b}
    fence(e, rings=ring_ff)
    tick(ring_ff)
    held = by_place(dot_t(e["glu"], weight_down))
    e = {"branch": rows_near(e["branch"]), "rows": sum_send(held, 1)}
    fence(e, rings=ring_ff)
    branch = e["branch"]

    mixed_grad = dot(branch, weight_out)
    retained_grads, gate_grads = [], []
    for h in range(heads):
        retained_grad, gate_grad = tails[h](mixed_grad[:, h * VAL_DIM : (h + 1) * VAL_DIM])
        retained_grads.append(retained_grad.astype(bf16))
        gate_grads.append(gate_grad.astype(bf16))
    gate_grad = padded(jnp.concatenate(gate_grads, axis=1))
    tick(ring_ff)
    held = sum_take(held, e["rows"], 1)
    ring_og = [Scatter(acts, gate_grad, 0), Scatter(branch, mixed_b, 1)]
    tick(ring_og)
    e = {"retained": retained_grads, "rows": sum_far(held)}
    fence(e, rings=ring_ff)
    retained_grads = e["retained"]
    out_rows = hidden + e["rows"]

    tick(ring_og)
    scores, value_grads = [], []
    for h in range(heads):
        scores.append(decayed(dot_t(retained_grads[h], values[h]), h))
        value_grads.append(t_dot(weights[h], retained_grads[h]).astype(bf16))
    value_grad = padded(jnp.concatenate(value_grads, axis=1))
    e = {
        "scores": scores,
        "ff": [ring.whole() for ring in ring_ff],
        "value": value_grad,
        "rows": out_rows.astype(bf16),
    }
    fence(e, rings=ring_og)
    scores, ff, value_grad = e["scores"], e["ff"], e["value"]
    ring_v = Scatter(acts, value_grad, 1)
    tick(ring_og)
    query_grads, key_grads = [], []
    for h in range(heads):
        query_grads.append(turn(dot(scores[h], key[h]), -1.0).astype(bf16))
        key_grads.append(turn(t_dot(scores[h], query[h]), -1.0).astype(bf16))
    qk_grad = jnp.concatenate(query_grads + key_grads, axis=1)
    e = {
        "grad": qk_grad,
        "pu": pieces_far(jnp.concatenate(ff[:2], axis=1)),
        "rows": lax.all_to_all(
            e["rows"].reshape(members, strip, width),
            "grp",
            split_axis=0,
            concat_axis=0,
            tiled=True,
        ),
        "down": ff[2],
    }
    fence(e, rings=ring_og)
    qk_grad, pu_far = e["grad"], e["pu"]
    out_seqs = e["rows"].reshape(micro, seqs, strip, width)
    out_bins = jnp.einsum("msk,msrd->mkrd", selector, out_seqs, preferred_element_type=f32)

    tick(ring_og + [ring_v])
    held = by_place(
        dot_t(jnp.concatenate([qk_grad, value_grad, gate_grad], axis=1), weight_qkvg)
    )
    ring_qk = Scatter(acts, qk_grad, 0)
    e = {
        "came": sum_send(held, 1),
        "pu": pieces_near(pu_far),
        "bins": lax.all_to_all(
            out_bins.astype(bf16), "rep", split_axis=1, concat_axis=1, tiled=True
        ),
        "down": e["down"],
    }
    fence(e, rings=ring_og)
    bin_out = e["bins"].reshape(micro, 1, block, width)
    held = sum_take(held, e["came"], 1)
    tick([ring_qk, ring_v])
    e = {
        "sum": sum_far(held),
        "gate": ring_og[0].whole(),
        "out": ring_og[1].whole(),
        "down": e["down"],
        "pu": e["pu"],
    }
    fence(e)
    input_grad = hidden_grad + norm_pullback(e["sum"])[0]
    tick([ring_qk, ring_v])
    e = {
        "rows": lax.all_to_all(
            input_grad.astype(bf16).reshape(members, strip, width),
            "grp",
            split_axis=0,
            concat_axis=0,
            tiled=True,
        ),
        "gate": pieces_far(e["gate"]),
        "down": slab_rows(e["down"][:, :hid_cols]),
        "out": e["out"],
        "pu": e["pu"],
    }
    fence(e, rings=[ring_qk, ring_v])
    token_grad = e["rows"].reshape(tokens.shape)

    tick([ring_qk, ring_v])
    proj_owned, up_owned, gain_two_owned = finished(
        e["pu"], ((0, hid_cols), (hid, hid_cols)), mlp_gain, (w_proj, w_up)
    )
    e = {
        "gate": pieces_near(e["gate"]),
        "slabs": pieces_far(
            jnp.concatenate([e["down"], slab_rows(e["out"][:, :val_cols])], axis=1)
        ),
        "gain": gain_two_owned,
    }
    fence(e, rings=[ring_qk, ring_v])
    gain_two_owned = e["gain"]
    tick([ring_qk])
    gate_owned, gate_sum = finished(e["gate"], ((0, val_cols),), norm_gain, (w_gate,))
    e = {
        "slabs": pieces_near(e["slabs"]),
        "gain": gate_sum,
        "last": pieces_far(jnp.concatenate([ring_qk.whole(), ring_v.whole()], axis=1)),
    }
    fence(e)
    size = width // reps
    down_owned, out_owned = finished(e["slabs"], ((0, size), (size, size)))
    query_owned, key_owned, value_owned, rest_sum = finished(
        pieces_near(e["last"]),
        ((0, qk_cols), (qk_cols, qk_cols), (2 * qk_cols, val_cols)),
        norm_gain,
        (w_query, w_key, w_value),
    )
    gain_one_owned = (e["gain"] + rest_sum)[:, 0]
    gain_two_owned = gain_two_owned[:, 0]
    return (
        bin_out,
        token_grad,
        gain_one_owned,
        query_owned,
        key_owned,
        value_owned,
        gate_owned,
        out_owned,
        gain_two_owned,
        proj_owned,
        up_owned,
        down_owned,
    )


def solution(mesh):
    return jax.shard_map(
        body,
        mesh=mesh,
        in_specs=(
            P(None, None, "grp", "rep", None),
            P(None, "rep", "grp", None),
            P(),
            P(),
            P("grp"),
            P("grp", None),
            P("grp", None),
            P("grp", None),
            P("grp", None),
            P("grp", None),
            P("grp"),
            P("grp", None),
            P("grp", None),
            P("grp", None),
        ),
        out_specs=(
            P(None, "rep", "grp", None),
            P(None, None, "grp", "rep", None),
            P("grp"),
            P("grp", None),
            P("grp", None),
            P("grp", None),
            P("grp", None),
            P("grp", None),
            P("grp"),
            P("grp", None),
            P("grp", None),
            P("grp", None),
        ),
        check_vma=False,
    )
```

time: 1250 us -> 1010 us (0.81)
  waiting for transfers between devices: 620 us -> 309 us
  starting transfers between devices: 185 us -> 282 us
  blocking collectives: 42.6 us -> 0 us
  Pallas kernels: 0 us -> 38.9 us
  other arithmetic: 95.1 us -> 128 us
  matrix products: 179 us -> 148 us
  between operations: 16.4 us -> 3.49 us
    ppermute x4 -> x99, waiting for transfers between devices: 0.01 us -> 267 us  [the longest x91 245 us: ring_step(): lax.ppermute(value, 'grp', [(ring[i], ring[(i + ahead) % count]) for i in...]
    reduce_scatter x5 -> x0, waiting for transfers between devices: 206 us -> none  [scatter_members(): return lax.psum_scatter(full, 'grp', scatter_dimension=0, tiled=True)]
    all_gather x5 -> x0, waiting for transfers between devices: 205 us -> none  [gather_members(): return lax.all_gather(part, 'grp', axis=0, tiled=True)]
    ppermute x4 -> x99, starting transfers between devices: 8.19 us -> 184 us  [the longest x91 169 us: ring_step(): lax.ppermute(value, 'grp', [(ring[i], ring[(i + ahead) % count]) for i in...]
    ppermute x44 -> x32, waiting for transfers between devices: 152 us -> 36.9 us  [swap(): return lax.ppermute(value, 'rep', [(i, i ^ bit) for i in range(count)])]
    all_to_all x1, starting transfers between devices: 56.8 us -> 4.24 us  [body(): lax.all_to_all(tokens.reshape(members, strip, width), 'grp', split_axis=0...]
    all_gather x1 -> x0, blocking collectives: 42.6 us -> none  [body(): lax.all_gather(jnp.stack([norm_gain, mlp_gain]), 'grp', axis=1, tiled=True)]
    pallas_call x0 -> x8, Pallas kernels: none -> 38.9 us  [the longest x4 20.1 us: assembled(): pl.pallas_call(functools.partial(assemble_kernel, spots), out_shape=jax.S...]
  transfers between devices with their start and end apart: 64 -> 138, of which waited for: 24 -> 50; matrix products, arithmetic and copies ran while one was open for 26% -> 25% of each run, Pallas kernels for 0% -> 3%
where the time goes in v2:
time: 1010 us; the launch traced here: 1000 us
  waiting for transfers between devices  309 us (31%)
  starting transfers between devices  282 us (28%)
  matrix products  148 us (15%)
  other arithmetic  128 us (13%)
  local copies, waits for them, and re-layouts  95.4 us (9%)
  Pallas kernels  38.9 us (4%)
    ppermute x91, waiting for transfers between devices, ring_step(): lax.ppermute(value, 'grp', [(ring[i], ring[(i + ahead) % count]) for i in...  245 us
    ppermute x91, starting transfers between devices, ring_step(): lax.ppermute(value, 'grp', [(ring[i], ring[(i + ahead) % count]) for i in...  169 us
    ppermute x32, starting transfers between devices, swap(): return lax.ppermute(value, 'rep', [(i, i ^ bit) for i in range(count)])  65.5 us
    dot_general x8, matrix products, dot_t(): lax.dot_general(left, right, (((1,), (1,)), ((), ())), preferred_element_...  52.1 us
    dot_general x11, matrix products, t_dot(): lax.dot_general(left, right, (((0,), (0,)), ((), ())), preferred_element_...  46.6 us
    dot_general x8, matrix products, dot(): return jnp.dot(left, right, preferred_element_type=f32)  44.5 us
    unnamed x338, local copies, waits for them, and re-layouts  37.3 us
    ppermute x32, waiting for transfers between devices, swap(): return lax.ppermute(value, 'rep', [(i, i ^ bit) for i in range(count)])  36.9 us
  transfers between devices with their start and end apart: 138, of which 50 were waited for; matrix products, arithmetic and copies ran while one was open for 25% of the time, Pallas kernels for 3%

profile of v2, /device:TPU:0, one launch (start us, length us, event | category | flops | bytes accessed | tf_op | source)
XLA Modules:
  0.0 1004.7 jit_solution(110491825537158994)
XLA Ops:
  35.4 21.2 %collective-permute-done.7.refs_1_ = bf16[256,1408]{1,0:T(8,128)(2,1)S(1)} collective-permute-done((bf16[256,1408]{1,0:T(8,128)(2,1)S(1)}, bf16[256,1408]{1,0:T(8,128)(2,1)S(1)}, u32[]{:S(2)}, u32[]{:S(2)}) %collective-permute-start.7) | collective-permute-done | bytes 720928 | tf_op jit(solution)/shard_map/ppermute | solution.py:129
  63.7 8.5 collective-permute-done.14.refs_9_
  86.0 9.1 collective-permute-done
  95.0 9.0 collective-permute-start.19
  104.9 23.6 %collective-permute-start.2 = (bf16[256,2048]{1,0:T(8,128)(2,1)}, bf16[256,2048]{1,0:T(8,128)(2,1)}, u32[]{:S(2)}, u32[]{:S(2)}) collective-permute-start(bf16[256,2048]{1,0:T(8,128)(2,1)} %fusion.41), channel_id=1, source_target_pairs={{0,16},{8,24},{16,0},{24,8},{1,17},{9,25},{17,1},{25,9},{2,18},{10... | collective-permute-start | bytes 3145736 | tf_op jit(solution)/shard_map/ppermute | solution.py:40
  130.6 10.0 collective-permute-start.20
  147.9 8.2 collective-permute-start.13
  176.5 11.8 %collective-permute-start.21 = (bf16[256,896]{0,1:T(8,128)(2,1)S(1)}, bf16[256,896]{0,1:T(8,128)(2,1)}, u32[]{:S(2)}, u32[]{:S(2)}) collective-permute-start(bf16[256,896]{0,1:T(8,128)(2,1)S(1)} %pad.33), channel_id=1, source_target_pairs={{0,2},{2,4},{4,6},{6,7},{7,5},{5,3},{3,1},{1,0},{8,10},{10,12},{12... | collective-permute-start | bytes 1376264 | tf_op jit(solution)/shard_map/ppermute | solution.py:129
  212.0 17.9 %fusion.98 = (bf16[1024,2816]{1,0:T(8,128)(2,1)S(1)}, f32[1024,2816]{1,0:T(8,128)S(1)}) fusion(bf16[1024,2048]{1,0:T(8,128)(2,1)S(1)} %pad_maximum_fusion, bf16[2048,2816]{1,0:T(8,128)(2,1)} %copy-done), kind=kOutput, calls=%fused_computation.298 | convolution fusion | flops 11814043648 | bytes 33030144 | tf_op jit(solution)/shard_map/dot_general | solution.py:27
  304.2 20.4 %collective-permute-done.30.refs_7_ = bf16[256,896]{1,0:T(8,128)(2,1)S(1)} collective-permute-done((bf16[256,896]{1,0:T(8,128)(2,1)S(1)}, bf16[256,896]{1,0:T(8,128)(2,1)S(1)}, u32[]{:S(2)}, u32[]{:S(2)}) %collective-permute-start.30) | collective-permute-done | bytes 458784 | tf_op jit(solution)/shard_map/ppermute | solution.py:129
  361.1 8.9 collective-permute-done.37.refs_6_
  399.6 9.9 collective-permute-done.48
  460.6 7.7 fusion.103
  480.6 10.1 %fusion.100 = (bf16[1024,2048]{1,0:T(8,128)(2,1)S(1)}, f32[1024,2048]{1,0:T(8,128)}) fusion(bf16[2048,1792]{1,0:T(8,128)(2,1)S(1)} %shard_map.231, bf16[1024,896]{1,0:T(8,128)(2,1)S(1)} %get-tuple-element.481, bf16[1024,896]{1,0:T(8,128)(2,1)S(1)} %get-tuple-element.480), kind=kOutput, calls=%fused_computation.300 | convolution fusion | flops 7525629952 | bytes 23592960 | tf_op jit(solution)/shard_map/dot_general | solution.py:31
  516.6 12.5 %collective-permute-done.59 = bf16[256,2048]{1,0:T(8,128)(2,1)S(1)} collective-permute-done((bf16[256,2048]{1,0:T(8,128)(2,1)S(1)}, bf16[256,2048]{1,0:T(8,128)(2,1)S(1)}, u32[]{:S(2)}, u32[]{:S(2)}) %collective-permute-start.59) | collective-permute-done | bytes 1048608 | tf_op jit(solution)/shard_map/ppermute | solution.py:40
  540.3 10.4 %collective-permute-done.63 = bf16[256,896]{1,0:T(8,128)(2,1)S(1)} collective-permute-done((bf16[256,896]{1,0:T(8,128)(2,1)S(1)}, bf16[256,896]{1,0:T(8,128)(2,1)S(1)}, u32[]{:S(2)}, u32[]{:S(2)}) %collective-permute-start.63) | collective-permute-done | bytes 458784 | tf_op jit(solution)/shard_map/ppermute | solution.py:129
  582.7 9.0 collective-permute-done.75
  731.8 19.5 %fusion.102 = (bf16[1024,2048]{1,0:T(8,128)(2,1)}, f32[1024,2048]{1,0:T(8,128)}) fusion(bf16[2048,2816]{1,0:T(8,128)(2,1)} %copy-done, bf16[1024,896]{1,0:T(8,128)(2,1)} %copy-done.80, bf16[1024,896]{1,0:T(8,128)(2,1)} %copy.260, bf16[1024,1024]{1,0:T(8,128)(2,1)} %fusion.69), kind=kOutput, calls=%fused_computation.302 | convolution fusion | flops 11830558720 | bytes 29884416 | tf_op jit(solution)/shard_map/dot_general | solution.py:31
  800.4 8.6 collective-permute-done.101
  842.3 12.6 %collective-permute-done.104 = bf16[256,432]{0,1:T(8,128)(2,1)S(1)} collective-permute-done((bf16[256,432]{0,1:T(8,128)(2,1)S(1)}, bf16[256,432]{0,1:T(8,128)(2,1)S(1)}, u32[]{:S(2)}, u32[]{:S(2)}) %collective-permute-start.104) | collective-permute-done | bytes 221216 | tf_op jit(solution)/shard_map/ppermute | solution.py:369
  854.9 23.0 %collective-permute-start.106 = (bf16[256,896]{1,0:T(8,128)(2,1)S(1)}, bf16[256,896]{1,0:T(8,128)(2,1)S(1)}, u32[]{:S(2)}, u32[]{:S(2)}) collective-permute-start(bf16[256,896]{1,0:T(8,128)(2,1)S(1)} %add_convert_fusion.16.refs_0_), channel_id=1, source_target_pairs={{0,16},{8,24},{16,0},{24,8},{1,17},{9,25},{17,1},{25,9},{2,18},{10... | collective-permute-start | bytes 1376264 | tf_op jit(solution)/shard_map/ppermute | solution.py:40
  891.4 9.9 collective-permute-start.118
  950.3 8.9 collective-permute-done.123
  964.8 17.5 %collective-permute-done.126.refs_2_ = bf16[256,1920]{1,0:T(8,128)(2,1)} collective-permute-done((bf16[256,1920]{1,0:T(8,128)(2,1)S(1)}, bf16[256,1920]{1,0:T(8,128)(2,1)}, u32[]{:S(2)}, u32[]{:S(2)}) %collective-permute-start.126) | collective-permute-done | bytes 983072 | tf_op jit(solution)/shard_map/ppermute | solution.py:40
  (800 shorter events, 692.7 us)
Async XLA Ops:
  16.4 55.8 %all-to-all-start.1 = ((bf16[8,32,2048]{2,1,0:T(8,128)(2,1)}), bf16[8,32,2048]{2,1,0:T(8,128)(2,1)}, u32[]{:S(2)}, u32[]{:S(2)}) async-start(bf16[8,32,2048]{2,1,0:T(8,128)(2,1)} %bitcast.6), calls=%async_computation.1 | async-start | bytes 2097152 | tf_op jit(solution)/shard_map/all_to_all | solution.py:457
  22.8 49.4 %collective-permute-start.14 = (bf16[256,1408]{1,0:T(8,128)(2,1)S(1)}, bf16[256,1408]{1,0:T(8,128)(2,1)}, u32[]{:S(2)}, u32[]{:S(2)}) collective-permute-start(bf16[256,1408]{1,0:T(8,128)(2,1)S(1)} %get-tuple-element.536.refs_8_), channel_id=1, source_target_pairs={{0,1},{2,0},{4,2},{6,4},{7,6},{5,7},{3,5},{1,3},{8,9},{10,8},{12,1... | collective-permute-start | bytes 2162696 | tf_op jit(solution)/shard_map/ppermute | solution.py:129
  24.7 58.0 %collective-permute-start.18 = (bf16[256,1408]{1,0:T(8,128)(2,1)S(1)}, bf16[256,1408]{1,0:T(8,128)(2,1)}, u32[]{:S(2)}, u32[]{:S(2)}) collective-permute-start(bf16[256,1408]{1,0:T(8,128)(2,1)S(1)} %get-tuple-element.536.refs_8_), channel_id=1, source_target_pairs={{0,2},{2,4},{4,6},{6,7},{7,5},{5,3},{3,1},{1,0},{8,10},{10,12},{12... | collective-permute-start | bytes 2162696 | tf_op jit(solution)/shard_map/ppermute | solution.py:129
  56.6 73.9 %collective-permute-start.8 = (bf16[256,1408]{1,0:T(8,128)(2,1)S(1)}, bf16[256,1408]{1,0:T(8,128)(2,1)}, u32[]{:S(2)}, u32[]{:S(2)}) collective-permute-start(bf16[256,1408]{1,0:T(8,128)(2,1)S(1)} %collective-permute-done.7.refs_1_), channel_id=1, source_target_pairs={{0,1},{2,0},{4,2},{6,4},{7,6},{5,7},{3,5},{1,3},{8,9},{10,8},{12,1... | collective-permute-start | bytes 2162696 | tf_op jit(solution)/shard_map/ppermute | solution.py:129
  56.7 71.9 %collective-permute-start.11 = (bf16[256,1408]{1,0:T(8,128)(2,1)}, bf16[256,1408]{1,0:T(8,128)(2,1)}, u32[]{:S(2)}, u32[]{:S(2)}) collective-permute-start(bf16[256,1408]{1,0:T(8,128)(2,1)} %collective-permute-done.10.refs_7_), channel_id=1, source_target_pairs={{0,2},{2,4},{4,6},{6,7},{7,5},{5,3},{3,1},{1,0},{8,10},{10,12},{12... | collective-permute-start | bytes 2162696 | tf_op jit(solution)/shard_map/ppermute | solution.py:129
  72.2 56.3 %collective-permute-start.15 = (bf16[256,1408]{1,0:T(8,128)(2,1)}, bf16[256,1408]{1,0:T(8,128)(2,1)}, u32[]{:S(2)}, u32[]{:S(2)}) collective-permute-start(bf16[256,1408]{1,0:T(8,128)(2,1)} %collective-permute-done.14.refs_9_), channel_id=1, source_target_pairs={{0,1},{2,0},{4,2},{6,4},{7,6},{5,7},{3,5},{1,3},{8,9},{10,8},{12,1... | collective-permute-start | bytes 2162696 | tf_op jit(solution)/shard_map/ppermute | solution.py:129
  104.9 51.2 %collective-permute-start.2 = (bf16[256,2048]{1,0:T(8,128)(2,1)}, bf16[256,2048]{1,0:T(8,128)(2,1)}, u32[]{:S(2)}, u32[]{:S(2)}) collective-permute-start(bf16[256,2048]{1,0:T(8,128)(2,1)} %fusion.41), channel_id=1, source_target_pairs={{0,16},{8,24},{16,0},{24,8},{1,17},{9,25},{17,1},{25,9},{2,18},{10... | collective-permute-start | bytes 3145736 | tf_op jit(solution)/shard_map/ppermute | solution.py:40
  156.1 53.4 %collective-permute-start.4 = (bf16[256,2048]{1,0:T(8,128)(2,1)}, bf16[256,2048]{1,0:T(8,128)(2,1)}, u32[]{:S(2)}, u32[]{:S(2)}) collective-permute-start(bf16[256,2048]{1,0:T(8,128)(2,1)} %collective-permute-done.2), channel_id=1, source_target_pairs={{0,8},{8,0},{16,24},{24,16},{1,9},{9,1},{17,25},{25,17},{2,10},{10... | collective-permute-start | bytes 3145736 | tf_op jit(solution)/shard_map/ppermute | solution.py:40
  159.0 50.5 %collective-permute-start.3 = (bf16[256,2048]{1,0:T(8,128)(2,1)}, bf16[256,2048]{1,0:T(8,128)(2,1)}, u32[]{:S(2)}, u32[]{:S(2)}) collective-permute-start(bf16[256,2048]{1,0:T(8,128)(2,1)} %fusion.41), channel_id=1, source_target_pairs={{0,8},{8,0},{16,24},{24,16},{1,9},{9,1},{17,25},{25,17},{2,10},{10... | collective-permute-start | bytes 3145736 | tf_op jit(solution)/shard_map/ppermute | solution.py:40
  291.6 53.5 %all-to-all-start.3 = ((bf16[8,32,2048]{2,1,0:T(8,128)(2,1)}), bf16[8,32,2048]{2,1,0:T(8,128)(2,1)}, u32[]{:S(2)}, u32[]{:S(2)}) async-start(bf16[8,32,2048]{2,1,0:T(8,128)(2,1)} %bitcast.24), calls=%async_computation.3 | async-start | bytes 2097152 | tf_op jit(solution)/shard_map/all_to_all | solution.py:551
  350.2 42.0 %collective-permute-start.36 = (bf16[256,2048]{1,0:T(8,128)(2,1)}, bf16[256,2048]{1,0:T(8,128)(2,1)}, u32[]{:S(2)}, u32[]{:S(2)}) collective-permute-start(bf16[256,2048]{1,0:T(8,128)(2,1)} %multiply_convert_fusion.6), channel_id=1, source_target_pairs={{0,16},{8,24},{16,0},{24,8},{1,17},{9,25},{17,1},{25,9},{2,18},{10... | collective-permute-start | bytes 3145736 | tf_op jit(solution)/shard_map/ppermute | solution.py:40
  399.6 57.6 %collective-permute-start.45 = (bf16[256,2048]{1,0:T(8,128)(2,1)}, bf16[256,2048]{1,0:T(8,128)(2,1)}, u32[]{:S(2)}, u32[]{:S(2)}) collective-permute-start(bf16[256,2048]{1,0:T(8,128)(2,1)} %collective-permute-done.36), channel_id=1, source_target_pairs={{0,8},{8,0},{16,24},{24,16},{1,9},{9,1},{17,25},{25,17},{2,10},{10... | collective-permute-start | bytes 3145736 | tf_op jit(solution)/shard_map/ppermute | solution.py:40
  409.5 47.7 %collective-permute-start.44 = (bf16[256,2048]{1,0:T(8,128)(2,1)}, bf16[256,2048]{1,0:T(8,128)(2,1)}, u32[]{:S(2)}, u32[]{:S(2)}) collective-permute-start(bf16[256,2048]{1,0:T(8,128)(2,1)} %multiply_convert_fusion.6), channel_id=1, source_target_pairs={{0,8},{8,0},{16,24},{24,16},{1,9},{9,1},{17,25},{25,17},{2,10},{10... | collective-permute-start | bytes 3145736 | tf_op jit(solution)/shard_map/ppermute | solution.py:40
  498.3 41.3 %collective-permute-start.65 = (bf16[256,896]{0,1:T(8,128)(2,1)S(1)}, bf16[256,896]{0,1:T(8,128)(2,1)S(1)}, u32[]{:S(2)}, u32[]{:S(2)}) collective-permute-start(bf16[256,896]{0,1:T(8,128)(2,1)S(1)} %get-tuple-element.299), channel_id=1, source_target_pairs={{0,2},{2,4},{4,6},{6,7},{7,5},{5,3},{3,1},{1,0},{8,10},{10,12},{12... | collective-permute-start | bytes 1376264 | tf_op jit(solution)/shard_map/ppermute | solution.py:129
  510.0 43.8 %collective-permute-start.62 = (bf16[256,896]{1,0:T(8,128)(2,1)S(1)}, bf16[256,896]{1,0:T(8,128)(2,1)S(1)}, u32[]{:S(2)}, u32[]{:S(2)}) collective-permute-start(bf16[256,896]{1,0:T(8,128)(2,1)S(1)} %get-tuple-element.296), channel_id=1, source_target_pairs={{0,1},{2,0},{4,2},{6,4},{7,6},{5,7},{3,5},{1,3},{8,9},{10,8},{12,1... | collective-permute-start | bytes 1376264 | tf_op jit(solution)/shard_map/ppermute | solution.py:129
  602.6 50.5 %collective-permute-start.78 = (bf16[256,896]{1,0:T(8,128)(2,1)}, bf16[256,896]{1,0:T(8,128)(2,1)}, u32[]{:S(2)}, u32[]{:S(2)}) collective-permute-start(bf16[256,896]{1,0:T(8,128)(2,1)} %get-tuple-element.313), channel_id=1, source_target_pairs={{0,2},{2,4},{4,6},{6,7},{7,5},{5,3},{3,1},{1,0},{8,10},{10,12},{12... | collective-permute-start | bytes 1376264 | tf_op jit(solution)/shard_map/ppermute | solution.py:129
  609.1 54.4 %collective-permute-start.83 = (bf16[256,896]{0,1:T(8,128)(2,1)}, bf16[256,896]{0,1:T(8,128)(2,1)}, u32[]{:S(2)}, u32[]{:S(2)}) collective-permute-start(bf16[256,896]{0,1:T(8,128)(2,1)} %get-tuple-element.318), channel_id=1, source_target_pairs={{0,1},{2,0},{4,2},{6,4},{7,6},{5,7},{3,5},{1,3},{8,9},{10,8},{12,1... | collective-permute-start | bytes 1376264 | tf_op jit(solution)/shard_map/ppermute | solution.py:129
  688.2 43.6 %collective-permute-start.89 = (bf16[256,1792]{1,0:T(8,128)(2,1)S(1)}, bf16[256,1792]{1,0:T(8,128)(2,1)S(1)}, u32[]{:S(2)}, u32[]{:S(2)}) collective-permute-start(bf16[256,1792]{1,0:T(8,128)(2,1)S(1)} %constant_dynamic-update-slice_fusion.5.refs_0_), channel_id=1, source_target_pairs={{0,16},{8,24},{16,0},{24,8},{1,17},{9,25},{17,1},{25,9},{2,18},{10... | collective-permute-start | bytes 2752520 | tf_op jit(solution)/shard_map/ppermute | solution.py:40
  688.7 43.1 %all-to-all-start.4 = ((bf16[8,32,2048]{2,1,0:T(8,128)(2,1)}), bf16[8,32,2048]{2,1,0:T(8,128)(2,1)}, u32[]{:S(2)}, u32[]{:S(2)}) async-start(bf16[8,32,2048]{2,1,0:T(8,128)(2,1)} %bitcast.126), calls=%async_computation.4 | async-start | bytes 2097152 | tf_op jit(solution)/shard_map/all_to_all | solution.py:646
  819.3 68.6 %all-to-all-start.6 = ((bf16[8,32,2048]{2,1,0:T(8,128)(2,1)}), bf16[8,32,2048]{2,1,0:T(8,128)(2,1)}, u32[]{:S(2)}, u32[]{:S(2)}) async-start(bf16[8,32,2048]{2,1,0:T(8,128)(2,1)} %bitcast.34), calls=%async_computation.6 | async-start | bytes 2097152 | tf_op jit(solution)/shard_map/all_to_all | solution.py:688
  831.1 47.6 %collective-permute-start.107 = (bf16[256,1024]{1,0:T(8,128)(2,1)S(1)}, bf16[256,1024]{1,0:T(8,128)(2,1)S(1)}, u32[]{:S(2)}, u32[]{:S(2)}) collective-permute-start(bf16[256,1024]{1,0:T(8,128)(2,1)S(1)} %get-tuple-element.364), channel_id=1, source_target_pairs={{0,2},{2,4},{4,6},{6,7},{7,5},{5,3},{3,1},{1,0},{8,10},{10,12},{12... | collective-permute-start | bytes 1572872 | tf_op jit(solution)/shard_map/ppermute | solution.py:129
  833.0 45.7 %collective-permute-start.108 = (bf16[256,1024]{1,0:T(8,128)(2,1)S(1)}, bf16[256,1024]{1,0:T(8,128)(2,1)S(1)}, u32[]{:S(2)}, u32[]{:S(2)}) collective-permute-start(bf16[256,1024]{1,0:T(8,128)(2,1)S(1)} %get-tuple-element.365), channel_id=1, source_target_pairs={{0,1},{2,0},{4,2},{6,4},{7,6},{5,7},{3,5},{1,3},{8,9},{10,8},{12,1... | collective-permute-start | bytes 1572872 | tf_op jit(solution)/shard_map/ppermute | solution.py:129
  835.2 42.7 %collective-permute-start.105 = (bf16[256,432]{0,1:T(8,128)(2,1)S(1)}, bf16[256,432]{0,1:T(8,128)(2,1)S(1)}, u32[]{:S(2)}, u32[]{:S(2)}) collective-permute-start(bf16[256,432]{0,1:T(8,128)(2,1)S(1)} %get-tuple-element.545), channel_id=1, source_target_pairs={{0,0},{1,1},{8,2},{9,3},{16,4},{17,5},{24,6},{25,7},{2,8},{3,9},{1... | collective-permute-start | bytes 663560 | tf_op jit(solution)/shard_map/ppermute | solution.py:369
  838.4 41.1 %collective-permute-start.110 = (bf16[256,896]{1,0:T(8,128)(2,1)S(1)}, bf16[256,896]{1,0:T(8,128)(2,1)S(1)}, u32[]{:S(2)}, u32[]{:S(2)}) collective-permute-start(bf16[256,896]{1,0:T(8,128)(2,1)S(1)} %get-tuple-element.367), channel_id=1, source_target_pairs={{0,2},{2,4},{4,6},{6,7},{7,5},{5,3},{3,1},{1,0},{8,10},{10,12},{12... | collective-permute-start | bytes 1376264 | tf_op jit(solution)/shard_map/ppermute | solution.py:129
  (280 other events, 4238.4 us)

commit v3 on v2

--- a/solution.py
+++ b/solution.py
@@ -48,9 +48,10 @@
 latest = {}
 
 
-def fence(*states, rings=()):
+def fence(*states, rings=(), done=()):
     leaves, tree = jax.tree.flatten(states)
-    marks = [mark for ring in rings for mark in ring.marks()]
+    marks = [mark for ring in rings for mark in ring.marks(2)]
+    marks += [mark for ring in done for mark in ring.marks(1)]
     fenced = lax.optimization_barrier((leaves, marks))[0]
     latest["mark"] = min(fenced, key=lambda leaf: leaf.size)
     for state, new in zip(states, jax.tree.unflatten(tree, fenced)):
@@ -155,8 +156,8 @@
         while max(self.left) > 0:
             self.tick(free=True)
 
-    def marks(self):
-        return [came[-2] for came in self.came if len(came) > 1]
+    def marks(self, back):
+        return [came[-back] for came in self.came if len(came) >= back]
 
     def tick(self, free=False):
         for way, ahead in enumerate((1, -1)):
@@ -210,28 +211,17 @@
 
 
 def assemble_kernel(spots, order_ref, *refs):
-    count = len(spots)
-    pieces, full_ref, held, in_sems, out_sems = (
-        refs[:count],
-        refs[count],
-        refs[count + 1 : 2 * count + 1],
-        refs[2 * count + 1],
-        refs[2 * count + 2],
-    )
-    comes, goes = [], []
+    pieces, full_ref, sems = refs[:-2], refs[-2], refs[-1]
+    copies = []
     for i, (place, member_rows, row, column) in enumerate(spots):
         rows, columns = pieces[i].shape
         start = pl.multiple_of(order_ref[place] * member_rows + row, rows)
         spot = full_ref.at[pl.ds(start, rows), pl.ds(column, columns)]
-        comes.append(pltpu.make_async_copy(pieces[i], held[i], in_sems.at[i]))
-        goes.append(pltpu.make_async_copy(held[i], spot, out_sems.at[i]))
-    for come in comes:
-        come.start()
-    for come, go in zip(comes, goes):
-        come.wait()
-        go.start()
-    for go in goes:
-        go.wait()
+        copies.append(pltpu.make_async_copy(pieces[i], spot, sems.at[i]))
+    for copy in copies:
+        copy.start()
+    for copy in copies:
+        copy.wait()
 
 
 def assembled(streams, member_rows, columns):
@@ -248,10 +238,9 @@
         functools.partial(assemble_kernel, spots),
         out_shape=jax.ShapeDtypeStruct((members * member_rows, columns), dtype),
         in_specs=[pl.BlockSpec(memory_space=pltpu.SMEM)]
-        + [pl.BlockSpec(memory_space=pl.ANY)] * len(pieces),
+        + [pl.BlockSpec(memory_space=pltpu.VMEM)] * len(pieces),
         out_specs=pl.BlockSpec(memory_space=pl.ANY),
-        scratch_shapes=[pltpu.VMEM(piece.shape, dtype) for piece in pieces]
-        + [pltpu.SemaphoreType.DMA((len(pieces),))] * 2,
+        scratch_shapes=[pltpu.SemaphoreType.DMA((len(pieces),))],
         compiler_params=pltpu.CompilerParams(vmem_limit_bytes=size + (2 << 20)),
         cost_estimate=pl.CostEstimate(flops=0, bytes_accessed=2 * size, transcendentals=0),
     )(order, *pieces)
@@ -313,6 +302,153 @@
         compiler_params=pltpu.CompilerParams(vmem_limit_bytes=40 << 20),
         cost_estimate=pl.CostEstimate(flops=4 * size, bytes_accessed=8 * size, transcendentals=0),
     )(*operands)
+
+
+def mixed_kernel(heads, q_ref, k_ref, v_ref, gate_ref, grow_ref, shrink_ref, row_ref, column_ref,
+                 mixed_ref, weights_ref):
+    seen = row_ref[...] >= column_ref[...]
+    if mixed_ref.shape[1] > heads * VAL_DIM:
+        mixed_ref[...] = jnp.zeros_like(mixed_ref)
+    for h in range(heads):
+        keys, cols = slice(h * KEY_DIM, (h + 1) * KEY_DIM), slice(h * VAL_DIM, (h + 1) * VAL_DIM)
+        decay = jnp.where(seen, grow_ref[:, h : h + 1] * shrink_ref[h : h + 1, :], 0.0)
+        weights = (dot_t(q_ref[:, keys], k_ref[:, keys]) * decay).astype(bf16)
+        weights_ref[h] = weights
+        retained = dot(weights, v_ref[:, cols])
+        scale = lax.rsqrt(jnp.mean(retained * retained, axis=-1, keepdims=True) + GROUP_EPS)
+        gate = gate_ref[:, cols]
+        mixed_ref[:, cols] = (gate * jax.nn.sigmoid(gate) * (retained * scale)).astype(bf16)
+
+
+def mixed_grad_kernel(heads, q_ref, k_ref, v_ref, gate_ref, grow_ref, shrink_ref, row_ref,
+                      column_ref, weights_ref, grad_ref, cos_ref, sin_ref, all_cos_ref, all_sin_ref,
+                      dq_ref, dgate_ref, dk_ref, dv_ref, dk_sum, dv_sum):
+    seen = row_ref[...] >= column_ref[...]
+    half = KEY_DIM // 2
+
+    def turned_back(grad, cosine, sine):
+        front, back = grad[:, :half], grad[:, half:]
+        return front * cosine + back * sine, back * cosine - front * sine
+
+    @pl.when(pl.program_id(0) == 0)
+    def _():
+        dk_sum[...] = jnp.zeros_like(dk_sum)
+        dv_sum[...] = jnp.zeros_like(dv_sum)
+
+    if dgate_ref.shape[1] > heads * VAL_DIM:
+        dgate_ref[...] = jnp.zeros_like(dgate_ref)
+    for h in range(heads):
+        keys, cols = slice(h * KEY_DIM, (h + 1) * KEY_DIM), slice(h * VAL_DIM, (h + 1) * VAL_DIM)
+        weights, value = weights_ref[h], v_ref[:, cols]
+        retained = dot(weights, value)
+        scale = lax.rsqrt(jnp.mean(retained * retained, axis=-1, keepdims=True) + GROUP_EPS)
+        normed = retained * scale
+        gate, grad = gate_ref[:, cols], grad_ref[:, cols]
+        sig = jax.nn.sigmoid(gate)
+        dgate_ref[:, cols] = (grad * normed * (sig * (1.0 + gate * (1.0 - sig)))).astype(bf16)
+        dnormed = grad * (gate * sig)
+        slope = jnp.mean(dnormed * normed, axis=-1, keepdims=True)
+        dretained = (scale * (dnormed - normed * slope)).astype(bf16)
+        decay = jnp.where(seen, grow_ref[:, h : h + 1] * shrink_ref[h : h + 1, :], 0.0)
+        dscores = (dot_t(dretained, value) * decay).astype(bf16)
+        front, back = turned_back(dot(dscores, k_ref[:, keys]), cos_ref[...], sin_ref[...])
+        dq_ref[:, h * KEY_DIM : h * KEY_DIM + half] = front.astype(bf16)
+        dq_ref[:, h * KEY_DIM + half : (h + 1) * KEY_DIM] = back.astype(bf16)
+        dk_sum[h] += t_dot(dscores, q_ref[:, keys])
+        dv_sum[h] += t_dot(weights, dretained)
+
+    @pl.when(pl.program_id(0) == pl.num_programs(0) - 1)
+    def _():
+        if dv_ref.shape[1] > heads * VAL_DIM:
+            dv_ref[...] = jnp.zeros_like(dv_ref)
+        for h in range(heads):
+            front, back = turned_back(dk_sum[h], all_cos_ref[...], all_sin_ref[...])
+            dk_ref[:, h * KEY_DIM : h * KEY_DIM + half] = front.astype(bf16)
+            dk_ref[:, h * KEY_DIM + half : (h + 1) * KEY_DIM] = back.astype(bf16)
+            dv_ref[:, h * VAL_DIM : (h + 1) * VAL_DIM] = dv_sum[h].astype(bf16)
+
+
+def retention_specs(heads, step, rows, value_cols):
+    def block(width, at=0):
+        return pl.BlockSpec((step, width), lambda i: (i, at))
+
+    def whole(height, width):
+        return pl.BlockSpec((height, width), lambda i: (0, 0))
+
+    return [
+        block(heads * KEY_DIM),
+        whole(rows, heads * KEY_DIM),
+        whole(rows, value_cols),
+        block(value_cols, 1),
+        block(heads),
+        whole(heads, rows),
+        block(1),
+        whole(1, rows),
+    ], block, whole
+
+
+def mixed_rows(query, key, value, value_gate, tables):
+    rows, value_cols = value.shape
+    heads = query.shape[1] // KEY_DIM
+    step = min(rows, 256)
+    specs, block, _ = retention_specs(heads, step, rows, value_cols)
+    return pl.pallas_call(
+        functools.partial(mixed_kernel, heads),
+        grid=(rows // step,),
+        in_specs=specs,
+        out_specs=[
+            block(value_cols),
+            pl.BlockSpec((heads, step, rows), lambda i: (0, i, 0)),
+        ],
+        out_shape=[
+            jax.ShapeDtypeStruct((rows, value_cols), bf16),
+            jax.ShapeDtypeStruct((heads, rows, rows), bf16),
+        ],
+        compiler_params=pltpu.CompilerParams(vmem_limit_bytes=48 << 20),
+        cost_estimate=pl.CostEstimate(
+            flops=2 * heads * rows * rows * (KEY_DIM + VAL_DIM),
+            bytes_accessed=heads * rows * rows * 2 + rows * value_cols * 8,
+            transcendentals=rows * value_cols,
+        ),
+    )(query, key, value, value_gate, *tables)
+
+
+def mixed_rows_back(query, key, value, value_gate, tables, weights, grad, cosine, sine):
+    rows, value_cols = value.shape
+    heads = query.shape[1] // KEY_DIM
+    step = min(rows, 256)
+    half = KEY_DIM // 2
+    specs, block, whole = retention_specs(heads, step, rows, value_cols)
+    return pl.pallas_call(
+        functools.partial(mixed_grad_kernel, heads),
+        grid=(rows // step,),
+        in_specs=specs
+        + [pl.BlockSpec((heads, step, rows), lambda i: (0, i, 0)), block(value_cols)]
+        + [block(half)] * 2
+        + [whole(rows, half)] * 2,
+        out_specs=[
+            block(heads * KEY_DIM),
+            block(value_cols),
+            whole(rows, heads * KEY_DIM),
+            whole(rows, value_cols),
+        ],
+        out_shape=[
+            jax.ShapeDtypeStruct((rows, heads * KEY_DIM), bf16),
+            jax.ShapeDtypeStruct((rows, value_cols), bf16),
+            jax.ShapeDtypeStruct((rows, heads * KEY_DIM), bf16),
+            jax.ShapeDtypeStruct((rows, value_cols), bf16),
+        ],
+        scratch_shapes=[
+            pltpu.VMEM((heads, rows, KEY_DIM), f32),
+            pltpu.VMEM((heads, rows, VAL_DIM), f32),
+        ],
+        compiler_params=pltpu.CompilerParams(vmem_limit_bytes=56 << 20),
+        cost_estimate=pl.CostEstimate(
+            flops=2 * heads * rows * rows * (2 * KEY_DIM + 3 * VAL_DIM),
+            bytes_accessed=heads * rows * rows * 2 + rows * value_cols * 16,
+            transcendentals=rows * value_cols,
+        ),
+    )(query, key, value, value_gate, *tables, weights, grad, cosine, sine, cosine, sine)
 
 
 def slab_routes():
@@ -420,23 +556,14 @@
         bin_order[:, :, None] == jnp.arange(seqs, dtype=jnp.int32)[None, None, :]
     ).astype(bf16)
 
-    qkvg_own = jnp.concatenate(
-        [padded(own_columns(weight)) for weight in (w_query, w_key, w_value, w_gate)],
-        axis=1,
-    )
-    qkvg_cols = qkvg_own.shape[1]
-    cut = qkvg_cols // 2
-    qkvg = [Gather(qkvg_own[:, :cut], 0), Gather(qkvg_own[:, cut:], 1)]
+    qk = Gather(jnp.concatenate([own_columns(w_query), own_columns(w_key)], axis=1), 0)
+    vg = Gather(
+        jnp.concatenate([padded(own_columns(w_value)), padded(own_columns(w_gate))], axis=1), 1
+    )
 
     def tick(rings, free=False):
         for ring in rings:
             ring.tick(free)
-
-    def mix_tail(retained, gate):
-        normed = retained * lax.rsqrt(
-            jnp.mean(retained * retained, axis=-1, keepdims=True) + GROUP_EPS
-        )
-        return jax.nn.silu(gate) * normed
 
     frequency = jnp.exp(
         -jnp.arange(KEY_DIM // 2, dtype=f32) * (2.0 / KEY_DIM) * math.log(10000.0)
@@ -447,12 +574,12 @@
     t = {
         "cos": jnp.cos(angles),
         "sin": jnp.sin(angles),
-        "grow": jnp.exp(spans),
+        "grow": jnp.exp(spans).T,
         "shrink": jnp.exp(-spans),
     }
 
     for _ in range(members // 2):
-        tick(qkvg, free=True)
+        tick([qk, vg], free=True)
     e = {
         "rows": lax.all_to_all(
             tokens.reshape(members, strip, width), "grp", split_axis=0, concat_axis=0, tiled=True
@@ -470,18 +597,14 @@
     }
     fence(e, t)
     cosine, sine = t["cos"], t["sin"]
-    lag = positions[:, None] >= positions[None, :]
-
-    def turn(pre, sign):
+    def turn(pre):
         half = KEY_DIM // 2
         front, back = pre[:, :half], pre[:, half:]
         return jnp.concatenate(
-            [front * cosine - sign * back * sine, back * cosine + sign * front * sine], axis=1
+            [front * cosine - back * sine, back * cosine + front * sine], axis=1
         )
 
-    def decayed(scores, h):
-        decay = t["grow"][h][:, None] * t["shrink"][h][None, :]
-        return (scores * jnp.where(lag, decay, 0.0)).astype(bf16)
+    tables = (t["grow"], t["shrink"], positions[:, None], positions[None, :])
 
     x = e["rows"].reshape(own_rows, width).astype(f32)
     gains = e.pop("gains").transpose(1, 0, 2).reshape(2, width).astype(f32)
@@ -503,39 +626,49 @@
     fence(e)
 
     acts = e["acts"]
-    weight_qkvg = assembled([(qkvg[0], 0, 0), (qkvg[1], 0, cut)], member_rows, qkvg_cols)
+    weight_qk = assembled([(qk, 0, 0)], member_rows, 2 * qk_cols)
     tick([out])
-    pre = dot(acts, weight_qkvg)
-    gate_at = 2 * qk_cols + val_cols + -val_cols % 128
-    value = pre[:, 2 * qk_cols : 2 * qk_cols + val_cols].astype(bf16)
-    gate_pre = pre[:, gate_at : gate_at + val_cols]
-    query, key = [], []
-    for h in range(heads):
-        query.append(turn(pre[:, h * KEY_DIM : (h + 1) * KEY_DIM], 1.0).astype(bf16))
-        key.append(
-            turn(pre[:, qk_cols + h * KEY_DIM : qk_cols + (h + 1) * KEY_DIM], 1.0).astype(bf16)
-        )
-    e = {"query": query, "cot": e["cot"], "down": e["down"], "pu": e["pu"]}
-    fence(e, rings=[out])
-    query = e["query"]
+    pre = dot(acts, weight_qk)
+    def turned(at):
+        parts = [
+            turn(pre[:, at + h * KEY_DIM : at + (h + 1) * KEY_DIM]).astype(bf16)
+            for h in range(heads)
+        ]
+        return jnp.concatenate(parts, axis=1)
+
+    query, key = turned(0), turned(qk_cols)
+    e = {
+        "query": query,
+        "key": key,
+        "cot": e["cot"],
+        "down": e["down"],
+        "pu": e["pu"],
+        "acts": acts,
+    }
+    fence(e, done=[vg])
+    query, key, acts = e["query"], e["key"], e["acts"]
+    weight_vg = assembled([(vg, 0, 0)], member_rows, vg.part.shape[1])
     tick([out])
-
-    values, weights, mixed, tails = [], [], [], []
-    for h in range(heads):
-        values.append(value[:, h * VAL_DIM : (h + 1) * VAL_DIM])
-        weights.append(decayed(dot_t(query[h], key[h]), h))
-        retained = dot(weights[h], values[h])
-        mix, pull = jax.vjp(mix_tail, retained, gate_pre[:, h * VAL_DIM : (h + 1) * VAL_DIM])
-        mixed.append(mix.astype(bf16))
-        tails.append(pull)
-    mixed_b = padded(jnp.concatenate(mixed, axis=1))
+    gate_at = vg.part.shape[1] // 2
+    value_gate = dot(acts, weight_vg)
+    e = {
+        "cot": e["cot"],
+        "down": e["down"],
+        "pu": e["pu"],
+        "value": value_gate[:, :gate_at].astype(bf16),
+    }
+    fence(e, done=[out])
+    value = e["value"]
+    tick([out])
+
+    mixed_b, weights = mixed_rows(query, key, value, value_gate, tables)
     tick([out], free=True)
-    e = {"mixed": mixed_b, "cot": e["cot"], "down": e["down"], "pu": e["pu"]}
-    fence(e, rings=[out])
     pu = [Gather(e["pu"][0], 0), Gather(e["pu"][1], 1)]
+    tick(pu)
+    e = {"mixed": mixed_b, "cot": e["cot"], "down": e["down"]}
+    fence(e, done=[out] + pu)
+    tick(pu)
     down = Gather(padded(e["down"]), 0)
-    ff = pu + [down]
-    tick(ff)
     mixed_b = e["mixed"]
     cot_seqs = jnp.einsum("msk,mkrd->msrd", selector, e["cot"], preferred_element_type=f32)
     cot_seqs = cot_seqs.astype(bf16).reshape(members, strip, width)
@@ -543,24 +676,24 @@
 
     held = by_place(dot_t(mixed_b, weight_out))
     e = {"came": sum_send(held, 1), "cot": cot_seqs}
-    fence(e, rings=ff)
+    fence(e, done=pu)
     held = sum_take(held, e["came"], 1)
-    tick(ff)
+    tick(pu)
     e = {
         "sum": sum_far(held),
         "cot": lax.all_to_all(e["cot"], "grp", split_axis=0, concat_axis=0, tiled=True),
     }
-    fence(e, rings=ff)
+    fence(e, done=pu)
 
     hidden = x + e["sum"]
     out_grad = e["cot"].reshape(own_rows, width).astype(f32) * live
     normed_mid, mid_pullback = jax.vjp(norm_rows, hidden, gain_two)
-    tick(ff)
+    tick(pu + [down])
     e = {"mid": pieces_far(normed_mid.astype(bf16)), "cot": out_grad.astype(bf16)}
-    fence(e, rings=ff)
-    tick(ff)
+    fence(e, done=pu + [down])
+    tick([down])
     e = {"mid": rows_near(e["mid"]), "cot": pieces_far(e["cot"])}
-    fence(e, rings=ff)
+    fence(e, rings=[down])
 
     middle = e["mid"]
     hid = pu[0].part.shape[1]
@@ -574,11 +707,12 @@
 
     glu_rows, glu_pullback = jax.vjp(glu_act, proj_pre, up_pre)
     glu_b = glu_rows.astype(bf16)
+    tick([down])
     ring_down = [Scatter(out_grad_full, glu_b, 0)]
     e = {"cot": out_grad_full, "glu": glu_b}
-    fence(e, rings=ring_down)
+    fence(e, done=[down])
+    tick([down])
     weight_down = assembled([(down, 0, 0)], member_rows, down.part.shape[1])
-    tick(ring_down)
     proj_grad, up_grad = glu_pullback(dot(e["cot"], weight_down))
     pu_grad = jnp.concatenate([proj_grad, up_grad], axis=1).astype(bf16)
     held = by_place(dot_t(pu_grad, weight_pu))
@@ -604,47 +738,32 @@
     branch = e["branch"]
 
     mixed_grad = dot(branch, weight_out)
-    retained_grads, gate_grads = [], []
-    for h in range(heads):
-        retained_grad, gate_grad = tails[h](mixed_grad[:, h * VAL_DIM : (h + 1) * VAL_DIM])
-        retained_grads.append(retained_grad.astype(bf16))
-        gate_grads.append(gate_grad.astype(bf16))
-    gate_grad = padded(jnp.concatenate(gate_grads, axis=1))
+    query_grad, gate_grad, key_grad, value_grad = mixed_rows_back(
+        query, key, value, value_gate, tables, weights, mixed_grad, cosine, sine
+    )
     tick(ring_ff)
     held = sum_take(held, e["rows"], 1)
     ring_og = [Scatter(acts, gate_grad, 0), Scatter(branch, mixed_b, 1)]
     tick(ring_og)
-    e = {"retained": retained_grads, "rows": sum_far(held)}
+    e = {
+        "qk": jnp.concatenate([query_grad, key_grad], axis=1),
+        "value": value_grad,
+        "gate": gate_grad,
+        "rows": sum_far(held),
+    }
     fence(e, rings=ring_ff)
-    retained_grads = e["retained"]
+    qk_grad, value_grad, gate_grad = e["qk"], e["value"], e["gate"]
     out_rows = hidden + e["rows"]
-
     tick(ring_og)
-    scores, value_grads = [], []
-    for h in range(heads):
-        scores.append(decayed(dot_t(retained_grads[h], values[h]), h))
-        value_grads.append(t_dot(weights[h], retained_grads[h]).astype(bf16))
-    value_grad = padded(jnp.concatenate(value_grads, axis=1))
-    e = {
-        "scores": scores,
-        "ff": [ring.whole() for ring in ring_ff],
-        "value": value_grad,
-        "rows": out_rows.astype(bf16),
-    }
-    fence(e, rings=ring_og)
-    scores, ff, value_grad = e["scores"], e["ff"], e["value"]
+    ff = [ring.whole() for ring in ring_ff]
     ring_v = Scatter(acts, value_grad, 1)
-    tick(ring_og)
-    query_grads, key_grads = [], []
-    for h in range(heads):
-        query_grads.append(turn(dot(scores[h], key[h]), -1.0).astype(bf16))
-        key_grads.append(turn(t_dot(scores[h], query[h]), -1.0).astype(bf16))
-    qk_grad = jnp.concatenate(query_grads + key_grads, axis=1)
-    e = {
-        "grad": qk_grad,
+    ring_qk = Scatter(acts, qk_grad, 0)
+    e = {
+        "qk": qk_grad,
+        "full": [ring_v.full, ring_qk.full],
         "pu": pieces_far(jnp.concatenate(ff[:2], axis=1)),
         "rows": lax.all_to_all(
-            e["rows"].reshape(members, strip, width),
+            out_rows.astype(bf16).reshape(members, strip, width),
             "grp",
             split_axis=0,
             concat_axis=0,
@@ -653,37 +772,31 @@
         "down": ff[2],
     }
     fence(e, rings=ring_og)
-    qk_grad, pu_far = e["grad"], e["pu"]
+    qk_grad, pu_far = e["qk"], e["pu"]
+    ring_v.full, ring_qk.full = e["full"]
     out_seqs = e["rows"].reshape(micro, seqs, strip, width)
     out_bins = jnp.einsum("msk,msrd->mkrd", selector, out_seqs, preferred_element_type=f32)
 
-    tick(ring_og + [ring_v])
-    held = by_place(
-        dot_t(jnp.concatenate([qk_grad, value_grad, gate_grad], axis=1), weight_qkvg)
-    )
-    ring_qk = Scatter(acts, qk_grad, 0)
+    tick(ring_og + [ring_v, ring_qk])
+    vg_grad = jnp.concatenate([value_grad, gate_grad], axis=1)
+    held = by_place(dot_t(qk_grad, weight_qk) + dot_t(vg_grad, weight_vg))
     e = {
         "came": sum_send(held, 1),
         "pu": pieces_near(pu_far),
         "bins": lax.all_to_all(
             out_bins.astype(bf16), "rep", split_axis=1, concat_axis=1, tiled=True
         ),
-        "down": e["down"],
+        "down": slab_rows(e["down"][:, :hid_cols]),
     }
     fence(e, rings=ring_og)
     bin_out = e["bins"].reshape(micro, 1, block, width)
     held = sum_take(held, e["came"], 1)
-    tick([ring_qk, ring_v])
-    e = {
-        "sum": sum_far(held),
-        "gate": ring_og[0].whole(),
-        "out": ring_og[1].whole(),
-        "down": e["down"],
-        "pu": e["pu"],
-    }
-    fence(e)
+    tick(ring_og + [ring_v, ring_qk])
+    e = {"sum": sum_far(held), "down": e["down"], "pu": e["pu"]}
+    fence(e, rings=[ring_v, ring_qk], done=ring_og)
+    gate_part, out_mine = ring_og[0].whole(), slab_rows(ring_og[1].whole()[:, :val_cols])
     input_grad = hidden_grad + norm_pullback(e["sum"])[0]
-    tick([ring_qk, ring_v])
+    tick([ring_v, ring_qk])
     e = {
         "rows": lax.all_to_all(
             input_grad.astype(bf16).reshape(members, strip, width),
@@ -692,33 +805,29 @@
             concat_axis=0,
             tiled=True,
         ),
-        "gate": pieces_far(e["gate"]),
-        "down": slab_rows(e["down"][:, :hid_cols]),
-        "out": e["out"],
+        "gate": pieces_far(gate_part),
+        "slabs": jnp.concatenate([e["down"], out_mine], axis=1),
         "pu": e["pu"],
     }
-    fence(e, rings=[ring_qk, ring_v])
+    fence(e, rings=[ring_v, ring_qk])
     token_grad = e["rows"].reshape(tokens.shape)
 
-    tick([ring_qk, ring_v])
+    tick([ring_v, ring_qk])
     proj_owned, up_owned, gain_two_owned = finished(
         e["pu"], ((0, hid_cols), (hid, hid_cols)), mlp_gain, (w_proj, w_up)
     )
     e = {
         "gate": pieces_near(e["gate"]),
-        "slabs": pieces_far(
-            jnp.concatenate([e["down"], slab_rows(e["out"][:, :val_cols])], axis=1)
-        ),
+        "slabs": pieces_far(e["slabs"]),
         "gain": gain_two_owned,
     }
-    fence(e, rings=[ring_qk, ring_v])
+    fence(e, done=[ring_v, ring_qk])
     gain_two_owned = e["gain"]
-    tick([ring_qk])
     gate_owned, gate_sum = finished(e["gate"], ((0, val_cols),), norm_gain, (w_gate,))
     e = {
         "slabs": pieces_near(e["slabs"]),
+        "last": pieces_far(jnp.concatenate([ring_qk.whole(), ring_v.whole()], axis=1)),
         "gain": gate_sum,
-        "last": pieces_far(jnp.concatenate([ring_qk.whole(), ring_v.whole()], axis=1)),
     }
     fence(e)
     size = width // reps

time: 1010 us -> 1010 us (level); the launches traced: 1000 us -> 992 us
  starting transfers between devices: 282 us -> 226 us
  waiting for transfers between devices: 309 us -> 358 us
  Pallas kernels: 38.9 us -> 64.9 us
  matrix products: 148 us -> 129 us
    ppermute x32, starting transfers between devices: 65.5 us -> 32.5 us  [swap(): return lax.ppermute(value, 'rep', [(i, i ^ bit) for i in range(count)])]
    pallas_call x0 -> x2, Pallas kernels: none -> 31.3 us  [the longest x1 22.7 us: mixed_rows_back(): pl.pallas_call(functools.partial(mixed_grad_kernel, heads), grid=(rows //...]
    ppermute x32, waiting for transfers between devices: 36.9 us -> 64.9 us  [swap(): return lax.ppermute(value, 'rep', [(i, i ^ bit) for i in range(count)])]
    ppermute x91, waiting for transfers between devices: 245 us -> 226 us  [ring_step(): lax.ppermute(value, 'grp', [(ring[i], ring[(i + ahead) % count]) for i in...]
    ppermute x91, starting transfers between devices: 169 us -> 152 us  [ring_step(): lax.ppermute(value, 'grp', [(ring[i], ring[(i + ahead) % count]) for i in...]
    all_to_all x1, waiting for transfers between devices: 0.01 us -> 16.9 us  [body(): lax.all_to_all(tokens.reshape(members, strip, width), 'grp', split_axis=0...]
    all_to_all x1, waiting for transfers between devices: 3.59 us -> 20.1 us  [body(): lax.all_to_all(jnp.broadcast_to(jnp.stack([norm_gain, mlp_gain]), (member...]
    ppermute x4, waiting for transfers between devices: 9.08 us -> 21.3 us  [slab_piece(): lax.ppermute(sent, ('rep', 'grp'), route)]
  transfers between devices with their start and end apart: 138 -> 138, of which waited for: 50 -> 54; matrix products, arithmetic and copies ran while one was open for 25% -> 25% of each run, Pallas kernels for 3% -> 5%
where the time goes in v3:
time: 1010 us; the launch traced here: 992 us
  waiting for transfers between devices  358 us (35%)
  starting transfers between devices  226 us (22%)
  matrix products  129 us (13%)
  other arithmetic  121 us (12%)
  local copies, waits for them, and re-layouts  90.3 us (9%)
  Pallas kernels  64.9 us (6%)
    ppermute x91, waiting for transfers between devices, ring_step(): lax.ppermute(value, 'grp', [(ring[i], ring[(i + ahead) % count]) for i in...  226 us
    ppermute x91, starting transfers between devices, ring_step(): lax.ppermute(value, 'grp', [(ring[i], ring[(i + ahead) % count]) for i in...  152 us
    ppermute x32, waiting for transfers between devices, swap(): return lax.ppermute(value, 'rep', [(i, i ^ bit) for i in range(count)])  64.9 us
    dot_general x5, matrix products, dot_t(): lax.dot_general(left, right, (((1,), (1,)), ((), ())), preferred_element_...  50.4 us
    dot_general x5, matrix products, dot(): return jnp.dot(left, right, preferred_element_type=f32)  38.5 us
    dot_general x7, matrix products, t_dot(): lax.dot_general(left, right, (((0,), (0,)), ((), ())), preferred_element_...  37 us
    convert_element_type x22, other arithmetic, next(): return term.astype(bf16)  36.9 us
    unnamed x281, local copies, waits for them, and re-layouts  36.7 us
  transfers between devices with their start and end apart: 138, of which 54 were waited for; matrix products, arithmetic and copies ran while one was open for 25% of the time, Pallas kernels for 5%

profile of v3, /device:TPU:0, one launch (start us, length us, event | category | flops | bytes accessed | tf_op | source)
XLA Modules:
  0.0 992.4 jit_solution(1070744038461379850)
XLA Ops:
  21.0 20.1 %all-to-all-done = bf16[8,2,256]{2,1,0:T(2,128)(2,1)S(1)} async-done(((bf16[8,2,256]{2,1,0:T(2,128)(2,1)}), bf16[8,2,256]{2,1,0:T(2,128)(2,1)S(1)}, u32[]{:S(2)}, u32[]{:S(2)}) %all-to-all-start) | async-done | bytes 8224 | tf_op jit(solution)/shard_map/all_to_all | solution.py:590
  55.6 16.9 %all-to-all-done.1 = bf16[8,32,2048]{2,1,0:T(8,128)(2,1)} async-done(((bf16[8,32,2048]{2,1,0:T(8,128)(2,1)}), bf16[8,32,2048]{2,1,0:T(8,128)(2,1)}, u32[]{:S(2)}, u32[]{:S(2)}) %all-to-all-start.1) | async-done | bytes 1048608 | tf_op jit(solution)/shard_map/all_to_all | solution.py:584
  93.9 17.1 %collective-permute-start.2 = (bf16[256,2048]{1,0:T(8,128)(2,1)}, bf16[256,2048]{1,0:T(8,128)(2,1)}, u32[]{:S(2)}, u32[]{:S(2)}) collective-permute-start(bf16[256,2048]{1,0:T(8,128)(2,1)} %fusion.25), channel_id=1, source_target_pairs={{0,16},{8,24},{16,0},{24,8},{1,17},{9,25},{17,1},{25,9},{2,18},{10... | collective-permute-start | bytes 3145736 | tf_op jit(solution)/shard_map/ppermute | solution.py:40
  125.3 16.9 %collective-permute-done.12.refs_5_ = bf16[256,1024]{1,0:T(8,128)(2,1)S(1)} collective-permute-done((bf16[256,1024]{1,0:T(8,128)(2,1)}, bf16[256,1024]{1,0:T(8,128)(2,1)S(1)}, u32[]{:S(2)}, u32[]{:S(2)}) %collective-permute-start.12) | collective-permute-done | bytes 524320 | tf_op jit(solution)/shard_map/ppermute | solution.py:130
  162.3 18.0 %collective-permute-done.5 = bf16[256,432]{0,1:T(8,128)(2,1)} collective-permute-done((bf16[256,432]{0,1:T(8,128)(2,1)}, bf16[256,432]{0,1:T(8,128)(2,1)}, u32[]{:S(2)}, u32[]{:S(2)}) %collective-permute-start.5) | collective-permute-done | bytes 221216 | tf_op jit(solution)/shard_map/ppermute | solution.py:488
  203.4 9.7 collective-permute-start.22
  258.8 8.6 shard_map.231
  325.1 20.6 %collective-permute-done.37 = bf16[256,2048]{1,0:T(8,128)(2,1)S(1)} collective-permute-done((bf16[256,2048]{1,0:T(8,128)(2,1)S(1)}, bf16[256,2048]{1,0:T(8,128)(2,1)S(1)}, u32[]{:S(2)}, u32[]{:S(2)}) %collective-permute-start.37) | collective-permute-done | bytes 1048608 | tf_op jit(solution)/shard_map/ppermute | solution.py:40
  375.8 15.1 %collective-permute-done.43.refs_4_ = bf16[256,896]{1,0:T(8,128)(2,1)S(1)} collective-permute-done((bf16[256,896]{1,0:T(8,128)(2,1)S(1)}, bf16[256,896]{1,0:T(8,128)(2,1)S(1)}, u32[]{:S(2)}, u32[]{:S(2)}) %collective-permute-start.43) | collective-permute-done | bytes 458784 | tf_op jit(solution)/shard_map/ppermute | solution.py:130
  403.6 15.2 %collective-permute-done.47 = bf16[256,2048]{1,0:T(8,128)(2,1)S(1)} collective-permute-done((bf16[256,2048]{1,0:T(8,128)(2,1)S(1)}, bf16[256,2048]{1,0:T(8,128)(2,1)S(1)}, u32[]{:S(2)}, u32[]{:S(2)}) %collective-permute-start.47) | collective-permute-done | bytes 1048608 | tf_op jit(solution)/shard_map/ppermute | solution.py:40
  453.8 12.2 %fusion.6 = (bf16[1024,896]{1,0:T(8,128)(2,1)S(1)}, bf16[1024,896]{1,0:T(8,128)(2,1)S(1)}) fusion(f32[1024,1792]{1,0:T(8,128)} %copy-done.55, bf16[1024,2048]{1,0:T(8,128)(2,1)} %copy-done.114, bf16[2048,896]{1,0:T(8,128)(2,1)S(1)} %shard_map.234), kind=kOutput, calls=%fused_computation.13 | convolution fusion | flops 3780116480 | bytes 18874368 | tf_op jit(solution)/shard_map/dot_general | solution.py:27
  466.1 10.1 %fusion.54 = (bf16[1024,2048]{1,0:T(8,128)(2,1)S(1)}, f32[1024,2048]{1,0:T(8,128)}) fusion(bf16[2048,1792]{1,0:T(8,128)(2,1)S(1)} %bitcast.111, bf16[1024,896]{1,0:T(8,128)(2,1)S(1)} %get-tuple-element.457, bf16[1024,896]{1,0:T(8,128)(2,1)S(1)} %get-tuple-element.456), kind=kOutput, calls=%fused_computation.218 | convolution fusion | flops 7525629952 | bytes 23592960 | tf_op jit(solution)/shard_map/dot_general | solution.py:31
  531.9 8.7 collective-permute-done.63
  552.3 10.1 %collective-permute-done.71 = bf16[256,896]{1,0:T(8,128)(2,1)} collective-permute-done((bf16[256,896]{1,0:T(8,128)(2,1)}, bf16[256,896]{1,0:T(8,128)(2,1)}, u32[]{:S(2)}, u32[]{:S(2)}) %collective-permute-start.71) | collective-permute-done | bytes 458784 | tf_op jit(solution)/shard_map/ppermute | solution.py:130
  608.6 22.7 %shard_map.235 = (bf16[1024,512]{1,0:T(8,128)(2,1)}, bf16[1024,896]{1,0:T(8,128)(2,1)}, bf16[1024,512]{1,0:T(8,128)(2,1)}, bf16[1024,896]{1,0:T(8,128)(2,1)}) custom-call(bf16[1024,512]{1,0:T(8,128)(2,1)} %copy-done.3, bf16[1024,512]{1,0:T(8,128)(2,1)} %copy-done.2, bf16[1024,896]{1,0:T(8,128)(2,1)} %slice.286.v_ref, f32[1024,1792]{1,0:T(8,128)} %copy-done.53, ...), custom_call_target="tpu_custom_call" | custom-call | flops 7583301632 | bytes 18874368 | tf_op jit(solution)/shard_map/pallas_call | solution.py:422
  679.0 13.4 %fusion.7 = f32[1024,2048]{1,0:T(8,128)} fusion(bf16[2048,1792]{1,0:T(8,128)(2,1)} %copy-done, bf16[1024,896]{1,0:T(8,128)(2,1)} %get-tuple-element.342, bf16[1024,896]{1,0:T(8,128)(2,1)} %get-tuple-element.329), kind=kOutput, calls=%fused_computation.16 | convolution fusion | flops 7523532800 | bytes 19398656 | tf_op jit(solution)/shard_map/dot_general | solution.py:31
  717.9 13.4 %fusion.56 = (bf16[1024,2048]{1,0:T(8,128)(2,1)S(1)}, f32[1024,2048]{1,0:T(8,128)}) fusion(f32[1024,2048]{1,0:T(8,128)} %fusion.7, bf16[1024,1024]{1,0:T(8,128)(2,1)} %pad_maximum_fusion.7, bf16[2048,1024]{1,0:T(8,128)(2,1)} %copy-done.4), kind=kOutput, calls=%fused_computation.220 | convolution fusion | flops 4299161600 | bytes 27262976 | tf_op jit(solution)/shard_map/dot_general | solution.py:31
  739.3 9.0 collective-permute-done.95
  772.2 14.4 %collective-permute-done.96 = bf16[256,896]{1,0:T(8,128)(2,1)S(1)} collective-permute-done((bf16[256,896]{1,0:T(8,128)(2,1)S(1)}, bf16[256,896]{1,0:T(8,128)(2,1)S(1)}, u32[]{:S(2)}, u32[]{:S(2)}) %collective-permute-start.96) | collective-permute-done | bytes 458784 | tf_op jit(solution)/shard_map/ppermute | solution.py:130
  809.4 16.8 %collective-permute-done.109 = bf16[256,896]{0,1:T(8,128)(2,1)} collective-permute-done((bf16[256,896]{0,1:T(8,128)(2,1)}, bf16[256,896]{0,1:T(8,128)(2,1)}, u32[]{:S(2)}, u32[]{:S(2)}) %collective-permute-start.109) | collective-permute-done | bytes 458784 | tf_op jit(solution)/shard_map/ppermute | solution.py:130
  849.8 9.5 collective-permute-done.100
  897.0 12.9 %collective-permute-done.121 = bf16[256,896]{1,0:T(8,128)(2,1)S(1)} collective-permute-done((bf16[256,896]{1,0:T(8,128)(2,1)S(1)}, bf16[256,896]{1,0:T(8,128)(2,1)S(1)}, u32[]{:S(2)}, u32[]{:S(2)}) %collective-permute-start.121) | collective-permute-done | bytes 458784 | tf_op jit(solution)/shard_map/ppermute | solution.py:130
  911.0 17.2 %collective-permute-start.120 = (bf16[256,896]{1,0:T(8,128)(2,1)}, bf16[256,896]{1,0:T(8,128)(2,1)S(1)}, u32[]{:S(2)}, u32[]{:S(2)}) collective-permute-start(bf16[256,896]{1,0:T(8,128)(2,1)} %get-tuple-element.388), channel_id=1, source_target_pairs={{0,2},{2,4},{4,6},{6,7},{7,5},{5,3},{3,1},{1,0},{8,10},{10,12},{12... | collective-permute-start | bytes 1376264 | tf_op jit(solution)/shard_map/ppermute | solution.py:130
  958.0 12.2 %collective-permute-done.126.refs_2_ = bf16[256,1920]{1,0:T(8,128)(2,1)} collective-permute-done((bf16[256,1920]{1,0:T(8,128)(2,1)S(1)}, bf16[256,1920]{1,0:T(8,128)(2,1)}, u32[]{:S(2)}, u32[]{:S(2)}) %collective-permute-start.126) | collective-permute-done | bytes 983072 | tf_op jit(solution)/shard_map/ppermute | solution.py:40
  (715 shorter events, 648.5 us)
Async XLA Ops:
  1.8 109.2 %collective-permute-start.7 = (bf16[256,1024]{1,0:T(8,128)(2,1)S(1)}, bf16[256,1024]{1,0:T(8,128)(2,1)S(1)}, u32[]{:S(2)}, u32[]{:S(2)}) collective-permute-start(bf16[256,1024]{1,0:T(8,128)(2,1)S(1)} %pad_maximum_fusion.14.refs_0_), channel_id=1, source_target_pairs={{0,1},{2,0},{4,2},{6,4},{7,6},{5,7},{3,5},{1,3},{8,9},{10,8},{12,1... | collective-permute-start | bytes 1572872 | tf_op jit(solution)/shard_map/ppermute | solution.py:130
  4.8 74.7 %collective-permute-start.10 = (bf16[256,1024]{1,0:T(8,128)(2,1)S(1)}, bf16[256,1024]{1,0:T(8,128)(2,1)}, u32[]{:S(2)}, u32[]{:S(2)}) collective-permute-start(bf16[256,1024]{1,0:T(8,128)(2,1)S(1)} %pad_maximum_fusion.14.refs_0_), channel_id=1, source_target_pairs={{0,2},{2,4},{4,6},{6,7},{7,5},{5,3},{3,1},{1,0},{8,10},{10,12},{12... | collective-permute-start | bytes 1572872 | tf_op jit(solution)/shard_map/ppermute | solution.py:130
  6.8 104.2 %collective-permute-start.14 = (bf16[256,1792]{1,0:T(8,128)(2,1)S(1)}, bf16[256,1792]{1,0:T(8,128)(2,1)S(1)}, u32[]{:S(2)}, u32[]{:S(2)}) collective-permute-start(bf16[256,1792]{1,0:T(8,128)(2,1)S(1)} %fusion.33.refs_0_), channel_id=1, source_target_pairs={{0,2},{2,4},{4,6},{6,7},{7,5},{5,3},{3,1},{1,0},{8,10},{10,12},{12... | collective-permute-start | bytes 2752520 | tf_op jit(solution)/shard_map/ppermute | solution.py:130
  8.9 44.9 %collective-permute-start.17 = (bf16[256,1792]{1,0:T(8,128)(2,1)S(1)}, bf16[256,1792]{1,0:T(8,128)(2,1)}, u32[]{:S(2)}, u32[]{:S(2)}) collective-permute-start(bf16[256,1792]{1,0:T(8,128)(2,1)S(1)} %fusion.33.refs_0_), channel_id=1, source_target_pairs={{0,1},{2,0},{4,2},{6,4},{7,6},{5,7},{3,5},{1,3},{8,9},{10,8},{12,1... | collective-permute-start | bytes 2752520 | tf_op jit(solution)/shard_map/ppermute | solution.py:130
  53.7 65.3 %collective-permute-start.18 = (bf16[256,1792]{1,0:T(8,128)(2,1)}, bf16[256,1792]{1,0:T(8,128)(2,1)}, u32[]{:S(2)}, u32[]{:S(2)}) collective-permute-start(bf16[256,1792]{1,0:T(8,128)(2,1)} %collective-permute-done.17.refs_1_), channel_id=1, source_target_pairs={{0,1},{2,0},{4,2},{6,4},{7,6},{5,7},{3,5},{1,3},{8,9},{10,8},{12,1... | collective-permute-start | bytes 2752520 | tf_op jit(solution)/shard_map/ppermute | solution.py:130
  93.9 56.0 %collective-permute-start.2 = (bf16[256,2048]{1,0:T(8,128)(2,1)}, bf16[256,2048]{1,0:T(8,128)(2,1)}, u32[]{:S(2)}, u32[]{:S(2)}) collective-permute-start(bf16[256,2048]{1,0:T(8,128)(2,1)} %fusion.25), channel_id=1, source_target_pairs={{0,16},{8,24},{16,0},{24,8},{1,17},{9,25},{17,1},{25,9},{2,18},{10... | collective-permute-start | bytes 3145736 | tf_op jit(solution)/shard_map/ppermute | solution.py:40
  111.0 41.4 %collective-permute-start.15 = (bf16[256,1792]{1,0:T(8,128)(2,1)S(1)}, bf16[256,1792]{1,0:T(8,128)(2,1)}, u32[]{:S(2)}, u32[]{:S(2)}) collective-permute-start(bf16[256,1792]{1,0:T(8,128)(2,1)S(1)} %collective-permute-done.14.refs_7_), channel_id=1, source_target_pairs={{0,2},{2,4},{4,6},{6,7},{7,5},{5,3},{3,1},{1,0},{8,10},{10,12},{12... | collective-permute-start | bytes 2752520 | tf_op jit(solution)/shard_map/ppermute | solution.py:130
  149.9 49.0 %collective-permute-start.4 = (bf16[256,2048]{1,0:T(8,128)(2,1)}, bf16[256,2048]{1,0:T(8,128)(2,1)}, u32[]{:S(2)}, u32[]{:S(2)}) collective-permute-start(bf16[256,2048]{1,0:T(8,128)(2,1)} %collective-permute-done.2), channel_id=1, source_target_pairs={{0,8},{8,0},{16,24},{24,16},{1,9},{9,1},{17,25},{25,17},{2,10},{10... | collective-permute-start | bytes 3145736 | tf_op jit(solution)/shard_map/ppermute | solution.py:40
  152.4 46.4 %collective-permute-start.3 = (bf16[256,2048]{1,0:T(8,128)(2,1)}, bf16[256,2048]{1,0:T(8,128)(2,1)}, u32[]{:S(2)}, u32[]{:S(2)}) collective-permute-start(bf16[256,2048]{1,0:T(8,128)(2,1)} %fusion.25), channel_id=1, source_target_pairs={{0,8},{8,0},{16,24},{24,16},{1,9},{9,1},{17,25},{25,17},{2,10},{10... | collective-permute-start | bytes 3145736 | tf_op jit(solution)/shard_map/ppermute | solution.py:40
  314.3 43.3 %all-to-all-start.3 = ((bf16[8,32,2048]{2,1,0:T(8,128)(2,1)}), bf16[8,32,2048]{2,1,0:T(8,128)(2,1)}, u32[]{:S(2)}, u32[]{:S(2)}) async-start(bf16[8,32,2048]{2,1,0:T(8,128)(2,1)} %bitcast.22), calls=%async_computation.3 | async-start | bytes 2097152 | tf_op jit(solution)/shard_map/all_to_all | solution.py:684
  547.9 43.2 %collective-permute-start.68 = (bf16[512,2048]{1,0:T(8,128)(2,1)S(1)}, bf16[512,2048]{1,0:T(8,128)(2,1)}, u32[]{:S(2)}, u32[]{:S(2)}) collective-permute-start(bf16[512,2048]{1,0:T(8,128)(2,1)S(1)} %pad_maximum_fusion.6), channel_id=1, source_target_pairs={{0,8},{8,0},{16,24},{24,16},{1,9},{9,1},{17,25},{25,17},{2,10},{10... | collective-permute-start | bytes 6291464 | tf_op jit(solution)/shard_map/ppermute | solution.py:40
  584.5 60.6 %collective-permute-start.83 = (bf16[256,896]{1,0:T(8,128)(2,1)}, bf16[256,896]{1,0:T(8,128)(2,1)}, u32[]{:S(2)}, u32[]{:S(2)}) collective-permute-start(bf16[256,896]{1,0:T(8,128)(2,1)} %get-tuple-element.333), channel_id=1, source_target_pairs={{0,2},{2,4},{4,6},{6,7},{7,5},{5,3},{3,1},{1,0},{8,10},{10,12},{12... | collective-permute-start | bytes 1376264 | tf_op jit(solution)/shard_map/ppermute | solution.py:130
  588.6 60.1 %collective-permute-start.82 = (bf16[256,896]{1,0:T(8,128)(2,1)}, bf16[256,896]{1,0:T(8,128)(2,1)}, u32[]{:S(2)}, u32[]{:S(2)}) collective-permute-start(bf16[256,896]{1,0:T(8,128)(2,1)} %get-tuple-element.332), channel_id=1, source_target_pairs={{0,1},{2,0},{4,2},{6,4},{7,6},{5,7},{3,5},{1,3},{8,9},{10,8},{12,1... | collective-permute-start | bytes 1376264 | tf_op jit(solution)/shard_map/ppermute | solution.py:130
  606.7 61.6 %collective-permute-start.78 = (bf16[256,2048]{1,0:T(8,128)(2,1)}, bf16[256,2048]{1,0:T(8,128)(2,1)}, u32[]{:S(2)}, u32[]{:S(2)}) collective-permute-start(bf16[256,2048]{1,0:T(8,128)(2,1)} %fusion.16), channel_id=1, source_target_pairs={{0,16},{8,24},{16,0},{24,8},{1,17},{9,25},{17,1},{25,9},{2,18},{10... | collective-permute-start | bytes 3145736 | tf_op jit(solution)/shard_map/ppermute | solution.py:40
  645.1 63.9 %collective-permute-start.86 = (bf16[256,896]{1,0:T(8,128)(2,1)}, bf16[256,896]{1,0:T(8,128)(2,1)}, u32[]{:S(2)}, u32[]{:S(2)}) collective-permute-start(bf16[256,896]{1,0:T(8,128)(2,1)} %get-tuple-element.336), channel_id=1, source_target_pairs={{0,2},{2,4},{4,6},{6,7},{7,5},{5,3},{3,1},{1,0},{8,10},{10,12},{12... | collective-permute-start | bytes 1376264 | tf_op jit(solution)/shard_map/ppermute | solution.py:130
  646.4 62.6 %collective-permute-start.87 = (bf16[256,896]{1,0:T(8,128)(2,1)}, bf16[256,896]{1,0:T(8,128)(2,1)}, u32[]{:S(2)}, u32[]{:S(2)}) collective-permute-start(bf16[256,896]{1,0:T(8,128)(2,1)} %get-tuple-element.337), channel_id=1, source_target_pairs={{0,1},{2,0},{4,2},{6,4},{7,6},{5,7},{3,5},{1,3},{8,9},{10,8},{12,1... | collective-permute-start | bytes 1376264 | tf_op jit(solution)/shard_map/ppermute | solution.py:130
  648.7 60.4 %collective-permute-start.88 = (bf16[256,896]{0,1:T(8,128)(2,1)}, bf16[256,896]{0,1:T(8,128)(2,1)}, u32[]{:S(2)}, u32[]{:S(2)}) collective-permute-start(bf16[256,896]{0,1:T(8,128)(2,1)} %get-tuple-element.338), channel_id=1, source_target_pairs={{0,2},{2,4},{4,6},{6,7},{7,5},{5,3},{3,1},{1,0},{8,10},{10,12},{12... | collective-permute-start | bytes 1376264 | tf_op jit(solution)/shard_map/ppermute | solution.py:130
  674.6 43.3 %all-to-all-start.4 = ((bf16[8,32,2048]{2,1,0:T(8,128)(2,1)}), bf16[8,32,2048]{2,1,0:T(8,128)(2,1)S(1)}, u32[]{:S(2)}, u32[]{:S(2)}) async-start(bf16[8,32,2048]{2,1,0:T(8,128)(2,1)} %bitcast.26), calls=%async_computation.4 | async-start | bytes 2097152 | tf_op jit(solution)/shard_map/all_to_all | solution.py:765
  733.0 64.0 %collective-permute-start.90 = (bf16[512,2048]{1,0:T(8,128)(2,1)}, bf16[512,2048]{1,0:T(8,128)(2,1)}, u32[]{:S(2)}, u32[]{:S(2)}) collective-permute-start(bf16[512,2048]{1,0:T(8,128)(2,1)} %pad_maximum_fusion.8), channel_id=1, source_target_pairs={{0,8},{8,0},{16,24},{24,16},{1,9},{9,1},{17,25},{25,17},{2,10},{10... | collective-permute-start | bytes 6291464 | tf_op jit(solution)/shard_map/ppermute | solution.py:40
  753.3 43.8 %all-to-all-start.5 = ((bf16[2,4,32,2048]{3,2,0,1:T(8,128)(2,1)}), bf16[2,4,32,2048]{3,2,0,1:T(8,128)(2,1)S(1)}, u32[]{:S(2)}, u32[]{:S(2)}) async-start(bf16[2,4,32,2048]{3,2,0,1:T(8,128)(2,1)} %copy.174), calls=%async_computation.5 | async-start | bytes 2097152 | tf_op jit(solution)/shard_map/all_to_all | solution.py:786
  864.2 64.0 %all-to-all-start.6 = ((bf16[8,32,2048]{2,1,0:T(8,128)(2,1)}), bf16[8,32,2048]{2,1,0:T(8,128)(2,1)}, u32[]{:S(2)}, u32[]{:S(2)}) async-start(bf16[8,32,2048]{2,1,0:T(8,128)(2,1)} %bitcast.32), calls=%async_computation.6 | async-start | bytes 2097152 | tf_op jit(solution)/shard_map/all_to_all | solution.py:801
  870.5 57.8 %collective-permute-start.102 = (bf16[256,896]{1,0:T(8,128)(2,1)S(1)}, bf16[256,896]{1,0:T(8,128)(2,1)}, u32[]{:S(2)}, u32[]{:S(2)}) collective-permute-start(bf16[256,896]{1,0:T(8,128)(2,1)S(1)} %add_convert_fusion.16.refs_0_), channel_id=1, source_target_pairs={{0,16},{8,24},{16,0},{24,8},{1,17},{9,25},{17,1},{25,9},{2,18},{10... | collective-permute-start | bytes 1376264 | tf_op jit(solution)/shard_map/ppermute | solution.py:40
  883.9 44.5 %collective-permute-start.123 = (bf16[256,1024]{1,0:T(8,128)(2,1)}, bf16[256,1024]{1,0:T(8,128)(2,1)}, u32[]{:S(2)}, u32[]{:S(2)}) collective-permute-start(bf16[256,1024]{1,0:T(8,128)(2,1)} %get-tuple-element.391), channel_id=1, source_target_pairs={{0,2},{2,4},{4,6},{6,7},{7,5},{5,3},{3,1},{1,0},{8,10},{10,12},{12... | collective-permute-start | bytes 1572872 | tf_op jit(solution)/shard_map/ppermute | solution.py:130
  891.4 49.9 %collective-permute-start.125 = (bf16[256,1024]{1,0:T(8,128)(2,1)}, bf16[256,1024]{1,0:T(8,128)(2,1)S(1)}, u32[]{:S(2)}, u32[]{:S(2)}) collective-permute-start(bf16[256,1024]{1,0:T(8,128)(2,1)} %get-tuple-element.393), channel_id=1, source_target_pairs={{0,1},{2,0},{4,2},{6,4},{7,6},{5,7},{3,5},{1,3},{8,9},{10,8},{12,1... | collective-permute-start | bytes 1572872 | tf_op jit(solution)/shard_map/ppermute | solution.py:130
  (251 other events, 4814.7 us)

commit v4 on v3

--- a/solution.py
+++ b/solution.py
@@ -611,7 +611,6 @@
     gain_one, gain_two = gains[0], gains[1]
     normed, norm_pullback = jax.vjp(norm_rows, x, gain_one)
     e["acts"] = normed.astype(bf16)
-    e["out"] = slab_piece(e["out"])
     e["cot"] = lax.all_to_all(
         cotangent.reshape(micro, reps, strip, width), "rep", split_axis=1, concat_axis=1, tiled=True
     )
@@ -619,11 +618,10 @@
     fence(e)
     e["acts"] = pieces_far(e["acts"])
     fence(e)
+    e["acts"] = rows_near(e["acts"])
+    e["out"] = slab_piece(e["out"])
+    fence(e)
     out = Gather(padded(e.pop("out")), 0)
-    tick([out])
-    e["acts"] = rows_near(e["acts"])
-    e["down"] = slab_piece(e["down"])
-    fence(e)
 
     acts = e["acts"]
     weight_qk = assembled([(qk, 0, 0)], member_rows, 2 * qk_cols)
@@ -653,7 +651,7 @@
     value_gate = dot(acts, weight_vg)
     e = {
         "cot": e["cot"],
-        "down": e["down"],
+        "down": slab_piece(e["down"]),
         "pu": e["pu"],
         "value": value_gate[:, :gate_at].astype(bf16),
     }

time: 1010 us -> 1010 us (level)
  waiting for transfers between devices: 358 us -> 390 us
  starting transfers between devices: 226 us -> 201 us
    ppermute x91, waiting for transfers between devices: 226 us -> 244 us  [ring_step(): lax.ppermute(value, 'grp', [(ring[i], ring[(i + ahead) % count]) for i in...]
    ppermute x32, starting transfers between devices: 32.5 us -> 15.8 us  [swap(): return lax.ppermute(value, 'rep', [(i, i ^ bit) for i in range(count)])]
    ppermute x91, starting transfers between devices: 152 us -> 142 us  [ring_step(): lax.ppermute(value, 'grp', [(ring[i], ring[(i + ahead) % count]) for i in...]
    unnamed x281 -> x279, local copies, waits for them, and re-layouts: 36.7 us -> 35.9 us
  transfers between devices with their start and end apart: 138 -> 138, of which waited for: 54 -> 52; matrix products, arithmetic and copies ran while one was open for 25% -> 24% of each run, Pallas kernels for 5% -> 5%
where the time goes in v4:
time: 1010 us; the launch traced here: 995 us
  waiting for transfers between devices  390 us (39%)
  starting transfers between devices  201 us (20%)
  matrix products  129 us (13%)
  other arithmetic  122 us (12%)
  local copies, waits for them, and re-layouts  85.1 us (8%)
  Pallas kernels  65 us (6%)
    ppermute x91, waiting for transfers between devices, ring_step(): lax.ppermute(value, 'grp', [(ring[i], ring[(i + ahead) % count]) for i in...  244 us
    ppermute x91, starting transfers between devices, ring_step(): lax.ppermute(value, 'grp', [(ring[i], ring[(i + ahead) % count]) for i in...  142 us
    ppermute x32, waiting for transfers between devices, swap(): return lax.ppermute(value, 'rep', [(i, i ^ bit) for i in range(count)])  70.7 us
    dot_general x5, matrix products, dot_t(): lax.dot_general(left, right, (((1,), (1,)), ((), ())), preferred_element_...  50.2 us
    dot_general x5, matrix products, dot(): return jnp.dot(left, right, preferred_element_type=f32)  38.5 us
    dot_general x7, matrix products, t_dot(): lax.dot_general(left, right, (((0,), (0,)), ((), ())), preferred_element_...  37 us
    convert_element_type x22, other arithmetic, next(): return term.astype(bf16)  36.9 us
    unnamed x279, local copies, waits for them, and re-layouts  35.9 us
  transfers between devices with their start and end apart: 138, of which 52 were waited for; matrix products, arithmetic and copies ran while one was open for 24% of the time, Pallas kernels for 5%

profile of v4, /device:TPU:0, one launch (start us, length us, event | category | flops | bytes accessed | tf_op | source)
XLA Modules:
  0.0 994.6 jit_solution(10078090450916091755)
XLA Ops:
  15.9 25.2 %all-to-all-done = bf16[8,2,256]{2,1,0:T(2,128)(2,1)S(1)} async-done(((bf16[8,2,256]{2,1,0:T(2,128)(2,1)}), bf16[8,2,256]{2,1,0:T(2,128)(2,1)S(1)}, u32[]{:S(2)}, u32[]{:S(2)}) %all-to-all-start) | async-done | bytes 8224 | tf_op jit(solution)/shard_map/all_to_all | solution.py:590
  58.3 14.2 %all-to-all-done.1 = bf16[8,32,2048]{2,1,0:T(8,128)(2,1)} async-done(((bf16[8,32,2048]{2,1,0:T(8,128)(2,1)}), bf16[8,32,2048]{2,1,0:T(8,128)(2,1)}, u32[]{:S(2)}, u32[]{:S(2)}) %all-to-all-start.1) | async-done | bytes 1048608 | tf_op jit(solution)/shard_map/all_to_all | solution.py:584
  82.2 9.1 all-to-all-done.2
  95.7 10.8 %collective-permute-done.6.refs_2_ = bf16[256,1024]{1,0:T(8,128)(2,1)S(1)} collective-permute-done((bf16[256,1024]{1,0:T(8,128)(2,1)S(1)}, bf16[256,1024]{1,0:T(8,128)(2,1)S(1)}, u32[]{:S(2)}, u32[]{:S(2)}) %collective-permute-start.6) | collective-permute-done | bytes 524320 | tf_op jit(solution)/shard_map/ppermute | solution.py:130
  116.3 19.7 %collective-permute-done.7.refs_3_ = bf16[256,1024]{1,0:T(8,128)(2,1)S(1)} collective-permute-done((bf16[256,1024]{1,0:T(8,128)(2,1)S(1)}, bf16[256,1024]{1,0:T(8,128)(2,1)S(1)}, u32[]{:S(2)}, u32[]{:S(2)}) %collective-permute-start.7) | collective-permute-done | bytes 524320 | tf_op jit(solution)/shard_map/ppermute | solution.py:130
  139.9 24.7 %collective-permute-done.3 = bf16[256,432]{0,1:T(8,128)(2,1)} collective-permute-done((bf16[256,432]{0,1:T(8,128)(2,1)}, bf16[256,432]{0,1:T(8,128)(2,1)}, u32[]{:S(2)}, u32[]{:S(2)}) %collective-permute-start.3) | collective-permute-done | bytes 221216 | tf_op jit(solution)/shard_map/ppermute | solution.py:488
  214.5 10.9 %collective-permute-done.24 = bf16[256,896]{0,1:T(8,128)(2,1)S(1)} collective-permute-done((bf16[256,896]{0,1:T(8,128)(2,1)S(1)}, bf16[256,896]{0,1:T(8,128)(2,1)S(1)}, u32[]{:S(2)}, u32[]{:S(2)}) %collective-permute-start.24) | collective-permute-done | bytes 458784 | tf_op jit(solution)/shard_map/ppermute | solution.py:130
  327.9 20.3 %collective-permute-done.37 = bf16[256,2048]{1,0:T(8,128)(2,1)S(1)} collective-permute-done((bf16[256,2048]{1,0:T(8,128)(2,1)S(1)}, bf16[256,2048]{1,0:T(8,128)(2,1)S(1)}, u32[]{:S(2)}, u32[]{:S(2)}) %collective-permute-start.37) | collective-permute-done | bytes 1048608 | tf_op jit(solution)/shard_map/ppermute | solution.py:40
  378.4 14.7 %collective-permute-done.43.refs_4_ = bf16[256,896]{1,0:T(8,128)(2,1)S(1)} collective-permute-done((bf16[256,896]{1,0:T(8,128)(2,1)S(1)}, bf16[256,896]{1,0:T(8,128)(2,1)S(1)}, u32[]{:S(2)}, u32[]{:S(2)}) %collective-permute-start.43) | collective-permute-done | bytes 458784 | tf_op jit(solution)/shard_map/ppermute | solution.py:130
  405.9 15.2 %collective-permute-done.47 = bf16[256,2048]{1,0:T(8,128)(2,1)S(1)} collective-permute-done((bf16[256,2048]{1,0:T(8,128)(2,1)S(1)}, bf16[256,2048]{1,0:T(8,128)(2,1)S(1)}, u32[]{:S(2)}, u32[]{:S(2)}) %collective-permute-start.47) | collective-permute-done | bytes 1048608 | tf_op jit(solution)/shard_map/ppermute | solution.py:40
  456.1 12.2 %fusion.6 = (bf16[1024,896]{1,0:T(8,128)(2,1)S(1)}, bf16[1024,896]{1,0:T(8,128)(2,1)S(1)}) fusion(f32[1024,1792]{1,0:T(8,128)} %copy-done.53, bf16[1024,2048]{1,0:T(8,128)(2,1)} %copy-done.112, bf16[2048,896]{1,0:T(8,128)(2,1)S(1)} %shard_map.234), kind=kOutput, calls=%fused_computation.13 | convolution fusion | flops 3780116480 | bytes 18874368 | tf_op jit(solution)/shard_map/dot_general | solution.py:27
  468.4 10.0 %fusion.54 = (bf16[1024,2048]{1,0:T(8,128)(2,1)S(1)}, f32[1024,2048]{1,0:T(8,128)}) fusion(bf16[2048,1792]{1,0:T(8,128)(2,1)S(1)} %bitcast.111, bf16[1024,896]{1,0:T(8,128)(2,1)S(1)} %get-tuple-element.465, bf16[1024,896]{1,0:T(8,128)(2,1)S(1)} %get-tuple-element.464), kind=kOutput, calls=%fused_computation.218 | convolution fusion | flops 7525629952 | bytes 23592960 | tf_op jit(solution)/shard_map/dot_general | solution.py:31
  534.1 8.8 collective-permute-done.63
  554.1 10.4 %collective-permute-done.71 = bf16[256,896]{1,0:T(8,128)(2,1)} collective-permute-done((bf16[256,896]{1,0:T(8,128)(2,1)}, bf16[256,896]{1,0:T(8,128)(2,1)}, u32[]{:S(2)}, u32[]{:S(2)}) %collective-permute-start.71) | collective-permute-done | bytes 458784 | tf_op jit(solution)/shard_map/ppermute | solution.py:130
  610.7 22.9 %shard_map.235 = (bf16[1024,512]{1,0:T(8,128)(2,1)}, bf16[1024,896]{1,0:T(8,128)(2,1)}, bf16[1024,512]{1,0:T(8,128)(2,1)}, bf16[1024,896]{1,0:T(8,128)(2,1)}) custom-call(bf16[1024,512]{1,0:T(8,128)(2,1)} %copy-done.3, bf16[1024,512]{1,0:T(8,128)(2,1)} %copy-done.2, bf16[1024,896]{1,0:T(8,128)(2,1)} %slice.286.v_ref, f32[1024,1792]{1,0:T(8,128)} %copy-done.51, ...), custom_call_target="tpu_custom_call" | custom-call | flops 7583301632 | bytes 18874368 | tf_op jit(solution)/shard_map/pallas_call | solution.py:422
  681.2 13.3 %fusion.7 = f32[1024,2048]{1,0:T(8,128)} fusion(bf16[2048,1792]{1,0:T(8,128)(2,1)} %copy-done, bf16[1024,896]{1,0:T(8,128)(2,1)} %get-tuple-element.350, bf16[1024,896]{1,0:T(8,128)(2,1)} %get-tuple-element.337), kind=kOutput, calls=%fused_computation.16 | convolution fusion | flops 7523532800 | bytes 19398656 | tf_op jit(solution)/shard_map/dot_general | solution.py:31
  720.1 13.4 %fusion.56 = (bf16[1024,2048]{1,0:T(8,128)(2,1)S(1)}, f32[1024,2048]{1,0:T(8,128)}) fusion(f32[1024,2048]{1,0:T(8,128)} %fusion.7, bf16[1024,1024]{1,0:T(8,128)(2,1)} %pad_maximum_fusion.7, bf16[2048,1024]{1,0:T(8,128)(2,1)} %copy-done.4), kind=kOutput, calls=%fused_computation.220 | convolution fusion | flops 4299161600 | bytes 27262976 | tf_op jit(solution)/shard_map/dot_general | solution.py:31
  741.4 9.0 collective-permute-done.95
  774.4 14.4 %collective-permute-done.96 = bf16[256,896]{1,0:T(8,128)(2,1)S(1)} collective-permute-done((bf16[256,896]{1,0:T(8,128)(2,1)S(1)}, bf16[256,896]{1,0:T(8,128)(2,1)S(1)}, u32[]{:S(2)}, u32[]{:S(2)}) %collective-permute-start.96) | collective-permute-done | bytes 458784 | tf_op jit(solution)/shard_map/ppermute | solution.py:130
  811.6 16.8 %collective-permute-done.109 = bf16[256,896]{0,1:T(8,128)(2,1)} collective-permute-done((bf16[256,896]{0,1:T(8,128)(2,1)}, bf16[256,896]{0,1:T(8,128)(2,1)}, u32[]{:S(2)}, u32[]{:S(2)}) %collective-permute-start.109) | collective-permute-done | bytes 458784 | tf_op jit(solution)/shard_map/ppermute | solution.py:130
  852.0 9.5 collective-permute-done.100
  899.2 12.9 %collective-permute-done.121 = bf16[256,896]{1,0:T(8,128)(2,1)S(1)} collective-permute-done((bf16[256,896]{1,0:T(8,128)(2,1)S(1)}, bf16[256,896]{1,0:T(8,128)(2,1)S(1)}, u32[]{:S(2)}, u32[]{:S(2)}) %collective-permute-start.121) | collective-permute-done | bytes 458784 | tf_op jit(solution)/shard_map/ppermute | solution.py:130
  913.2 17.1 %collective-permute-start.120 = (bf16[256,896]{1,0:T(8,128)(2,1)}, bf16[256,896]{1,0:T(8,128)(2,1)S(1)}, u32[]{:S(2)}, u32[]{:S(2)}) collective-permute-start(bf16[256,896]{1,0:T(8,128)(2,1)} %get-tuple-element.396), channel_id=1, source_target_pairs={{0,2},{2,4},{4,6},{6,7},{7,5},{5,3},{3,1},{1,0},{8,10},{10,12},{12... | collective-permute-start | bytes 1376264 | tf_op jit(solution)/shard_map/ppermute | solution.py:130
  960.4 12.0 %collective-permute-done.126.refs_2_ = bf16[256,1920]{1,0:T(8,128)(2,1)} collective-permute-done((bf16[256,1920]{1,0:T(8,128)(2,1)S(1)}, bf16[256,1920]{1,0:T(8,128)(2,1)}, u32[]{:S(2)}, u32[]{:S(2)}) %collective-permute-start.126) | collective-permute-done | bytes 983072 | tf_op jit(solution)/shard_map/ppermute | solution.py:40
  (713 shorter events, 643.9 us)
Async XLA Ops:
  1.8 89.8 %collective-permute-start.5 = (bf16[256,1024]{1,0:T(8,128)(2,1)S(1)}, bf16[256,1024]{1,0:T(8,128)(2,1)S(1)}, u32[]{:S(2)}, u32[]{:S(2)}) collective-permute-start(bf16[256,1024]{1,0:T(8,128)(2,1)S(1)} %pad_maximum_fusion.14.refs_0_), channel_id=1, source_target_pairs={{0,1},{2,0},{4,2},{6,4},{7,6},{5,7},{3,5},{1,3},{8,9},{10,8},{12,1... | collective-permute-start | bytes 1572872 | tf_op jit(solution)/shard_map/ppermute | solution.py:130
  4.8 51.4 %collective-permute-start.8 = (bf16[256,1024]{1,0:T(8,128)(2,1)S(1)}, bf16[256,1024]{1,0:T(8,128)(2,1)}, u32[]{:S(2)}, u32[]{:S(2)}) collective-permute-start(bf16[256,1024]{1,0:T(8,128)(2,1)S(1)} %pad_maximum_fusion.14.refs_0_), channel_id=1, source_target_pairs={{0,2},{2,4},{4,6},{6,7},{7,5},{5,3},{3,1},{1,0},{8,10},{10,12},{12... | collective-permute-start | bytes 1572872 | tf_op jit(solution)/shard_map/ppermute | solution.py:130
  6.8 86.8 %collective-permute-start.12 = (bf16[256,1792]{1,0:T(8,128)(2,1)S(1)}, bf16[256,1792]{1,0:T(8,128)(2,1)S(1)}, u32[]{:S(2)}, u32[]{:S(2)}) collective-permute-start(bf16[256,1792]{1,0:T(8,128)(2,1)S(1)} %fusion.33.refs_0_), channel_id=1, source_target_pairs={{0,2},{2,4},{4,6},{6,7},{7,5},{5,3},{3,1},{1,0},{8,10},{10,12},{12... | collective-permute-start | bytes 2752520 | tf_op jit(solution)/shard_map/ppermute | solution.py:130
  8.9 49.3 %collective-permute-start.15 = (bf16[256,1792]{1,0:T(8,128)(2,1)S(1)}, bf16[256,1792]{1,0:T(8,128)(2,1)}, u32[]{:S(2)}, u32[]{:S(2)}) collective-permute-start(bf16[256,1792]{1,0:T(8,128)(2,1)S(1)} %fusion.33.refs_0_), channel_id=1, source_target_pairs={{0,1},{2,0},{4,2},{6,4},{7,6},{5,7},{3,5},{1,3},{8,9},{10,8},{12,1... | collective-permute-start | bytes 2752520 | tf_op jit(solution)/shard_map/ppermute | solution.py:130
  93.6 43.1 %collective-permute-start.13 = (bf16[256,1792]{1,0:T(8,128)(2,1)S(1)}, bf16[256,1792]{1,0:T(8,128)(2,1)}, u32[]{:S(2)}, u32[]{:S(2)}) collective-permute-start(bf16[256,1792]{1,0:T(8,128)(2,1)S(1)} %collective-permute-done.12.refs_7_), channel_id=1, source_target_pairs={{0,2},{2,4},{4,6},{6,7},{7,5},{5,3},{3,1},{1,0},{8,10},{10,12},{12... | collective-permute-start | bytes 2752520 | tf_op jit(solution)/shard_map/ppermute | solution.py:130
  93.7 43.1 %collective-permute-start.17 = (bf16[256,1792]{1,0:T(8,128)(2,1)}, bf16[256,1792]{1,0:T(8,128)(2,1)}, u32[]{:S(2)}, u32[]{:S(2)}) collective-permute-start(bf16[256,1792]{1,0:T(8,128)(2,1)} %collective-permute-done.16.refs_2_), channel_id=1, source_target_pairs={{0,1},{2,0},{4,2},{6,4},{7,6},{5,7},{3,5},{1,3},{8,9},{10,8},{12,1... | collective-permute-start | bytes 2752520 | tf_op jit(solution)/shard_map/ppermute | solution.py:130
  116.3 63.9 %collective-permute-start.2 = (bf16[256,2048]{1,0:T(8,128)(2,1)}, bf16[256,2048]{1,0:T(8,128)(2,1)}, u32[]{:S(2)}, u32[]{:S(2)}) collective-permute-start(bf16[256,2048]{1,0:T(8,128)(2,1)} %collective-permute-done), channel_id=1, source_target_pairs={{0,8},{8,0},{16,24},{24,16},{1,9},{9,1},{17,25},{25,17},{2,10},{10... | collective-permute-start | bytes 3145736 | tf_op jit(solution)/shard_map/ppermute | solution.py:40
  136.8 43.5 %collective-permute-start.1 = (bf16[256,2048]{1,0:T(8,128)(2,1)}, bf16[256,2048]{1,0:T(8,128)(2,1)}, u32[]{:S(2)}, u32[]{:S(2)}) collective-permute-start(bf16[256,2048]{1,0:T(8,128)(2,1)} %fusion.25), channel_id=1, source_target_pairs={{0,8},{8,0},{16,24},{24,16},{1,9},{9,1},{17,25},{25,17},{2,10},{10... | collective-permute-start | bytes 3145736 | tf_op jit(solution)/shard_map/ppermute | solution.py:40
  317.1 42.9 %all-to-all-start.3 = ((bf16[8,32,2048]{2,1,0:T(8,128)(2,1)}), bf16[8,32,2048]{2,1,0:T(8,128)(2,1)}, u32[]{:S(2)}, u32[]{:S(2)}) async-start(bf16[8,32,2048]{2,1,0:T(8,128)(2,1)} %bitcast.22), calls=%async_computation.3 | async-start | bytes 2097152 | tf_op jit(solution)/shard_map/all_to_all | solution.py:682
  550.0 43.0 %collective-permute-start.68 = (bf16[512,2048]{1,0:T(8,128)(2,1)S(1)}, bf16[512,2048]{1,0:T(8,128)(2,1)}, u32[]{:S(2)}, u32[]{:S(2)}) collective-permute-start(bf16[512,2048]{1,0:T(8,128)(2,1)S(1)} %pad_maximum_fusion.6), channel_id=1, source_target_pairs={{0,8},{8,0},{16,24},{24,16},{1,9},{9,1},{17,25},{25,17},{2,10},{10... | collective-permute-start | bytes 6291464 | tf_op jit(solution)/shard_map/ppermute | solution.py:40
  586.6 60.6 %collective-permute-start.83 = (bf16[256,896]{1,0:T(8,128)(2,1)}, bf16[256,896]{1,0:T(8,128)(2,1)}, u32[]{:S(2)}, u32[]{:S(2)}) collective-permute-start(bf16[256,896]{1,0:T(8,128)(2,1)} %get-tuple-element.341), channel_id=1, source_target_pairs={{0,2},{2,4},{4,6},{6,7},{7,5},{5,3},{3,1},{1,0},{8,10},{10,12},{12... | collective-permute-start | bytes 1376264 | tf_op jit(solution)/shard_map/ppermute | solution.py:130
  590.4 60.3 %collective-permute-start.82 = (bf16[256,896]{1,0:T(8,128)(2,1)}, bf16[256,896]{1,0:T(8,128)(2,1)}, u32[]{:S(2)}, u32[]{:S(2)}) collective-permute-start(bf16[256,896]{1,0:T(8,128)(2,1)} %get-tuple-element.340), channel_id=1, source_target_pairs={{0,1},{2,0},{4,2},{6,4},{7,6},{5,7},{3,5},{1,3},{8,9},{10,8},{12,1... | collective-permute-start | bytes 1376264 | tf_op jit(solution)/shard_map/ppermute | solution.py:130
  604.0 40.5 %collective-permute-start.74 = (bf16[256,896]{0,1:T(8,128)(2,1)}, bf16[256,896]{0,1:T(8,128)(2,1)S(1)}, u32[]{:S(2)}, u32[]{:S(2)}) collective-permute-start(bf16[256,896]{0,1:T(8,128)(2,1)} %add_convert_fusion.40), channel_id=1, source_target_pairs={{0,2},{2,4},{4,6},{6,7},{7,5},{5,3},{3,1},{1,0},{8,10},{10,12},{12... | collective-permute-start | bytes 1376264 | tf_op jit(solution)/shard_map/ppermute | solution.py:130
  608.5 62.0 %collective-permute-start.78 = (bf16[256,2048]{1,0:T(8,128)(2,1)}, bf16[256,2048]{1,0:T(8,128)(2,1)}, u32[]{:S(2)}, u32[]{:S(2)}) collective-permute-start(bf16[256,2048]{1,0:T(8,128)(2,1)} %fusion.16), channel_id=1, source_target_pairs={{0,16},{8,24},{16,0},{24,8},{1,17},{9,25},{17,1},{25,9},{2,18},{10... | collective-permute-start | bytes 3145736 | tf_op jit(solution)/shard_map/ppermute | solution.py:40
  647.2 64.0 %collective-permute-start.86 = (bf16[256,896]{1,0:T(8,128)(2,1)}, bf16[256,896]{1,0:T(8,128)(2,1)}, u32[]{:S(2)}, u32[]{:S(2)}) collective-permute-start(bf16[256,896]{1,0:T(8,128)(2,1)} %get-tuple-element.344), channel_id=1, source_target_pairs={{0,2},{2,4},{4,6},{6,7},{7,5},{5,3},{3,1},{1,0},{8,10},{10,12},{12... | collective-permute-start | bytes 1376264 | tf_op jit(solution)/shard_map/ppermute | solution.py:130
  648.4 62.9 %collective-permute-start.87 = (bf16[256,896]{1,0:T(8,128)(2,1)}, bf16[256,896]{1,0:T(8,128)(2,1)}, u32[]{:S(2)}, u32[]{:S(2)}) collective-permute-start(bf16[256,896]{1,0:T(8,128)(2,1)} %get-tuple-element.345), channel_id=1, source_target_pairs={{0,1},{2,0},{4,2},{6,4},{7,6},{5,7},{3,5},{1,3},{8,9},{10,8},{12,1... | collective-permute-start | bytes 1376264 | tf_op jit(solution)/shard_map/ppermute | solution.py:130
  650.8 60.5 %collective-permute-start.88 = (bf16[256,896]{0,1:T(8,128)(2,1)}, bf16[256,896]{0,1:T(8,128)(2,1)}, u32[]{:S(2)}, u32[]{:S(2)}) collective-permute-start(bf16[256,896]{0,1:T(8,128)(2,1)} %get-tuple-element.346), channel_id=1, source_target_pairs={{0,2},{2,4},{4,6},{6,7},{7,5},{5,3},{3,1},{1,0},{8,10},{10,12},{12... | collective-permute-start | bytes 1376264 | tf_op jit(solution)/shard_map/ppermute | solution.py:130
  676.6 43.5 %all-to-all-start.4 = ((bf16[8,32,2048]{2,1,0:T(8,128)(2,1)}), bf16[8,32,2048]{2,1,0:T(8,128)(2,1)S(1)}, u32[]{:S(2)}, u32[]{:S(2)}) async-start(bf16[8,32,2048]{2,1,0:T(8,128)(2,1)} %bitcast.26), calls=%async_computation.4 | async-start | bytes 2097152 | tf_op jit(solution)/shard_map/all_to_all | solution.py:763
  735.2 64.0 %collective-permute-start.90 = (bf16[512,2048]{1,0:T(8,128)(2,1)}, bf16[512,2048]{1,0:T(8,128)(2,1)}, u32[]{:S(2)}, u32[]{:S(2)}) collective-permute-start(bf16[512,2048]{1,0:T(8,128)(2,1)} %pad_maximum_fusion.8), channel_id=1, source_target_pairs={{0,8},{8,0},{16,24},{24,16},{1,9},{9,1},{17,25},{25,17},{2,10},{10... | collective-permute-start | bytes 6291464 | tf_op jit(solution)/shard_map/ppermute | solution.py:40
  755.5 43.8 %all-to-all-start.5 = ((bf16[2,4,32,2048]{3,2,0,1:T(8,128)(2,1)}), bf16[2,4,32,2048]{3,2,0,1:T(8,128)(2,1)S(1)}, u32[]{:S(2)}, u32[]{:S(2)}) async-start(bf16[2,4,32,2048]{3,2,0,1:T(8,128)(2,1)} %copy.174), calls=%async_computation.5 | async-start | bytes 2097152 | tf_op jit(solution)/shard_map/all_to_all | solution.py:784
  866.4 63.9 %all-to-all-start.6 = ((bf16[8,32,2048]{2,1,0:T(8,128)(2,1)}), bf16[8,32,2048]{2,1,0:T(8,128)(2,1)}, u32[]{:S(2)}, u32[]{:S(2)}) async-start(bf16[8,32,2048]{2,1,0:T(8,128)(2,1)} %bitcast.32), calls=%async_computation.6 | async-start | bytes 2097152 | tf_op jit(solution)/shard_map/all_to_all | solution.py:799
  872.6 57.7 %collective-permute-start.102 = (bf16[256,896]{1,0:T(8,128)(2,1)S(1)}, bf16[256,896]{1,0:T(8,128)(2,1)}, u32[]{:S(2)}, u32[]{:S(2)}) collective-permute-start(bf16[256,896]{1,0:T(8,128)(2,1)S(1)} %add_convert_fusion.16.refs_0_), channel_id=1, source_target_pairs={{0,16},{8,24},{16,0},{24,8},{1,17},{9,25},{17,1},{25,9},{2,18},{10... | collective-permute-start | bytes 1376264 | tf_op jit(solution)/shard_map/ppermute | solution.py:40
  886.1 44.4 %collective-permute-start.123 = (bf16[256,1024]{1,0:T(8,128)(2,1)}, bf16[256,1024]{1,0:T(8,128)(2,1)}, u32[]{:S(2)}, u32[]{:S(2)}) collective-permute-start(bf16[256,1024]{1,0:T(8,128)(2,1)} %get-tuple-element.399), channel_id=1, source_target_pairs={{0,2},{2,4},{4,6},{6,7},{7,5},{5,3},{3,1},{1,0},{8,10},{10,12},{12... | collective-permute-start | bytes 1572872 | tf_op jit(solution)/shard_map/ppermute | solution.py:130
  893.6 49.7 %collective-permute-start.125 = (bf16[256,1024]{1,0:T(8,128)(2,1)}, bf16[256,1024]{1,0:T(8,128)(2,1)S(1)}, u32[]{:S(2)}, u32[]{:S(2)}) collective-permute-start(bf16[256,1024]{1,0:T(8,128)(2,1)} %get-tuple-element.401), channel_id=1, source_target_pairs={{0,1},{2,0},{4,2},{6,4},{7,6},{5,7},{3,5},{1,3},{8,9},{10,8},{12,1... | collective-permute-start | bytes 1572872 | tf_op jit(solution)/shard_map/ppermute | solution.py:130
  (250 other events, 4961.5 us)

commit v5 on v4

--- a/solution.py
+++ b/solution.py
@@ -755,10 +755,11 @@
     tick(ring_og)
     ff = [ring.whole() for ring in ring_ff]
     ring_v = Scatter(acts, value_grad, 1)
+    tick([ring_v])
     ring_qk = Scatter(acts, qk_grad, 0)
     e = {
         "qk": qk_grad,
-        "full": [ring_v.full, ring_qk.full],
+        "full": ring_qk.full,
         "pu": pieces_far(jnp.concatenate(ff[:2], axis=1)),
         "rows": lax.all_to_all(
             out_rows.astype(bf16).reshape(members, strip, width),
@@ -771,7 +772,7 @@
     }
     fence(e, rings=ring_og)
     qk_grad, pu_far = e["qk"], e["pu"]
-    ring_v.full, ring_qk.full = e["full"]
+    ring_qk.full = e["full"]
     out_seqs = e["rows"].reshape(micro, seqs, strip, width)
     out_bins = jnp.einsum("msk,msrd->mkrd", selector, out_seqs, preferred_element_type=f32)
 
@@ -796,47 +797,47 @@
     input_grad = hidden_grad + norm_pullback(e["sum"])[0]
     tick([ring_v, ring_qk])
     e = {
-        "rows": lax.all_to_all(
-            input_grad.astype(bf16).reshape(members, strip, width),
-            "grp",
-            split_axis=0,
-            concat_axis=0,
-            tiled=True,
-        ),
+        "rows": input_grad.astype(bf16).reshape(members, strip, width),
         "gate": pieces_far(gate_part),
         "slabs": jnp.concatenate([e["down"], out_mine], axis=1),
         "pu": e["pu"],
     }
     fence(e, rings=[ring_v, ring_qk])
-    token_grad = e["rows"].reshape(tokens.shape)
-
-    tick([ring_v, ring_qk])
+    rows_out = e["rows"]
+
+    tick([ring_qk])
     proj_owned, up_owned, gain_two_owned = finished(
         e["pu"], ((0, hid_cols), (hid, hid_cols)), mlp_gain, (w_proj, w_up)
     )
     e = {
         "gate": pieces_near(e["gate"]),
         "slabs": pieces_far(e["slabs"]),
+        "value": pieces_far(ring_v.whole()),
+        "rows": rows_out,
         "gain": gain_two_owned,
     }
-    fence(e, done=[ring_v, ring_qk])
+    fence(e, done=[ring_qk])
     gain_two_owned = e["gain"]
     gate_owned, gate_sum = finished(e["gate"], ((0, val_cols),), norm_gain, (w_gate,))
     e = {
         "slabs": pieces_near(e["slabs"]),
-        "last": pieces_far(jnp.concatenate([ring_qk.whole(), ring_v.whole()], axis=1)),
+        "value": pieces_near(e["value"]),
+        "last": pieces_far(ring_qk.whole()),
+        "rows": lax.all_to_all(e["rows"], "grp", split_axis=0, concat_axis=0, tiled=True),
         "gain": gate_sum,
     }
     fence(e)
+    token_grad = e["rows"].reshape(tokens.shape)
     size = width // reps
     down_owned, out_owned = finished(e["slabs"], ((0, size), (size, size)))
-    query_owned, key_owned, value_owned, rest_sum = finished(
+    value_owned, value_sum = finished(e["value"], ((0, val_cols),), norm_gain, (w_value,))
+    query_owned, key_owned, rest_sum = finished(
         pieces_near(e["last"]),
-        ((0, qk_cols), (qk_cols, qk_cols), (2 * qk_cols, val_cols)),
+        ((0, qk_cols), (qk_cols, qk_cols)),
         norm_gain,
-        (w_query, w_key, w_value),
-    )
-    gain_one_owned = (e["gain"] + rest_sum)[:, 0]
+        (w_query, w_key),
+    )
+    gain_one_owned = (e["gain"] + value_sum + rest_sum)[:, 0]
     gain_two_owned = gain_two_owned[:, 0]
     return (
         bin_out,

time: 1010 us -> 997 us (0.987)
  local copies, waits for them, and re-layouts: 85.1 us -> 95.5 us
    ppermute x91, waiting for transfers between devices: 244 us -> 228 us  [ring_step(): lax.ppermute(value, 'grp', [(ring[i], ring[(i + ahead) % count]) for i in...]
    ppermute x91, starting transfers between devices: 142 us -> 128 us  [ring_step(): lax.ppermute(value, 'grp', [(ring[i], ring[(i + ahead) % count]) for i in...]
    unnamed x279 -> x281, local copies, waits for them, and re-layouts: 35.9 us -> 47.1 us
    ppermute x32 -> x35, waiting for transfers between devices: 70.7 us -> 69.6 us  [swap(): return lax.ppermute(value, 'rep', [(i, i ^ bit) for i in range(count)])]
  transfers between devices with their start and end apart: 138 -> 141, of which waited for: 52 -> 52; matrix products, arithmetic and copies ran while one was open for 24% -> 26% of each run, Pallas kernels for 5% -> 5%
where the time goes in v5:
time: 997 us; the launch traced here: 985 us
  waiting for transfers between devices  380 us (38%)
  starting transfers between devices  193 us (19%)
  matrix products  128 us (13%)
  other arithmetic  121 us (12%)
  local copies, waits for them, and re-layouts  95.5 us (10%)
  Pallas kernels  64 us (6%)
    ppermute x91, waiting for transfers between devices, ring_step(): lax.ppermute(value, 'grp', [(ring[i], ring[(i + ahead) % count]) for i in...  228 us
    ppermute x91, starting transfers between devices, ring_step(): lax.ppermute(value, 'grp', [(ring[i], ring[(i + ahead) % count]) for i in...  128 us
    ppermute x35, waiting for transfers between devices, swap(): return lax.ppermute(value, 'rep', [(i, i ^ bit) for i in range(count)])  69.6 us
    dot_general x5, matrix products, dot_t(): lax.dot_general(left, right, (((1,), (1,)), ((), ())), preferred_element_...  50.2 us
    unnamed x281, local copies, waits for them, and re-layouts  47.1 us
    dot_general x5, matrix products, dot(): return jnp.dot(left, right, preferred_element_type=f32)  38.5 us
    convert_element_type x22, other arithmetic, next(): return term.astype(bf16)  37.9 us
    dot_general x7, matrix products, t_dot(): lax.dot_general(left, right, (((0,), (0,)), ((), ())), preferred_element_...  35.8 us
  transfers between devices with their start and end apart: 141, of which 52 were waited for; matrix products, arithmetic and copies ran while one was open for 26% of the time, Pallas kernels for 5%

profile of v5, /device:TPU:0, one launch (start us, length us, event | category | flops | bytes accessed | tf_op | source)
XLA Modules:
  0.0 984.7 jit_solution(8229552320245437710)
XLA Ops:
  15.9 25.2 %all-to-all-done = bf16[8,2,256]{2,1,0:T(2,128)(2,1)S(1)} async-done(((bf16[8,2,256]{2,1,0:T(2,128)(2,1)}), bf16[8,2,256]{2,1,0:T(2,128)(2,1)S(1)}, u32[]{:S(2)}, u32[]{:S(2)}) %all-to-all-start) | async-done | bytes 8224 | tf_op jit(solution)/shard_map/all_to_all | solution.py:590
  58.0 14.4 %all-to-all-done.1 = bf16[8,32,2048]{2,1,0:T(8,128)(2,1)} async-done(((bf16[8,32,2048]{2,1,0:T(8,128)(2,1)}), bf16[8,32,2048]{2,1,0:T(8,128)(2,1)}, u32[]{:S(2)}, u32[]{:S(2)}) %all-to-all-start.1) | async-done | bytes 1048608 | tf_op jit(solution)/shard_map/all_to_all | solution.py:584
  81.4 9.8 all-to-all-done.2
  95.6 10.8 %collective-permute-done.6.refs_2_ = bf16[256,1024]{1,0:T(8,128)(2,1)S(1)} collective-permute-done((bf16[256,1024]{1,0:T(8,128)(2,1)S(1)}, bf16[256,1024]{1,0:T(8,128)(2,1)S(1)}, u32[]{:S(2)}, u32[]{:S(2)}) %collective-permute-start.6) | collective-permute-done | bytes 524320 | tf_op jit(solution)/shard_map/ppermute | solution.py:130
  116.2 19.7 %collective-permute-done.7.refs_3_ = bf16[256,1024]{1,0:T(8,128)(2,1)S(1)} collective-permute-done((bf16[256,1024]{1,0:T(8,128)(2,1)S(1)}, bf16[256,1024]{1,0:T(8,128)(2,1)S(1)}, u32[]{:S(2)}, u32[]{:S(2)}) %collective-permute-start.7) | collective-permute-done | bytes 524320 | tf_op jit(solution)/shard_map/ppermute | solution.py:130
  139.8 24.7 %collective-permute-done.3 = bf16[256,432]{0,1:T(8,128)(2,1)} collective-permute-done((bf16[256,432]{0,1:T(8,128)(2,1)}, bf16[256,432]{0,1:T(8,128)(2,1)}, u32[]{:S(2)}, u32[]{:S(2)}) %collective-permute-start.3) | collective-permute-done | bytes 221216 | tf_op jit(solution)/shard_map/ppermute | solution.py:488
  214.6 10.6 %collective-permute-done.24 = bf16[256,896]{0,1:T(8,128)(2,1)S(1)} collective-permute-done((bf16[256,896]{0,1:T(8,128)(2,1)S(1)}, bf16[256,896]{0,1:T(8,128)(2,1)S(1)}, u32[]{:S(2)}, u32[]{:S(2)}) %collective-permute-start.24) | collective-permute-done | bytes 458784 | tf_op jit(solution)/shard_map/ppermute | solution.py:130
  225.2 8.9 collective-permute-start.25
  258.7 8.6 shard_map.231
  327.8 20.3 %collective-permute-done.37 = bf16[256,2048]{1,0:T(8,128)(2,1)S(1)} collective-permute-done((bf16[256,2048]{1,0:T(8,128)(2,1)S(1)}, bf16[256,2048]{1,0:T(8,128)(2,1)S(1)}, u32[]{:S(2)}, u32[]{:S(2)}) %collective-permute-start.37) | collective-permute-done | bytes 1048608 | tf_op jit(solution)/shard_map/ppermute | solution.py:40
  378.3 14.7 %collective-permute-done.43.refs_4_ = bf16[256,896]{1,0:T(8,128)(2,1)S(1)} collective-permute-done((bf16[256,896]{1,0:T(8,128)(2,1)S(1)}, bf16[256,896]{1,0:T(8,128)(2,1)S(1)}, u32[]{:S(2)}, u32[]{:S(2)}) %collective-permute-start.43) | collective-permute-done | bytes 458784 | tf_op jit(solution)/shard_map/ppermute | solution.py:130
  405.8 15.2 %collective-permute-done.47 = bf16[256,2048]{1,0:T(8,128)(2,1)S(1)} collective-permute-done((bf16[256,2048]{1,0:T(8,128)(2,1)S(1)}, bf16[256,2048]{1,0:T(8,128)(2,1)S(1)}, u32[]{:S(2)}, u32[]{:S(2)}) %collective-permute-start.47) | collective-permute-done | bytes 1048608 | tf_op jit(solution)/shard_map/ppermute | solution.py:40
  456.5 12.2 %fusion.6 = (bf16[1024,896]{1,0:T(8,128)(2,1)S(1)}, bf16[1024,896]{1,0:T(8,128)(2,1)S(1)}) fusion(f32[1024,1792]{1,0:T(8,128)} %copy-done.65, bf16[1024,2048]{1,0:T(8,128)(2,1)} %copy-done.115, bf16[2048,896]{1,0:T(8,128)(2,1)S(1)} %shard_map.234), kind=kOutput, calls=%fused_computation.13 | convolution fusion | flops 3780116480 | bytes 18874368 | tf_op jit(solution)/shard_map/dot_general | solution.py:27
  468.8 10.0 %fusion.54 = (bf16[1024,2048]{1,0:T(8,128)(2,1)S(1)}, f32[1024,2048]{1,0:T(8,128)}) fusion(bf16[2048,1792]{1,0:T(8,128)(2,1)S(1)} %bitcast.111, bf16[1024,896]{1,0:T(8,128)(2,1)S(1)} %get-tuple-element.481, bf16[1024,896]{1,0:T(8,128)(2,1)S(1)} %get-tuple-element.480), kind=kOutput, calls=%fused_computation.217 | convolution fusion | flops 7525629952 | bytes 23592960 | tf_op jit(solution)/shard_map/dot_general | solution.py:31
  534.5 8.8 collective-permute-done.63
  554.6 10.3 %collective-permute-done.71 = bf16[256,896]{1,0:T(8,128)(2,1)} collective-permute-done((bf16[256,896]{1,0:T(8,128)(2,1)}, bf16[256,896]{1,0:T(8,128)(2,1)}, u32[]{:S(2)}, u32[]{:S(2)}) %collective-permute-start.71) | collective-permute-done | bytes 458784 | tf_op jit(solution)/shard_map/ppermute | solution.py:130
  611.2 22.7 %shard_map.235 = (bf16[1024,512]{1,0:T(8,128)(2,1)}, bf16[1024,896]{1,0:T(8,128)(2,1)}, bf16[1024,512]{1,0:T(8,128)(2,1)}, bf16[1024,896]{1,0:T(8,128)(2,1)}) custom-call(bf16[1024,512]{1,0:T(8,128)(2,1)} %copy-done.3, bf16[1024,512]{1,0:T(8,128)(2,1)} %copy-done.2, bf16[1024,896]{1,0:T(8,128)(2,1)} %slice.286.v_ref, f32[1024,1792]{1,0:T(8,128)} %copy-done.63, ...), custom_call_target="tpu_custom_call" | custom-call | flops 7583301632 | bytes 18874368 | tf_op jit(solution)/shard_map/pallas_call | solution.py:422
  693.3 13.1 %fusion.7 = f32[1024,2048]{1,0:T(8,128)} fusion(bf16[2048,1792]{1,0:T(8,128)(2,1)} %copy-done, bf16[1024,896]{1,0:T(8,128)(2,1)} %get-tuple-element.358, bf16[1024,896]{1,0:T(8,128)(2,1)} %get-tuple-element.357), kind=kOutput, calls=%fused_computation.16 | convolution fusion | flops 7523532800 | bytes 19398656 | tf_op jit(solution)/shard_map/dot_general | solution.py:31
  736.2 13.4 %fusion.56 = (bf16[1024,2048]{1,0:T(8,128)(2,1)S(1)}, f32[1024,2048]{1,0:T(8,128)}) fusion(f32[1024,2048]{1,0:T(8,128)} %fusion.7, bf16[1024,1024]{1,0:T(8,128)(2,1)} %pad_maximum_fusion.7, bf16[2048,1024]{1,0:T(8,128)(2,1)} %copy-done.4), kind=kOutput, calls=%fused_computation.219 | convolution fusion | flops 4299161600 | bytes 27262976 | tf_op jit(solution)/shard_map/dot_general | solution.py:31
  782.0 9.4 collective-permute-done.99
  822.2 15.7 %collective-permute-done.110 = bf16[256,896]{0,1:T(8,128)(2,1)} collective-permute-done((bf16[256,896]{0,1:T(8,128)(2,1)}, bf16[256,896]{0,1:T(8,128)(2,1)}, u32[]{:S(2)}, u32[]{:S(2)}) %collective-permute-start.110) | collective-permute-done | bytes 458784 | tf_op jit(solution)/shard_map/ppermute | solution.py:130
  859.7 12.2 %collective-permute-start.121 = (bf16[256,896]{1,0:T(8,128)(2,1)S(1)}, bf16[256,896]{1,0:T(8,128)(2,1)S(1)}, u32[]{:S(2)}, u32[]{:S(2)}) collective-permute-start(bf16[256,896]{1,0:T(8,128)(2,1)S(1)} %get-tuple-element.404), channel_id=1, source_target_pairs={{0,2},{2,4},{4,6},{6,7},{7,5},{5,3},{3,1},{1,0},{8,10},{10,12},{12... | collective-permute-start | bytes 1376264 | tf_op jit(solution)/shard_map/ppermute | solution.py:130
  917.6 9.8 collective-permute-done.123.refs_2_
  951.2 8.4 all-to-all-done.6
  (721 shorter events, 652.5 us)
Async XLA Ops:
  1.8 89.8 %collective-permute-start.5 = (bf16[256,1024]{1,0:T(8,128)(2,1)S(1)}, bf16[256,1024]{1,0:T(8,128)(2,1)S(1)}, u32[]{:S(2)}, u32[]{:S(2)}) collective-permute-start(bf16[256,1024]{1,0:T(8,128)(2,1)S(1)} %pad_maximum_fusion.13.refs_0_), channel_id=1, source_target_pairs={{0,1},{2,0},{4,2},{6,4},{7,6},{5,7},{3,5},{1,3},{8,9},{10,8},{12,1... | collective-permute-start | bytes 1572872 | tf_op jit(solution)/shard_map/ppermute | solution.py:130
  4.8 51.1 %collective-permute-start.8 = (bf16[256,1024]{1,0:T(8,128)(2,1)S(1)}, bf16[256,1024]{1,0:T(8,128)(2,1)}, u32[]{:S(2)}, u32[]{:S(2)}) collective-permute-start(bf16[256,1024]{1,0:T(8,128)(2,1)S(1)} %pad_maximum_fusion.13.refs_0_), channel_id=1, source_target_pairs={{0,2},{2,4},{4,6},{6,7},{7,5},{5,3},{3,1},{1,0},{8,10},{10,12},{12... | collective-permute-start | bytes 1572872 | tf_op jit(solution)/shard_map/ppermute | solution.py:130
  6.8 86.8 %collective-permute-start.12 = (bf16[256,1792]{1,0:T(8,128)(2,1)S(1)}, bf16[256,1792]{1,0:T(8,128)(2,1)S(1)}, u32[]{:S(2)}, u32[]{:S(2)}) collective-permute-start(bf16[256,1792]{1,0:T(8,128)(2,1)S(1)} %fusion.33.refs_0_), channel_id=1, source_target_pairs={{0,2},{2,4},{4,6},{6,7},{7,5},{5,3},{3,1},{1,0},{8,10},{10,12},{12... | collective-permute-start | bytes 2752520 | tf_op jit(solution)/shard_map/ppermute | solution.py:130
  8.9 49.0 %collective-permute-start.15 = (bf16[256,1792]{1,0:T(8,128)(2,1)S(1)}, bf16[256,1792]{1,0:T(8,128)(2,1)}, u32[]{:S(2)}, u32[]{:S(2)}) collective-permute-start(bf16[256,1792]{1,0:T(8,128)(2,1)S(1)} %fusion.33.refs_0_), channel_id=1, source_target_pairs={{0,1},{2,0},{4,2},{6,4},{7,6},{5,7},{3,5},{1,3},{8,9},{10,8},{12,1... | collective-permute-start | bytes 2752520 | tf_op jit(solution)/shard_map/ppermute | solution.py:130
  93.6 43.1 %collective-permute-start.13 = (bf16[256,1792]{1,0:T(8,128)(2,1)S(1)}, bf16[256,1792]{1,0:T(8,128)(2,1)}, u32[]{:S(2)}, u32[]{:S(2)}) collective-permute-start(bf16[256,1792]{1,0:T(8,128)(2,1)S(1)} %collective-permute-done.12.refs_7_), channel_id=1, source_target_pairs={{0,2},{2,4},{4,6},{6,7},{7,5},{5,3},{3,1},{1,0},{8,10},{10,12},{12... | collective-permute-start | bytes 2752520 | tf_op jit(solution)/shard_map/ppermute | solution.py:130
  93.7 43.1 %collective-permute-start.17 = (bf16[256,1792]{1,0:T(8,128)(2,1)}, bf16[256,1792]{1,0:T(8,128)(2,1)}, u32[]{:S(2)}, u32[]{:S(2)}) collective-permute-start(bf16[256,1792]{1,0:T(8,128)(2,1)} %collective-permute-done.16.refs_2_), channel_id=1, source_target_pairs={{0,1},{2,0},{4,2},{6,4},{7,6},{5,7},{3,5},{1,3},{8,9},{10,8},{12,1... | collective-permute-start | bytes 2752520 | tf_op jit(solution)/shard_map/ppermute | solution.py:130
  116.2 63.9 %collective-permute-start.2 = (bf16[256,2048]{1,0:T(8,128)(2,1)}, bf16[256,2048]{1,0:T(8,128)(2,1)}, u32[]{:S(2)}, u32[]{:S(2)}) collective-permute-start(bf16[256,2048]{1,0:T(8,128)(2,1)} %collective-permute-done), channel_id=1, source_target_pairs={{0,8},{8,0},{16,24},{24,16},{1,9},{9,1},{17,25},{25,17},{2,10},{10... | collective-permute-start | bytes 3145736 | tf_op jit(solution)/shard_map/ppermute | solution.py:40
  136.7 43.5 %collective-permute-start.1 = (bf16[256,2048]{1,0:T(8,128)(2,1)}, bf16[256,2048]{1,0:T(8,128)(2,1)}, u32[]{:S(2)}, u32[]{:S(2)}) collective-permute-start(bf16[256,2048]{1,0:T(8,128)(2,1)} %fusion.25), channel_id=1, source_target_pairs={{0,8},{8,0},{16,24},{24,16},{1,9},{9,1},{17,25},{25,17},{2,10},{10... | collective-permute-start | bytes 3145736 | tf_op jit(solution)/shard_map/ppermute | solution.py:40
  136.7 38.9 %collective-permute-start.14 = (bf16[256,1792]{1,0:T(8,128)(2,1)}, bf16[256,1792]{1,0:T(8,128)(2,1)}, u32[]{:S(2)}, u32[]{:S(2)}) collective-permute-start(bf16[256,1792]{1,0:T(8,128)(2,1)} %collective-permute-done.13.refs_6_), channel_id=1, source_target_pairs={{0,2},{2,4},{4,6},{6,7},{7,5},{5,3},{3,1},{1,0},{8,10},{10,12},{12... | collective-permute-start | bytes 2752520 | tf_op jit(solution)/shard_map/ppermute | solution.py:130
  136.7 38.9 %collective-permute-start.18 = (bf16[256,1792]{1,0:T(8,128)(2,1)}, bf16[256,1792]{1,0:T(8,128)(2,1)}, u32[]{:S(2)}, u32[]{:S(2)}) collective-permute-start(bf16[256,1792]{1,0:T(8,128)(2,1)} %collective-permute-done.17.refs_3_), channel_id=1, source_target_pairs={{0,1},{2,0},{4,2},{6,4},{7,6},{5,7},{3,5},{1,3},{8,9},{10,8},{12,1... | collective-permute-start | bytes 2752520 | tf_op jit(solution)/shard_map/ppermute | solution.py:130
  317.0 42.9 %all-to-all-start.3 = ((bf16[8,32,2048]{2,1,0:T(8,128)(2,1)}), bf16[8,32,2048]{2,1,0:T(8,128)(2,1)}, u32[]{:S(2)}, u32[]{:S(2)}) async-start(bf16[8,32,2048]{2,1,0:T(8,128)(2,1)} %bitcast.22), calls=%async_computation.3 | async-start | bytes 2097152 | tf_op jit(solution)/shard_map/all_to_all | solution.py:682
  550.5 43.0 %collective-permute-start.68 = (bf16[512,2048]{1,0:T(8,128)(2,1)S(1)}, bf16[512,2048]{1,0:T(8,128)(2,1)}, u32[]{:S(2)}, u32[]{:S(2)}) collective-permute-start(bf16[512,2048]{1,0:T(8,128)(2,1)S(1)} %pad_maximum_fusion.6), channel_id=1, source_target_pairs={{0,8},{8,0},{16,24},{24,16},{1,9},{9,1},{17,25},{25,17},{2,10},{10... | collective-permute-start | bytes 6291464 | tf_op jit(solution)/shard_map/ppermute | solution.py:40
  587.1 60.4 %collective-permute-start.83 = (bf16[256,896]{1,0:T(8,128)(2,1)}, bf16[256,896]{1,0:T(8,128)(2,1)}, u32[]{:S(2)}, u32[]{:S(2)}) collective-permute-start(bf16[256,896]{1,0:T(8,128)(2,1)} %get-tuple-element.348), channel_id=1, source_target_pairs={{0,2},{2,4},{4,6},{6,7},{7,5},{5,3},{3,1},{1,0},{8,10},{10,12},{12... | collective-permute-start | bytes 1376264 | tf_op jit(solution)/shard_map/ppermute | solution.py:130
  591.0 60.1 %collective-permute-start.82 = (bf16[256,896]{1,0:T(8,128)(2,1)}, bf16[256,896]{1,0:T(8,128)(2,1)}, u32[]{:S(2)}, u32[]{:S(2)}) collective-permute-start(bf16[256,896]{1,0:T(8,128)(2,1)} %get-tuple-element.347), channel_id=1, source_target_pairs={{0,1},{2,0},{4,2},{6,4},{7,6},{5,7},{3,5},{1,3},{8,9},{10,8},{12,1... | collective-permute-start | bytes 1376264 | tf_op jit(solution)/shard_map/ppermute | solution.py:130
  604.5 40.4 %collective-permute-start.74 = (bf16[256,896]{0,1:T(8,128)(2,1)}, bf16[256,896]{0,1:T(8,128)(2,1)S(1)}, u32[]{:S(2)}, u32[]{:S(2)}) collective-permute-start(bf16[256,896]{0,1:T(8,128)(2,1)} %add_convert_fusion.40), channel_id=1, source_target_pairs={{0,2},{2,4},{4,6},{6,7},{7,5},{5,3},{3,1},{1,0},{8,10},{10,12},{12... | collective-permute-start | bytes 1376264 | tf_op jit(solution)/shard_map/ppermute | solution.py:130
  609.1 72.0 %collective-permute-start.78 = (bf16[256,2048]{1,0:T(8,128)(2,1)}, bf16[256,2048]{1,0:T(8,128)(2,1)}, u32[]{:S(2)}, u32[]{:S(2)}) collective-permute-start(bf16[256,2048]{1,0:T(8,128)(2,1)} %fusion.16), channel_id=1, source_target_pairs={{0,16},{8,24},{16,0},{24,8},{1,17},{9,25},{17,1},{25,9},{2,18},{10... | collective-permute-start | bytes 3145736 | tf_op jit(solution)/shard_map/ppermute | solution.py:40
  648.7 73.5 %collective-permute-start.87 = (bf16[256,896]{1,0:T(8,128)(2,1)}, bf16[256,896]{1,0:T(8,128)(2,1)}, u32[]{:S(2)}, u32[]{:S(2)}) collective-permute-start(bf16[256,896]{1,0:T(8,128)(2,1)} %get-tuple-element.352), channel_id=1, source_target_pairs={{0,1},{2,0},{4,2},{6,4},{7,6},{5,7},{3,5},{1,3},{8,9},{10,8},{12,1... | collective-permute-start | bytes 1376264 | tf_op jit(solution)/shard_map/ppermute | solution.py:130
  665.3 53.3 %collective-permute-start.75 = (bf16[256,896]{0,1:T(8,128)(2,1)S(1)}, bf16[256,896]{0,1:T(8,128)(2,1)}, u32[]{:S(2)}, u32[]{:S(2)}) collective-permute-start(bf16[256,896]{0,1:T(8,128)(2,1)S(1)} %get-tuple-element.530), channel_id=1, source_target_pairs={{0,2},{2,4},{4,6},{6,7},{7,5},{5,3},{3,1},{1,0},{8,10},{10,12},{12... | collective-permute-start | bytes 1376264 | tf_op jit(solution)/shard_map/ppermute | solution.py:130
  672.2 64.0 %collective-permute-start.85 = (bf16[256,1792]{1,0:T(8,128)(2,1)S(1)}, bf16[256,1792]{1,0:T(8,128)(2,1)S(1)}, u32[]{:S(2)}, u32[]{:S(2)}) collective-permute-start(bf16[256,1792]{1,0:T(8,128)(2,1)S(1)} %pad_maximum_fusion.11.refs_0_), channel_id=1, source_target_pairs={{0,16},{8,24},{16,0},{24,8},{1,17},{9,25},{17,1},{25,9},{2,18},{10... | collective-permute-start | bytes 2752520 | tf_op jit(solution)/shard_map/ppermute | solution.py:40
  680.1 40.3 %collective-permute-start.77 = (bf16[256,896]{0,1:T(8,128)(2,1)}, bf16[256,896]{0,1:T(8,128)(2,1)}, u32[]{:S(2)}, u32[]{:S(2)}) collective-permute-start(bf16[256,896]{0,1:T(8,128)(2,1)} %add_convert_fusion.33), channel_id=1, source_target_pairs={{0,1},{2,0},{4,2},{6,4},{7,6},{5,7},{3,5},{1,3},{8,9},{10,8},{12,1... | collective-permute-start | bytes 1376264 | tf_op jit(solution)/shard_map/ppermute | solution.py:130
  686.4 49.8 %all-to-all-start.4 = ((bf16[8,32,2048]{2,1,0:T(8,128)(2,1)}), bf16[8,32,2048]{2,1,0:T(8,128)(2,1)S(1)}, u32[]{:S(2)}, u32[]{:S(2)}) async-start(bf16[8,32,2048]{2,1,0:T(8,128)(2,1)} %bitcast.26), calls=%async_computation.4 | async-start | bytes 2097152 | tf_op jit(solution)/shard_map/all_to_all | solution.py:764
  722.7 45.8 %collective-permute-start.104 = (bf16[256,896]{1,0:T(8,128)(2,1)}, bf16[256,896]{1,0:T(8,128)(2,1)}, u32[]{:S(2)}, u32[]{:S(2)}) collective-permute-start(bf16[256,896]{1,0:T(8,128)(2,1)} %get-tuple-element.376), channel_id=1, source_target_pairs={{0,2},{2,4},{4,6},{6,7},{7,5},{5,3},{3,1},{1,0},{8,10},{10,12},{12... | collective-permute-start | bytes 1376264 | tf_op jit(solution)/shard_map/ppermute | solution.py:130
  751.3 66.5 %collective-permute-start.90 = (bf16[512,2048]{1,0:T(8,128)(2,1)}, bf16[512,2048]{1,0:T(8,128)(2,1)}, u32[]{:S(2)}, u32[]{:S(2)}) collective-permute-start(bf16[512,2048]{1,0:T(8,128)(2,1)} %pad_maximum_fusion.8), channel_id=1, source_target_pairs={{0,8},{8,0},{16,24},{24,16},{1,9},{9,1},{17,25},{25,17},{2,10},{10... | collective-permute-start | bytes 6291464 | tf_op jit(solution)/shard_map/ppermute | solution.py:40
  762.0 55.8 %all-to-all-start.5 = ((bf16[2,4,32,2048]{3,2,0,1:T(8,128)(2,1)}), bf16[2,4,32,2048]{3,2,0,1:T(8,128)(2,1)}, u32[]{:S(2)}, u32[]{:S(2)}) async-start(bf16[2,4,32,2048]{3,2,0,1:T(8,128)(2,1)} %copy.176), calls=%async_computation.5 | async-start | bytes 2097152 | tf_op jit(solution)/shard_map/all_to_all | solution.py:785
  (254 other events, 4794.5 us)
